TPU v7x, 32 devices: a whole 2x2x4 slice. The times are simulated.
32 devices in a mesh: parts: 2 (over y), dp: 4 (over z), tensor: 4 (over x, core).
Axes of the slice: x: 2, y: 2, z: 4, core: 2. Of those that a mesh axis runs over, the one named last changes fastest.
Arguments:
- hidden_in: bfloat16 [4096, 4096], P(('parts', 'dp'), 'tensor'), parts along dimension 0, may hold values from -80 to 80
- row_loads: int32 [8, 4], P(('parts', 'dp')), parts along dimension 0, may hold values from 0 to 256, as said below
- seg_ids: int32 [4096], P(('parts', 'dp')), parts along dimension 0, may hold values from 0 to 3, as said below
- pos_ids: int32 [4096], P(('parts', 'dp')), parts along dimension 0, may hold values from 0 to 511, as said below
- prompt_order: int32 [8, 512], P(('parts', 'dp')), parts along dimension 0, may hold values from 0 to 511, each once within a row
- attn_gain: bfloat16 [4096], replicated, may hold values from 0.099609375 to 1.8984375
- w_query: bfloat16 [4096, 2048], P(None, 'tensor'), may hold values from -2 to 2
- key_matrix: bfloat16 [4096, 512], P(None, 'tensor'), may hold values from -2 to 2
- value_matrix: bfloat16 [4096, 512], P(None, 'tensor'), may hold values from -0.09375 to 0.09375
- w_out: bfloat16 [2048, 4096], P('tensor'), may hold values from -0.125 to 0.125
- final_gain: bfloat16 [4096], P('tensor'), may hold values from 0.099609375 to 1.8984375
- value_head: bfloat16 [4096], P('tensor'), may hold values from -0.09375 to 0.09375
Outputs:
- hidden_out: bfloat16 [4096, 4096], P(('parts', 'dp'), 'tensor'), parts along dimension 0
- token_values: float32 [4096], P(('parts', 'dp')), parts along dimension 0
There are 2 independent parts, one for each index of `parts`. A program takes and returns all parts, laid end to end along the dimension named above; an argument that names none is the same for every part. Nothing has to cross between parts.
Inputs may be any that keep to these rules, and one draw needn't show every extreme that they name: `row_loads`: row s lists how many rows of shard s go to each destination shard, in destination order; each row sums to 512, and one destination receives exactly 256 rows from every shard. `seg_ids`: over one destination's rows, taken in shard order and then in row order, ids never fall; rows with one id there form one document. `pos_ids`: A row's position counts the earlier rows of its document in that order.
All inputs are finite; a program needn't handle non-finite values.
Results may differ from a plain program's by a relative error of at most 0.005.
Values may be sent and summed in bfloat16 or wider, within the bound.
No kernel may reach another device: no remote copies, remote signals or barrier semaphores. Data moves between devices by JAX's collectives and lax.ppermute only.
A program may use at most 128 MiB of HBM per device.

v0:
```python
import jax
import jax.numpy as jnp
from jax import lax
from jax.sharding import PartitionSpec as P

MODEL_WIDTH = 4096
QUERY_HEADS = 16
KEY_VALUE_HEADS = 4
HEAD_WIDTH = 128


norm_eps = 1e-05
rope_base = 500000.0


def rotary_embed(vectors, positions):
    head_size = vectors.shape[-1]
    half_size = head_size // 2
    inverse = rope_base ** (-(jnp.arange(half_size, dtype=jnp.float32) * 2.0) / head_size)
    angles = positions.astype(jnp.float32)[..., None] * inverse
    cosine = jnp.cos(angles)[..., None, :]
    sine_part = jnp.sin(angles)[..., None, :]
    first_half = vectors[..., :half_size]
    second_half = vectors[..., half_size:]
    return jnp.concatenate(
        [
            first_half * cosine - second_half * sine_part,
            second_half * cosine + first_half * sine_part,
        ],
        -1,
    )


def rms_norm(full_rows, attn_gain):
    as_float = full_rows.astype(jnp.float32)
    scale = lax.rsqrt(jnp.mean(as_float * as_float, -1, keepdims=True) + norm_eps)
    return (as_float * scale * attn_gain.astype(jnp.float32)).astype(jnp.bfloat16)


def projections(normed_hidden, positions, w_query, key_matrix, value_matrix):
    lead = normed_hidden.shape[:-1]
    query_cols = w_query.shape[1]
    key_cols = key_matrix.shape[1]
    raw_query = jnp.einsum(
        "...d,dc->...c", normed_hidden, w_query, preferred_element_type=jnp.float32
    )
    raw_key = jnp.einsum(
        "...d,dc->...c", normed_hidden, key_matrix, preferred_element_type=jnp.float32
    )
    raw_value = jnp.einsum(
        "...d,dc->...c", normed_hidden, value_matrix, preferred_element_type=jnp.float32
    )
    query_rows = (
        rotary_embed(raw_query.reshape(lead + (query_cols // HEAD_WIDTH, HEAD_WIDTH)), positions)
        .astype(jnp.bfloat16)
        .reshape(lead + (query_cols,))
    )
    key_head_rows = (
        rotary_embed(raw_key.reshape(lead + (key_cols // HEAD_WIDTH, HEAD_WIDTH)), positions)
        .astype(jnp.bfloat16)
        .reshape(lead + (key_cols,))
    )
    return (query_rows, key_head_rows, raw_value.astype(jnp.bfloat16))


def attend(query_rows, key_head_rows, value_head_rows, seg_slots):
    total_slots = query_rows.shape[0]
    kv_local = key_head_rows.shape[1] // HEAD_WIDTH
    heads_per_group = QUERY_HEADS // KEY_VALUE_HEADS
    query_group_rows = query_rows.reshape(total_slots, kv_local, heads_per_group, HEAD_WIDTH)
    key_groups = key_head_rows.reshape(total_slots, kv_local, HEAD_WIDTH)
    value_groups = value_head_rows.reshape(total_slots, kv_local, HEAD_WIDTH)
    slot_ids = jnp.arange(total_slots)
    block_rows = min(512, total_slots)
    outputs = []
    for block_start in range(0, total_slots, block_rows):
        query_block = query_group_rows[block_start : block_start + block_rows]
        scores = (
            jnp.einsum(
                "qgjd,kgd->gjqk", query_block, key_groups, preferred_element_type=jnp.float32
            )
            / HEAD_WIDTH**0.5
        )
        block_seg = seg_slots[block_start : block_start + block_rows]
        block_ids = slot_ids[block_start : block_start + block_rows]
        allowed = (block_seg[:, None] == seg_slots[None, :]) & (
            slot_ids[None, :] <= block_ids[:, None]
        )
        scores = jnp.where(allowed, scores, -jnp.inf)
        row_max = jnp.max(scores, -1, keepdims=True)
        exp_terms = jnp.where(allowed, jnp.exp(scores - row_max), 0.0)
        probabilities = (exp_terms / jnp.sum(exp_terms, -1, keepdims=True)).astype(jnp.bfloat16)
        block_out = jnp.einsum(
            "gjqk,kgd->qgjd", probabilities, value_groups, preferred_element_type=jnp.float32
        ).astype(jnp.bfloat16)
        outputs.append(block_out.reshape(block_rows, kv_local * heads_per_group * HEAD_WIDTH))
    return jnp.concatenate(outputs, 0)


def finish(own_rows, attended, final_gain, value_head):
    hidden = (own_rows.astype(jnp.float32) + attended).astype(jnp.bfloat16)
    hidden_float = hidden.astype(jnp.float32)
    square_sum = jnp.sum(hidden_float * hidden_float, -1)
    head_dot = jnp.sum(
        hidden_float * final_gain.astype(jnp.float32) * value_head.astype(jnp.float32), -1
    )
    return (hidden, square_sum, head_dot)


def on_device(
    hidden_in,
    row_loads,
    seg_ids,
    pos_ids,
    prompt_order,
    attn_gain,
    w_query,
    key_matrix,
    value_matrix,
    w_out,
    final_gain,
    value_head,
):
    dp_count = lax.axis_size("dp")
    row_count = hidden_in.shape[0]
    slot_count = 2 * row_count // dp_count
    total_slots = dp_count * slot_count
    load_row = row_loads[0]
    block_end = jnp.cumsum(load_row)
    starts = block_end - load_row
    lane_ids = jnp.arange(slot_count, dtype=jnp.int32)
    is_used = lane_ids[None, :] < load_row[:, None]
    row_index = jnp.minimum(starts[:, None] + lane_ids[None, :], row_count - 1)
    row_ids = jnp.arange(row_count, dtype=jnp.int32)
    dest_of = jnp.sum((block_end[None, :] <= row_ids[:, None]).astype(jnp.int32), 1)
    lane_of = row_ids - starts[dest_of]
    pick_dest = dest_of[prompt_order[0]]
    pick_lane = lane_of[prompt_order[0]]
    seg_send = jnp.where(is_used, seg_ids[row_index], -1)
    send_rows = jnp.where(is_used[:, :, None], hidden_in[row_index], 0)
    pos_send = jnp.where(is_used, pos_ids[row_index], 0)
    rows = lax.all_to_all(send_rows, "dp", split_axis=0, concat_axis=0, tiled=True)
    seg_piece = lax.all_to_all(seg_send, "dp", split_axis=0, concat_axis=0, tiled=True)
    pos_piece = lax.all_to_all(pos_send, "dp", split_axis=0, concat_axis=0, tiled=True)
    full_rows = lax.all_gather(rows, "tensor", axis=2, tiled=True)
    normed_hidden = rms_norm(full_rows, attn_gain)
    query_rows, key_head_rows, value_head_rows = projections(
        normed_hidden, pos_piece, w_query, key_matrix, value_matrix
    )
    query_rows, key_head_rows, value_head_rows, own_rows, seg_slots = (
        query_rows,
        key_head_rows,
        value_head_rows,
        rows,
        seg_piece,
    )
    mixed_heads = attend(
        query_rows.reshape(total_slots, -1),
        key_head_rows.reshape(total_slots, -1),
        value_head_rows.reshape(total_slots, -1),
        seg_slots.reshape(total_slots),
    )
    partial_value = jnp.dot(mixed_heads, w_out, preferred_element_type=jnp.float32)
    attended = lax.psum_scatter(partial_value, "tensor", scatter_dimension=1, tiled=True)
    hidden, square_sum, head_dot = finish(
        own_rows.reshape(total_slots, -1), attended, final_gain, value_head
    )
    square_sum, head_dot = lax.psum((square_sum, head_dot), "tensor")
    values = head_dot * lax.rsqrt(square_sum / MODEL_WIDTH + norm_eps)
    back_rows = lax.all_to_all(
        hidden.reshape(dp_count, slot_count, -1), "dp", split_axis=0, concat_axis=0, tiled=True
    )
    back_values = lax.all_to_all(
        values.reshape(dp_count, slot_count), "dp", split_axis=0, concat_axis=0, tiled=True
    )
    return (back_rows[pick_dest, pick_lane], back_values[pick_dest, pick_lane])


def solution(mesh):
    return jax.shard_map(
        on_device,
        mesh=mesh,
        in_specs=(
            P(("parts", "dp"), "tensor"),
            P(("parts", "dp"), None),
            P(("parts", "dp")),
            P(("parts", "dp")),
            P(("parts", "dp"), None),
            P(),
            P(None, "tensor"),
            P(None, "tensor"),
            P(None, "tensor"),
            P("tensor", None),
            P("tensor"),
            P("tensor"),
        ),
        out_specs=(P(("parts", "dp"), "tensor"), P(("parts", "dp"))),
        check_vma=False,
    )
```

profile of v0, /device:TPU:9, one launch (start us, length us, event | category | flops | bytes accessed | tf_op | source)
XLA Modules:
  0.0 382.3 jit_solution(17291818268542342460)
XLA Ops:
  7.2 0.0 copy-start
  7.2 0.0 all-gather.2.cloned.1.call-start
  7.2 0.9 reduce-window.7
  8.1 0.7 bitcast_subtract_fusion
  8.8 0.1 fusion.53
  8.9 0.7 iota_compare_fusion.3
  9.6 4.1 %gather_fusion = bf16[1024,1024]{1,0:T(8,128)(2,1)S(1)} fusion(bf16[512,1024]{1,0:T(8,128)(2,1)S(1)} %copy-done, s32[1024]{0:T(1024)S(1)} %broadcast_clamp_fusion), kind=kCustom, calls=%fused_computation | custom fusion | bytes 4198400 | tf_op jit(solution)/shard_map/gather | solution.py:140
  13.7 0.0 copy-start.2
  13.7 0.0 copy-start.3
  13.7 0.2 broadcast_select_fusion
  13.9 0.0 copy-start.10
  13.9 0.0 copy-start.6
  14.0 50.1 %all_to_all.34 = bf16[4,256,1024]{2,1,0:T(8,128)(2,1)} all-to-all(bf16[4,256,1024]{2,1,0:T(8,128)(2,1)S(1)} %broadcast_select_fusion), channel_id=1, replica_groups=mesh['parts'=2,'dp'=4,'tensor'=4] {'dp'}, dimensions={0} | all-to-all | bytes 4194304 | tf_op jit(solution)/shard_map/all_to_all | solution.py:142
  64.1 0.0 all-gather.2.cloned.1.call-update
  64.1 6.9 %gather_fusion.1 = s32[1024]{0:T(1024)S(1)} fusion(s32[512]{0:T(512)S(1)} %copy-done.2, s32[1024]{0:T(1024)S(1)} %broadcast_clamp_fusion), kind=kCustom, calls=%fused_computation.1 | custom fusion | bytes 12288 | tf_op jit(solution)/shard_map/gather | solution.py:139
  71.0 6.9 %gather_fusion.2 = s32[1024]{0:T(1024)S(1)} fusion(s32[512]{0:T(512)S(1)} %copy-done.3, s32[1024]{0:T(1024)S(1)} %broadcast_clamp_fusion), kind=kCustom, calls=%fused_computation.2 | custom fusion | bytes 12288 | tf_op jit(solution)/shard_map/gather | solution.py:141
  77.9 0.7 compare_select_fusion.6
  78.6 8.2 %all_to_all.35 = s32[4,1,256]{2,1,0:T(1,128)S(1)} all-to-all(s32[4,1,256]{2,1,0:T(1,128)S(1)} %get-tuple-element.24), channel_id=1, replica_groups=mesh['parts'=2,'dp'=4,'tensor'=4] {'dp'}, dimensions={0} | all-to-all | bytes 8192 | tf_op jit(solution)/shard_map/all_to_all | solution.py:144
  86.7 4.4 %all-to-all-start.1 = ((s32[4,1,256]{2,1,0:T(1,128)}), s32[4,1,256]{2,1,0:T(1,128)S(1)}, u32[]{:S(2)}, u32[]{:S(2)}) async-start(s32[4,1,256]{2,1,0:T(1,128)} %get-tuple-element.23), calls=%async_computation.1 | async-start | bytes 8192 | tf_op jit(solution)/shard_map/all_to_all | solution.py:143
  91.2 3.2 all-to-all-done.1
  94.4 3.0 multiply_cosine_fusion
  97.4 0.9 fusion.22
  98.3 26.7 %all-gather.2.cloned.1.call-done = bf16[4,256,4096]{2,1,0:T(8,128)(2,1)} async-done(((bf16[4,256,1024]{2,1,0:T(8,128)(2,1)}), bf16[4,256,4096]{2,1,0:T(8,128)(2,1)}) %all-gather.2.cloned.1.call-update) | async-done | bytes 8388624 | tf_op jit(solution)/shard_map/all_gather | solution.py:145
  125.0 5.2 %fusion = f32[4,256]{1,0:T(4,128)S(1)} fusion(bf16[4,256,4096]{2,1,0:T(8,128)(2,1)} %all-gather.2.cloned.1.call-done), kind=kLoop, calls=%fused_computation.9 | loop fusion | flops 12581888 | bytes 8392704 | tf_op jit(solution)/shard_map/reduce_sum | solution.py:36
  130.2 0.5 copy-done.5
  130.7 8.1 %fusion.7 = f32[4,256,512]{2,1,0:T(8,128)} fusion(bf16[4,256,4096]{2,1,0:T(8,128)(2,1)S(1)} %copy-done.5, f32[4096]{0:T(1024)S(1)} %convert_element_type.80, f32[4,256]{1,0:T(4,128)S(1)} %add_rsqrt_fusion, bf16[4096,512]{1,0:T(8,128)(2,1)} %param.18), kind=kOutput, calls=%fused_computation.24 | convolution fusion | flops 4311744512 | bytes 14700544 | tf_op jit(solution)/shard_map/...d,dc->...c/dot_general | solution.py:44
  138.8 1.9 reshape.398
  140.8 0.0 copy-start.12
  140.8 2.7 subtract_convert_fusion
  143.5 1.4 fusion.42
  145.0 0.1 copy.48
  145.1 5.5 %fusion.30 = f32[4,256,1,128]{1,3,0,2:T(8,128)S(1)} fusion(bf16[4,256,4096]{2,1,0:T(8,128)(2,1)} %all-gather.2.cloned.1.call-done, f32[4096]{0:T(1024)S(1)} %convert_element_type.80, f32[4,256]{1,0:T(4,128)S(1)} %add_rsqrt_fusion, bf16[4096,128]{1,0:T(8,128)(2,1)S(1)} %copy-done.12), kind=kOutput, calls=%fused_computation.46 | convolution fusion | flops 1090519040 | bytes 9981952 | tf_op jit(solution)/shard_map/...d,dc->...c/dot_general | solution.py:47
  150.5 1.4 fusion.48
  151.9 0.2 copy.62
  152.1 0.2 copy.61
  152.3 0.1 copy.51
  152.3 1.6 fusion.3
  153.9 0.0 slice-start
  153.9 1.6 fusion.4
  155.5 0.0 slice-start.1
  155.5 0.0 copy-start.13
  155.6 4.2 %fusion.5 = (f32[4,512]{1,0:T(4,128)S(1)}, f32[4,512]{1,0:T(4,128)S(1)}) fusion(f32[1024,512,4]{1,0,2:T(8,128)S(1)} %get-tuple-element.28, f32[4,512]{1,0:T(4,128)S(1)} %get-tuple-element.27, pred[512,1024]{0,1:T(8,128)(4,1)S(1)} %get-tuple-element.15, f32[4,512]{1,0:T(4,128)S(1)} %get-tuple-element.25, f32[1024,512,4]{1,0,2:T(8,128)S(1)} %get-tuple-element.26, ...), kind=kLoop, calls=%fused_computation.20 | loop fusion | flops 20967424 | bytes 17858560 | tf_op jit(solution)/shard_map/reduce_sum | solution.py:92
  159.8 2.4 fusion.33
  162.2 3.0 fusion.27
  165.2 0.0 copy-start.11
  165.2 2.9 fusion.24
  168.1 0.0 copy-done.11
  168.1 8.4 %fusion.36 = f32[1024,4096]{1,0:T(8,128)} fusion(bf16[512,4096]{1,0:T(8,128)(2,1)S(1)} %copy-done.11, bf16[512,512]{0,1:T(8,128)(2,1)S(1)} %bitcast.156, bf16[512,512]{0,1:T(8,128)(2,1)S(1)} %bitcast.157), kind=kOutput, calls=%fused_computation.50 | convolution fusion | flops 4297064448 | bytes 22020096 | tf_op jit(solution)/shard_map/dot_general | solution.py:163
  176.6 0.0 reduce-scatter.2.cloned.1.call-update
  176.6 0.7 copy-done.7
  177.2 0.0 copy-done.8
  177.2 125.2 %reduce-scatter.2.cloned.1.call-done = f32[1024,1024]{1,0:T(8,128)} async-done(((f32[1024,4096]{1,0:T(8,128)}), f32[1024,1024]{1,0:T(8,128)}) %reduce-scatter.2.cloned.1.call-update) | async-done | bytes 4194320 | tf_op jit(solution)/shard_map/reduce_scatter | solution.py:164
  302.4 4.2 %fusion.15 = (f32[1024]{0:T(1024)S(1)}, f32[1024]{0:T(1024)S(1)}, bf16[1024,1024]{1,0:T(8,128)(2,1)}) fusion(f32[1024]{0:T(1024)S(1)} %convert_element_type.97, f32[1024]{0:T(1024)S(1)} %convert_element_type.96, f32[1024,1024]{1,0:T(8,128)} %reduce-scatter.2.cloned.1.call-done, bf16[4,256,1024]{2,1,0:T(8,128)(2,1)S(1)} %copy-done.4), kind=kLoop, calls=%fused_computation.29 | loop fusion | flops 9435136 | bytes 8404992 | tf_op jit(solution)/shard_map/reduce_sum | solution.py:103
  306.6 5.8 %all-reduce = (f32[1024]{0:T(1024)S(1)}, f32[1024]{0:T(1024)S(1)}) all-reduce(f32[1024]{0:T(1024)S(1)} %get-tuple-element.3, f32[1024]{0:T(1024)S(1)} %get-tuple-element.2), channel_id=1, replica_groups=mesh['parts'=2,'dp'=4,'tensor'=4] {'tensor'}, use_global_device_ids=true, to_apply=%region_9.10 | all-reduce | flops 2048 | bytes 16384 | tf_op jit(solution)/shard_map/psum | solution.py:168
  312.4 7.6 %all_to_all.36 = f32[4,1,256]{2,1,0:T(1,128)S(1)} all-to-all(f32[4,1,256]{2,1,0:T(1,128)S(1)} %bitcast.142), channel_id=1, replica_groups=mesh['parts'=2,'dp'=4,'tensor'=4] {'dp'}, dimensions={0} | all-to-all | bytes 8192 | tf_op jit(solution)/shard_map/all_to_all | solution.py:173
  320.0 4.7 %all-to-all-start.3 = ((bf16[4,256,1024]{2,1,0:T(8,128)(2,1)}), bf16[4,256,1024]{2,1,0:T(8,128)(2,1)S(1)}, u32[]{:S(2)}, u32[]{:S(2)}) async-start(bf16[4,256,1024]{2,1,0:T(8,128)(2,1)} %bitcast.132), calls=%async_computation.4 | async-start | bytes 4194304 | tf_op jit(solution)/shard_map/all_to_all | solution.py:170
  324.8 0.1 convert_reduce_fusion
  324.9 3.5 gather_fusion.3
  328.4 0.7 fusion.70
  329.0 2.6 compare_select_fusion.7
  331.6 3.5 gather_fusion.4
  335.1 7.0 %gather_fusion.6 = f32[512]{0:T(512)} fusion(f32[4,256]{1,0:T(4,128)S(1)} %bitcast.126, s32[512]{0:T(512)S(1)} %bitcast.127), kind=kCustom, calls=%fused_computation.6 | custom fusion | bytes 8192 | tf_op jit(solution)/shard_map/gather | solution.py:176
  342.2 25.4 %all-to-all-done.3 = bf16[4,256,1024]{2,1,0:T(8,128)(2,1)S(1)} async-done(((bf16[4,256,1024]{2,1,0:T(8,128)(2,1)}), bf16[4,256,1024]{2,1,0:T(8,128)(2,1)S(1)}, u32[]{:S(2)}, u32[]{:S(2)}) %all-to-all-start.3) | async-done | bytes 2097184 | tf_op jit(solution)/shard_map/all_to_all | solution.py:170
  367.6 7.9 %gather_fusion.5 = bf16[512,1024]{1,0:T(8,128)(2,1)} fusion(bf16[4,256,1024]{2,1,0:T(8,128)(2,1)S(1)} %all-to-all-done.3, s32[512]{0:T(512)S(1)} %bitcast.128), kind=kCustom, calls=%fused_computation.5 | custom fusion | bytes 2101248 | tf_op jit(solution)/shard_map/gather | solution.py:176
  (40 shorter events, 0.1 us)
Async XLA Ops:
  7.2 2.4 copy-start
  7.2 117.8 %all-gather.2.cloned.1.call-start = ((), (), s32[]{:S(2)}) async-start(), calls=%async_computation.6 | async-start | bytes 10485760 | tf_op jit(solution)/shard_map/all_gather | solution.py:145
  13.7 50.4 %copy-start.2 = (s32[512]{0:T(512)S(1)}, s32[512]{0:T(512)}, u32[]{:S(2)}) copy-start(s32[512]{0:T(512)} %param.14) | copy-start | bytes 6148
  13.7 57.3 %copy-start.3 = (s32[512]{0:T(512)S(1)}, s32[512]{0:T(512)}, u32[]{:S(2)}) copy-start(s32[512]{0:T(512)} %param.15) | copy-start | bytes 6148
  13.9 63.9 %copy-start.10 = (s32[1,4]{1,0:T(1,128)S(1)}, s32[1,4]{1,0:T(1,128)}, u32[]{:S(2)}) copy-start(s32[1,4]{1,0:T(1,128)} %param.13) | copy-start | bytes 52
  13.9 77.2 %copy-start.6 = (bf16[4096]{0:T(1024)(128)(2,1)S(1)}, bf16[4096]{0:T(1024)(128)(2,1)}, u32[]{:S(2)}) copy-start(bf16[4096]{0:T(1024)(128)(2,1)} %param.17) | copy-start | bytes 24580
  86.7 7.7 %all-to-all-start.1 = ((s32[4,1,256]{2,1,0:T(1,128)}), s32[4,1,256]{2,1,0:T(1,128)S(1)}, u32[]{:S(2)}, u32[]{:S(2)}) async-start(s32[4,1,256]{2,1,0:T(1,128)} %get-tuple-element.23), calls=%async_computation.1 | async-start | bytes 8192 | tf_op jit(solution)/shard_map/all_to_all | solution.py:143
  91.1 211.3 %reduce-scatter.2.cloned.1.call-start = ((), (), s32[]{:S(2)}) async-start(), calls=%async_computation.7 | async-start | bytes 20971520 | tf_op jit(solution)/shard_map/reduce_scatter | solution.py:164
  125.0 5.8 %copy-start.5 = (bf16[4,256,4096]{2,1,0:T(8,128)(2,1)S(1)}, bf16[4,256,4096]{2,1,0:T(8,128)(2,1)}, u32[]{:S(2)}) copy-start(bf16[4,256,4096]{2,1,0:T(8,128)(2,1)} %all-gather.2.cloned.1.call-done) | copy-start | bytes 25165828
  140.8 4.3 %copy-start.12 = (bf16[4096,128]{1,0:T(8,128)(2,1)S(1)}, bf16[4096,128]{1,0:T(8,128)(2,1)}, u32[]{:S(2)}) copy-start(bf16[4096,128]{1,0:T(8,128)(2,1)} %param.19) | copy-start | bytes 3145732
  153.9 5.8 %slice-start = ((s8[8388608]{0:T(1024)(128)(4,1)}), s8[4194304]{0:T(1024)(128)(4,1)S(1)}, s32[]{:S(2)}) async-start(s8[8388608]{0:T(1024)(128)(4,1)} %bitcast.130), calls=%async_computation.8 | async-start | bytes 8388608
  155.5 4.2 %slice-start.1 = ((s8[8388608]{0:T(1024)(128)(4,1)}), s8[4194304]{0:T(1024)(128)(4,1)S(1)}, s32[]{:S(2)}) async-start(s8[8388608]{0:T(1024)(128)(4,1)} %bitcast.130), calls=%async_computation.9 | async-start | bytes 8388608
  155.5 4.2 %copy-start.13 = (bf16[4096,128]{1,0:T(8,128)(2,1)S(1)}, bf16[4096,128]{1,0:T(8,128)(2,1)}, u32[]{:S(2)}) copy-start(bf16[4096,128]{1,0:T(8,128)(2,1)} %param.20) | copy-start | bytes 3145732
  165.2 3.0 copy-start.11
  176.5 0.7 copy-start.7
  176.5 0.7 copy-start.8
  176.6 125.9 %copy-start.4 = (bf16[4,256,1024]{2,1,0:T(8,128)(2,1)S(1)}, bf16[4,256,1024]{2,1,0:T(8,128)(2,1)}, u32[]{:S(2)}) copy-start(bf16[4,256,1024]{2,1,0:T(8,128)(2,1)} %all_to_all.34) | copy-start | bytes 6291460
  177.2 147.5 %copy-start.9 = (s32[1,512]{1,0:T(1,128)S(1)}, s32[1,512]{1,0:T(1,128)}, u32[]{:S(2)}) copy-start(s32[1,512]{1,0:T(1,128)} %param.16) | copy-start | bytes 6148
  320.0 47.5 %all-to-all-start.3 = ((bf16[4,256,1024]{2,1,0:T(8,128)(2,1)}), bf16[4,256,1024]{2,1,0:T(8,128)(2,1)S(1)}, u32[]{:S(2)}, u32[]{:S(2)}) async-start(bf16[4,256,1024]{2,1,0:T(8,128)(2,1)} %bitcast.132), calls=%async_computation.4 | async-start | bytes 4194304 | tf_op jit(solution)/shard_map/all_to_all | solution.py:170
  324.8 50.7 %copy-start.1 = (bf16[512,1024]{1,0:T(8,128)(2,1)S(1)}, bf16[512,1024]{1,0:T(8,128)(2,1)}, u32[]{:S(2)}) copy-start(bf16[512,1024]{1,0:T(8,128)(2,1)} %param.12) | copy-start | bytes 3145732
Sparse Core Ops, SparseCore 0:
  64.2 60.6 all-gather.1
  176.7 125.6 reduce-scatter.1
where the time goes:
time: 390 us; the launch traced here: 382 us
  waiting for transfers between devices  180 us (46%)
  blocking collectives  71.7 us (18%)
  local copies, waits for them, and re-layouts  44.1 us (11%)
  matrix products  33.5 us (9%)
  other arithmetic  28.9 us (7%)
  between operations  14.5 us (4%)
  starting transfers between devices  9.14 us (2%)
    reduce_scatter x1, waiting for transfers between devices, on_device(): lax.psum_scatter(partial_value, 'tensor', scatter_dimension=1, tiled=True)  125 us
    all_to_all x1, blocking collectives, on_device(): lax.all_to_all(send_rows, 'dp', split_axis=0, concat_axis=0, tiled=True)  50.1 us
    all_gather x1, waiting for transfers between devices, on_device(): full_rows = lax.all_gather(rows, 'tensor', axis=2, tiled=True)  26.7 us
    all_to_all x1, waiting for transfers between devices, on_device(): lax.all_to_all(hidden.reshape(dp_count, slot_count, -1), 'dp', split_axis...  25.4 us
    gather x2, local copies, waits for them, and re-layouts, on_device(): return (back_rows[pick_dest, pick_lane], back_values[pick_dest, pick_lane])  15 us
    dot_general x1, matrix products, on_device(): jnp.dot(mixed_heads, w_out, preferred_element_type=jnp.float32)  8.41 us
    all_to_all x1, blocking collectives, on_device(): lax.all_to_all(pos_send, 'dp', split_axis=0, concat_axis=0, tiled=True)  8.18 us
    dot_general x1, matrix products, projections(): jnp.einsum('...d,dc->...c', normed_hidden, w_query, preferred_element_typ...  8.12 us
  transfers between devices with their start and end apart: 4, of which 4 were waited for; matrix products, arithmetic and copies ran while one was open for 9% of the time, Pallas kernels for 0%

commit v1 on v0

v1 whole, which is shorter than its diff:
```python
import functools

import jax
import jax.numpy as jnp
from jax import lax
from jax.experimental import pallas as pl
from jax.experimental.pallas import tpu as pltpu
from jax.sharding import PartitionSpec as P

MODEL_WIDTH = 4096
HEAD_WIDTH = 128
NORM_EPS = 1e-05
ROPE_BASE = 500000.0

SEG_SPAN = 64
POS_SPAN = 1024

QUERY_BLOCK = 128
KEY_BLOCK = 256
MASKED = -1e30

VMEM = pltpu.VMEM


def params(limit_mib):
    return pltpu.CompilerParams(vmem_limit_bytes=limit_mib * 2**20)


def whole():
    return pl.BlockSpec(memory_space=VMEM)


def qkv_kernel(ids, r0, r1, r2, r3, gain, wq, wk, wv, cos, sin, q_out, kv_out):
    pieces = (r0, r1, r2, r3)
    width = r0.shape[1]
    square = jnp.zeros((r0.shape[0], 1), jnp.float32)
    for piece in pieces:
        x = piece[...].astype(jnp.float32)
        square += jnp.sum(x * x, -1, keepdims=True)
    scale = lax.rsqrt(square / MODEL_WIDTH + NORM_EPS)
    q = k = v = None
    for i, piece in enumerate(pieces):
        own = ids[i]
        x = piece[...].astype(jnp.float32)
        normed = (x * scale * gain[pl.ds(own, 1), :]).astype(jnp.bfloat16)
        at = pl.ds(pl.multiple_of(own * width, width), width)
        qi = jnp.dot(normed, wq[at, :], preferred_element_type=jnp.float32)
        ki = jnp.dot(normed, wk[at, :], preferred_element_type=jnp.float32)
        vi = jnp.dot(normed, wv[at, :], preferred_element_type=jnp.float32)
        q, k, v = (qi, ki, vi) if i == 0 else (q + qi, k + ki, v + vi)

    def rope(x):
        return (x * cos[...] + pltpu.roll(x, HEAD_WIDTH // 2, 1) * sin[...]).astype(jnp.bfloat16)

    for h in range(q_out.shape[0]):
        q_out[h] = rope(q[:, h * HEAD_WIDTH : (h + 1) * HEAD_WIDTH])
    kv_out[:, :HEAD_WIDTH] = rope(k)
    kv_out[:, HEAD_WIDTH:] = v.astype(jnp.bfloat16)


def qkv(ids, pieces, gain, wq, wk, wv, cos, sin):
    rows = pieces[0].shape[0]
    heads = wq.shape[1] // HEAD_WIDTH
    return pl.pallas_call(
        qkv_kernel,
        out_shape=(
            jax.ShapeDtypeStruct((heads, rows, HEAD_WIDTH), jnp.bfloat16),
            jax.ShapeDtypeStruct((rows, 2 * HEAD_WIDTH), jnp.bfloat16),
        ),
        in_specs=[pl.BlockSpec(memory_space=pltpu.SMEM)] + [whole()] * 10,
        out_specs=(whole(), whole()),
        compiler_params=params(24),
        cost_estimate=pl.CostEstimate(
            flops=2 * rows * MODEL_WIDTH * (wq.shape[1] + 2 * HEAD_WIDTH),
            bytes_accessed=MODEL_WIDTH * 2 * (rows + wq.shape[1] + 2 * HEAD_WIDTH),
            transcendentals=0,
        ),
        name="qkv",
    )(ids, *pieces, gain, wq, wk, wv, cos, sin)


def attend_kernel(n_chunk, n_shard, begin, end, *refs):
    q_in = refs[:n_chunk]
    kv_in = refs[n_chunk : n_chunk + n_chunk * n_shard]
    key_q, low_q, key_k, order, out, q_all, kv_all, heads, m_s, l_s, acc_s, sem = refs[
        n_chunk + n_chunk * n_shard :
    ]
    n_head, rows, _ = q_all.shape
    step = rows // n_chunk
    copies = []
    for c in range(n_chunk):
        copies.append(pltpu.make_async_copy(q_in[c], q_all.at[:, pl.ds(c * step, step), :], sem.at[c]))
    for i in range(n_chunk * n_shard):
        copies.append(
            pltpu.make_async_copy(kv_in[i], kv_all.at[pl.ds(i * step, step), :], sem.at[n_chunk + i])
        )
    for copy in copies:
        copy.start()
    for copy in copies:
        copy.wait()
    scale = 1.4426950408889634 / HEAD_WIDTH**0.5
    stacked = n_head * QUERY_BLOCK
    per_shard = rows // KEY_BLOCK

    def block(qb, _):
        at = pl.ds(pl.multiple_of(qb * QUERY_BLOCK, QUERY_BLOCK), QUERY_BLOCK)
        q = q_all[:, at, :].reshape(stacked, HEAD_WIDTH)
        high = key_q[at, :]
        low = low_q[at, :]
        m_s[...] = jnp.full(m_s.shape, MASKED, jnp.float32)
        l_s[...] = jnp.zeros(l_s.shape, jnp.float32)
        acc_s[...] = jnp.zeros(acc_s.shape, jnp.float32)

        def shard(d, _):
            def keys(kb, _):
                index = d * per_shard + kb
                span = pl.ds(pl.multiple_of(index * KEY_BLOCK, KEY_BLOCK), KEY_BLOCK)
                k = kv_all[span, :HEAD_WIDTH]
                v = kv_all[span, HEAD_WIDTH:]
                s = lax.dot_general(q, k, (((1,), (1,)), ((), ())), preferred_element_type=jnp.float32)
                ids = key_k[pl.ds(index, 1), :]
                allowed = (ids <= high) & (ids >= low)
                s = jnp.where(allowed[None], (s * scale).reshape(n_head, QUERY_BLOCK, KEY_BLOCK), MASKED)
                s = s.reshape(stacked, KEY_BLOCK)
                m_old = m_s[...]
                m_new = jnp.maximum(m_old, jnp.max(s, -1, keepdims=True))
                alpha = jnp.exp2(m_old - m_new)
                p = [
                    jnp.exp2(s[:, i : i + HEAD_WIDTH] - m_new) for i in range(0, KEY_BLOCK, HEAD_WIDTH)
                ]
                m_s[...] = m_new
                l_s[...] = l_s[...] * alpha + functools.reduce(jnp.add, p)
                p = jnp.concatenate(p, 1).astype(jnp.bfloat16)
                acc_s[...] = acc_s[...] * alpha + jnp.dot(p, v, preferred_element_type=jnp.float32)
                return 0

            return lax.fori_loop(begin[qb, d], end[qb, d], keys, 0)

        lax.fori_loop(0, n_shard, shard, 0)
        done = (acc_s[...] / jnp.sum(l_s[...], -1, keepdims=True)).astype(jnp.bfloat16)
        for h in range(n_head):
            heads[at, h * HEAD_WIDTH : (h + 1) * HEAD_WIDTH] = done[h * QUERY_BLOCK : (h + 1) * QUERY_BLOCK]
        return 0

    lax.fori_loop(0, rows // QUERY_BLOCK, block, 0)
    pick = (order[...] == lax.broadcasted_iota(jnp.int32, (rows, rows), 1)).astype(jnp.bfloat16)
    out[...] = jnp.dot(pick, heads[...], preferred_element_type=jnp.float32).astype(jnp.bfloat16)


def attend(begin, end, q_parts, kv_parts, key_q, low_q, key_k, order):
    n_chunk = len(q_parts)
    n_shard = len(kv_parts) // n_chunk
    n_head, step, _ = q_parts[0].shape
    rows = step * n_chunk
    stacked = n_head * QUERY_BLOCK
    smem = pl.BlockSpec(memory_space=pltpu.SMEM)
    return pl.pallas_call(
        functools.partial(attend_kernel, n_chunk, n_shard),
        out_shape=jax.ShapeDtypeStruct((rows, n_head * HEAD_WIDTH), jnp.bfloat16),
        in_specs=[smem, smem]
        + [pl.BlockSpec(memory_space=pl.ANY)] * (len(q_parts) + len(kv_parts))
        + [whole()] * 4,
        out_specs=whole(),
        scratch_shapes=[
            VMEM((n_head, rows, HEAD_WIDTH), jnp.bfloat16),
            VMEM((n_shard * rows, 2 * HEAD_WIDTH), jnp.bfloat16),
            VMEM((rows, n_head * HEAD_WIDTH), jnp.bfloat16),
            VMEM((stacked, HEAD_WIDTH), jnp.float32),
            VMEM((stacked, HEAD_WIDTH), jnp.float32),
            VMEM((stacked, HEAD_WIDTH), jnp.float32),
            pltpu.SemaphoreType.DMA((len(q_parts) + len(kv_parts),)),
        ],
        compiler_params=params(32),
        cost_estimate=pl.CostEstimate(
            flops=4 * rows * rows * n_shard * n_head * HEAD_WIDTH,
            bytes_accessed=4 * rows * n_head * HEAD_WIDTH + 4 * rows * n_shard * HEAD_WIDTH,
            transcendentals=rows * rows * n_shard * n_head,
        ),
        name="attend",
    )(begin, end, *q_parts, *kv_parts, key_q, low_q, key_k, order)


def project_kernel(ids, h0, h1, w0, w1, out):
    total = jnp.dot(h0[...], w0[...], preferred_element_type=jnp.float32)
    total += jnp.dot(h1[...], w1[...], preferred_element_type=jnp.float32)
    out[...] = total.astype(out.dtype)


def project(ids, h0, h1, w0, w1, width, part, n_part):
    rows, depth = h0.shape
    step = rows // n_part
    return pl.pallas_call(
        project_kernel,
        grid_spec=pltpu.PrefetchScalarGridSpec(
            num_scalar_prefetch=1,
            grid=(1,),
            in_specs=[
                pl.BlockSpec((step, depth), lambda i, ids: (part, 0)),
                pl.BlockSpec((step, depth), lambda i, ids: (part, 0)),
                pl.BlockSpec((depth, width), lambda i, ids: (0, ids[0])),
                pl.BlockSpec((depth, width), lambda i, ids: (0, ids[1])),
            ],
            out_specs=pl.BlockSpec((step, width), lambda i, ids: (0, 0)),
        ),
        out_shape=jax.ShapeDtypeStruct((step, width), jnp.bfloat16),
        compiler_params=params(24),
        cost_estimate=pl.CostEstimate(
            flops=4 * step * depth * width, bytes_accessed=4 * depth * width, transcendentals=0
        ),
        name="project",
    )(ids, h0, h1, w0, w1)


def keep_kernel(ids, order, own, h0, h1, w0, w1, out):
    rows = own.shape[0]
    pick = (order[...] == lax.broadcasted_iota(jnp.int32, (rows, rows), 1)).astype(jnp.bfloat16)
    total = jnp.dot(h0[...], w0[...], preferred_element_type=jnp.float32)
    total += jnp.dot(h1[...], w1[...], preferred_element_type=jnp.float32)
    out[...] = total + jnp.dot(pick, own[...], preferred_element_type=jnp.float32)


def keep(ids, order, own, h0, h1, w0, w1):
    rows, width = own.shape
    depth = h0.shape[1]
    return pl.pallas_call(
        keep_kernel,
        grid_spec=pltpu.PrefetchScalarGridSpec(
            num_scalar_prefetch=1,
            grid=(1,),
            in_specs=[
                pl.BlockSpec((rows, 1), lambda i, ids: (0, 0)),
                pl.BlockSpec((rows, width), lambda i, ids: (0, 0)),
                pl.BlockSpec((rows, depth), lambda i, ids: (0, 0)),
                pl.BlockSpec((rows, depth), lambda i, ids: (0, 0)),
                pl.BlockSpec((depth, width), lambda i, ids: (0, ids[0])),
                pl.BlockSpec((depth, width), lambda i, ids: (0, ids[1])),
            ],
            out_specs=pl.BlockSpec((rows, width), lambda i, ids: (0, 0)),
        ),
        out_shape=jax.ShapeDtypeStruct((rows, width), jnp.float32),
        compiler_params=params(32),
        cost_estimate=pl.CostEstimate(
            flops=2 * rows * (2 * depth + rows) * width,
            bytes_accessed=4 * depth * width + 6 * rows * width,
            transcendentals=0,
        ),
        name="keep",
    )(ids, order, own, h0, h1, w0, w1)


def finish_kernel(kept, received, gain, head, *refs):
    hidden_out, sums = refs[-2:]
    hidden = (kept[...] + received[...].astype(jnp.float32)).astype(jnp.bfloat16)
    hidden_out[...] = hidden
    x = hidden.astype(jnp.float32)
    weighted = x * (gain[...] * head[...])
    squared = x * x
    for i, terms in enumerate((squared, weighted)):
        lanes = functools.reduce(
            jnp.add, [terms[:, j : j + 128] for j in range(0, terms.shape[1], 128)]
        )
        sums[i : i + 1, :] = jnp.sum(lanes.T, 0, keepdims=True)


def finish(kept, received, gain, head, part, n_part, hidden):
    rows, width = kept.shape
    step = rows // n_part
    specs = [
        pl.BlockSpec((step, width), lambda i: (part, 0)),
        pl.BlockSpec((step, width), lambda i: (0, 0)),
        pl.BlockSpec((1, width), lambda i: (0, 0)),
        pl.BlockSpec((1, width), lambda i: (0, 0)),
    ]
    args = [kept, received, gain, head]
    aliases = {}
    if hidden is not None:
        specs.append(pl.BlockSpec(memory_space=pl.ANY))
        args.append(hidden)
        aliases = {4: 0}
    return pl.pallas_call(
        finish_kernel,
        grid=(1,),
        in_specs=specs,
        out_specs=(
            pl.BlockSpec((step, width), lambda i: (part, 0)),
            pl.BlockSpec((2, step), lambda i: (0, 0)),
        ),
        out_shape=(
            jax.ShapeDtypeStruct((rows, width), jnp.bfloat16),
            jax.ShapeDtypeStruct((2, step), jnp.float32),
        ),
        input_output_aliases=aliases,
        compiler_params=params(24),
        cost_estimate=pl.CostEstimate(
            flops=6 * step * width, bytes_accessed=8 * step * width, transcendentals=0
        ),
        name="finish",
    )(*args)


def flip(x, bit):
    count = lax.axis_size("tensor")
    return lax.ppermute(x, "tensor", [(i, i ^ bit) for i in range(count)])


def on_device(
    hidden_in,
    row_loads,
    seg_ids,
    pos_ids,
    prompt_order,
    attn_gain,
    w_query,
    key_matrix,
    value_matrix,
    w_out,
    final_gain,
    value_head,
):
    n_dp = lax.axis_size("dp")
    me = lax.axis_index("dp")
    t = lax.axis_index("tensor")
    rows, width = hidden_in.shape
    n_chunk = 4 if n_dp <= 8 else 1
    n_part = 2
    step = rows // n_chunk

    w_blocks = w_out.reshape(w_out.shape[0], 2, 2, width)
    w_send = lax.dynamic_index_in_dim(w_blocks, 1 - t % 2, 2, keepdims=False)
    w_other = flip(w_send.reshape(w_out.shape[0], 2 * width), 1)

    own = [hidden_in[c * step : (c + 1) * step] for c in range(n_chunk)]
    pair = flip(hidden_in, 1)
    pairs = [pair[c * step : (c + 1) * step] for c in range(n_chunk)]
    across = [flip(x, 2) for x in own]
    diagonal = [flip(x, 1) for x in across]

    block_end = jnp.sum(
        jnp.where(jnp.arange(n_dp)[:, None] <= jnp.arange(n_dp)[None, :], row_loads[0][:, None], 0), 0
    )
    row_ids = jnp.arange(rows, dtype=jnp.int32)
    dest_of = jnp.sum((block_end[:, None] <= row_ids[None, :]).astype(jnp.int32), 0)
    key_own = (dest_of * SEG_SPAN + seg_ids) * POS_SPAN + pos_ids
    key_all = lax.all_gather(key_own, "dp", axis=0)
    shard_of = me - jnp.arange(n_dp)
    key_k = key_all[shard_of % n_dp]
    doc_q = (key_own // POS_SPAN).reshape(-1, QUERY_BLOCK)
    doc_k = (key_k // POS_SPAN).reshape(n_dp, -1, KEY_BLOCK)
    first_q, last_q = doc_q[:, 0], doc_q[:, -1]
    first_k, last_k = doc_k[:, :, 0], doc_k[:, :, -1]
    begin = jnp.sum((last_k[None] < first_q[:, None, None]).astype(jnp.int32), 2)
    end = jnp.sum((first_k[None] <= last_q[:, None, None]).astype(jnp.int32), 2)
    end = jnp.where(shard_of[None, :] >= 0, end, 0)

    half = HEAD_WIDTH // 2
    inverse = ROPE_BASE ** (-(jnp.arange(half, dtype=jnp.float32) * 2.0) / HEAD_WIDTH)
    angles = pos_ids.astype(jnp.float32)[:, None] * inverse
    cosine, sine = jnp.cos(angles), jnp.sin(angles)
    cos = jnp.concatenate([cosine, cosine], 1)
    sin = jnp.concatenate([-sine, sine], 1)
    gain = attn_gain.astype(jnp.float32).reshape(-1, width)
    ids = jnp.stack([t, t ^ 1, t ^ 2, t ^ 3]).astype(jnp.int32)

    q_parts, kv_parts = [], [[] for _ in range(n_dp)]
    for c in range(n_chunk):
        span = slice(c * step, (c + 1) * step)
        q, kv = qkv(
            ids,
            (own[c], pairs[c], across[c], diagonal[c]),
            gain,
            w_query,
            key_matrix,
            value_matrix,
            cos[span],
            sin[span],
        )
        q_parts.append(q)
        kv_parts[0].append(kv)
        for d in range(1, n_dp):
            kv_parts[d].append(lax.ppermute(kv, "dp", [(i, i + d) for i in range(n_dp - d)]))

    order = prompt_order.reshape(rows, 1)
    heads = attend(
        begin,
        end,
        q_parts,
        [kv for parts in kv_parts for kv in parts],
        key_own.reshape(rows, 1),
        (key_own // POS_SPAN * POS_SPAN).reshape(rows, 1),
        key_k.reshape(-1, KEY_BLOCK),
        order,
    )
    heads_other = flip(heads, 1)
    far = jnp.stack([t ^ 2, 1 - t // 2]).astype(jnp.int32)
    near = jnp.stack([t, t // 2]).astype(jnp.int32)
    sent = [
        flip(project(far, heads, heads_other, w_out, w_other, width, j, n_part), 2)
        for j in range(n_part)
    ]
    kept = keep(near, order, hidden_in, heads, heads_other, w_out, w_other)
    final = final_gain.astype(jnp.float32).reshape(1, width)
    head = value_head.astype(jnp.float32).reshape(1, width)
    hidden, sums = None, []
    for j in range(n_part):
        hidden, part = finish(kept, sent[j], final, head, j, n_part, hidden)
        sums.append(part)
    square, product = lax.psum(jnp.concatenate(sums, 1), "tensor")
    return hidden, product * lax.rsqrt(square / MODEL_WIDTH + NORM_EPS)


def solution(mesh):
    return jax.shard_map(
        on_device,
        mesh=mesh,
        in_specs=(
            P(("parts", "dp"), "tensor"),
            P(("parts", "dp"), None),
            P(("parts", "dp")),
            P(("parts", "dp")),
            P(("parts", "dp"), None),
            P(),
            P(None, "tensor"),
            P(None, "tensor"),
            P(None, "tensor"),
            P("tensor", None),
            P("tensor"),
            P("tensor"),
        ),
        out_specs=(P(("parts", "dp"), "tensor"), P(("parts", "dp"))),
        check_vma=False,
    )
```

time: 390 us -> 176 us (0.45)
  the two profiles are of different devices: /device:TPU:9 before, /device:TPU:28 now
where the time goes in v1:
time: 176 us; the launch traced here: 174 us
  local copies, waits for them, and re-layouts  56.4 us (32%)
  Pallas kernels  34.1 us (19%)
  waiting for transfers between devices  33.7 us (19%)
  starting transfers between devices  23.2 us (13%)
  blocking collectives  16.5 us (9%)
  other arithmetic  9.17 us (5%)
    unnamed x86, local copies, waits for them, and re-layouts  23 us
    ppermute x13, waiting for transfers between devices, flip(): return lax.ppermute(x, 'tensor', [(i, i ^ bit) for i in range(count)])  21.4 us
    ppermute x12, starting transfers between devices, on_device(): lax.ppermute(kv, 'dp', [(i, i + d) for i in range(n_dp - d)])  15.7 us
    dynamic_slice x1, local copies, waits for them, and re-layouts, on_device(): w_send = lax.dynamic_index_in_dim(w_blocks, 1 - t % 2, 2, keepdims=False)  15.6 us
    pallas_call x1, Pallas kernels, attend(): pl.pallas_call(functools.partial(attend_kernel, n_chunk, n_shard), out_sh...  14.3 us
    pallas_call x4, Pallas kernels, qkv(): pl.pallas_call(qkv_kernel, out_shape=(jax.ShapeDtypeStruct((heads, rows,...  12.9 us
    ppermute x12, waiting for transfers between devices, on_device(): lax.ppermute(kv, 'dp', [(i, i + d) for i in range(n_dp - d)])  12.3 us
    all_gather x1, blocking collectives, on_device(): key_all = lax.all_gather(key_own, 'dp', axis=0)  10.6 us
  transfers between devices with their start and end apart: 25, of which 10 were waited for; matrix products, arithmetic and copies ran while one was open for 25% of the time, Pallas kernels for 18%

profile of v1, /device:TPU:28, one launch (start us, length us, event | category | flops | bytes accessed | tf_op | source)
XLA Modules:
  0.0 174.2 jit_solution(77429111280644560)
XLA Ops:
  0.7 2.1 %fusion.16 = (bf16[128,1024]{1,0:T(8,128)(2,1)S(1)}, bf16[128,1024]{1,0:T(8,128)(2,1)}, bf16[128,1024]{1,0:T(8,128)(2,1)}, bf16[128,1024]{1,0:T(8,128)(2,1)}) fusion(bf16[512,1024]{1,0:T(8,128)(2,1)} %own.1), kind=kLoop, calls=%fused_computation.69 | loop fusion | bytes 2097152 | tf_op jit(solution)/shard_map/slice | solution.py:332
  2.8 1.5 collective-permute-start.1
  4.9 1.5 collective-permute-start.5
  6.3 7.8 %reshape.125 = bf16[512,2,2,1024]{3,2,1,0:T(2,128)(2,1)} reshape(bf16[512,4096]{1,0:T(8,128)(2,1)} %w0.5) | data formatting | bytes 8388608 | tf_op jit(solution)/shard_map/reshape | solution.py:328
  14.2 15.6 %dynamic-slice_reduce_fusion = bf16[512,2,1024]{2,1,0:T(2,128)(2,1)S(1)} fusion(bf16[512,2,2,1024]{3,2,1,0:T(2,128)(2,1)} %reshape.125, s32[]{:T(128)S(6)} %select_n.67), kind=kLoop, calls=%fused_computation.1 | loop fusion | bytes 4194308 | tf_op jit(solution)/shard_map/jit(dynamic_index_in_dim)/dynamic_slice | solution.py:329
  29.8 2.0 %copy.66 = bf16[64,8,2,1024]{3,1,2,0:T(8,128)(2,1)} copy(bf16[64,8,2,1024]{3,2,1,0:T(2,128)(2,1)S(1)} %bitcast.31) | data formatting | bytes 4194304
  32.5 10.6 %all-gather.1 = s32[4,1,512]{2,1,0:T(1,128)S(1)} all-gather(s32[1,1,512]{2,1,0:T(1,128)S(1)} %bitcast.33), channel_id=2, replica_groups=mesh['parts'=2,'dp'=4,'tensor'=4] {'dp'}, dimensions={0}, use_global_device_ids=true | all-gather | bytes 10240 | tf_op jit(solution)/shard_map/all_gather | solution.py:344
  43.8 0.9 copy.55
  44.6 1.5 and_select_fusion
  46.2 1.9 %multiply_sine_fusion = (f32[512,64]{1,0:T(8,128)}, f32[512,64]{1,0:T(8,128)}, f32[512,64]{1,0:T(8,128)}) fusion(f32[64]{0:T(128)S(1)} %multiply_power_fusion, f32[512]{0:T(512)S(1)} %get-tuple-element.51), kind=kLoop, calls=%fused_computation.6 | loop fusion | flops 65536 | bytes 395520 | tf_op jit(solution)/shard_map/sin | solution.py:358
  50.5 2.2 %pad_maximum_fusion = (f32[128,128]{1,0:T(8,128)S(1)}, f32[128,128]{1,0:T(8,128)}, f32[128,128]{1,0:T(8,128)}, f32[128,128]{1,0:T(8,128)}, f32[128,128]{1,0:T(8,...) fusion(f32[512,64]{1,0:T(8,128)} %get-tuple-element.48, f32[512,64]{1,0:T(8,128)} %get-tuple-element.49, ...), kind=kLoop, calls=%fused_computation.27 | loop fusion | flops 131072 | bytes 917504 | tf_op jit(solution)/shard_map/concatenate | solution.py:360
  54.6 1.2 collective-permute-done.7.r2
  56.3 1.3 fusion.15
  57.7 2.2 %copy-done = bf16[4096,512]{1,0:T(8,128)(2,1)S(1)} copy-done((bf16[4096,512]{1,0:T(8,128)(2,1)S(1)}, bf16[4096,512]{1,0:T(8,128)(2,1)}, u32[]{:S(2)}) %copy-start) | copy-done | bytes 4194328
  59.9 1.2 copy-done.5
  61.1 0.8 copy-done.11
  61.9 0.8 copy-done.12
  63.4 3.5 %qkv.4 = (bf16[4,128,128]{2,1,0:T(8,128)(2,1)S(1)}, bf16[128,256]{1,0:T(8,128)(2,1)}) custom-call(s32[4]{0:T(128)S(1)} %copy-done.13, bf16[128,1024]{1,0:T(8,128)(2,1)} %get-tuple-element.37.r0, bf16[128,1024]{1,0:T(8,128)(2,1)S(1)} %get-tuple-element.33.r1, bf16[128,1024]{1,0:T(8,128)(2,1)} %collective-permute-done.1.r2, ...), custom_call_target="tpu_custom_call" | custom-call | flops 805306368 | bytes 7340032 | tf_op jit(solution)/shard_map/qkv/pallas_call | solution.py:64
  66.9 1.4 collective-permute-start.9
  68.4 3.2 %qkv.5 = (bf16[4,128,128]{2,1,0:T(8,128)(2,1)S(1)}, bf16[128,256]{1,0:T(8,128)(2,1)}) custom-call(s32[4]{0:T(128)S(1)} %copy-done.13, bf16[128,1024]{1,0:T(8,128)(2,1)} %get-tuple-element.36.r0, bf16[128,1024]{1,0:T(8,128)(2,1)S(1)} %get-tuple-element.32.r1, bf16[128,1024]{1,0:T(8,128)(2,1)} %collective-permute-done.3.r2, ...), custom_call_target="tpu_custom_call" | custom-call | flops 805306368 | bytes 7340032 | tf_op jit(solution)/shard_map/qkv/pallas_call | solution.py:64
  71.6 1.5 collective-permute-start.10
  73.1 3.2 %qkv.6 = (bf16[4,128,128]{2,1,0:T(8,128)(2,1)S(1)}, bf16[128,256]{1,0:T(8,128)(2,1)}) custom-call(s32[4]{0:T(128)S(1)} %copy-done.13, bf16[128,1024]{1,0:T(8,128)(2,1)} %get-tuple-element.35.r0, bf16[128,1024]{1,0:T(8,128)(2,1)S(1)} %get-tuple-element.31.r1, bf16[128,1024]{1,0:T(8,128)(2,1)} %collective-permute-done.5.r2, ...), custom_call_target="tpu_custom_call" | custom-call | flops 805306368 | bytes 7340032 | tf_op jit(solution)/shard_map/qkv/pallas_call | solution.py:64
  76.3 1.3 collective-permute-start.11
  77.6 3.1 %qkv.7 = (bf16[4,128,128]{2,1,0:T(8,128)(2,1)S(1)}, bf16[128,256]{1,0:T(8,128)(2,1)}) custom-call(s32[4]{0:T(128)S(1)} %copy-done.13, bf16[128,1024]{1,0:T(8,128)(2,1)S(1)} %get-tuple-element.34.r0, bf16[128,1024]{1,0:T(8,128)(2,1)S(1)} %get-tuple-element.30.r1, bf16[128,1024]{1,0:T(8,128)(2,1)} %collective-permute-done.7.r2, ...), custom_call_target="tpu_custom_call" | custom-call | flops 805306368 | bytes 7340032 | tf_op jit(solution)/shard_map/qkv/pallas_call | solution.py:64
  81.3 1.3 collective-permute-start.12
  83.3 1.3 collective-permute-start.13
  85.2 1.3 collective-permute-start.14
  87.1 1.3 collective-permute-start.15
  88.4 1.2 collective-permute-done.12.refs_11_
  89.6 1.3 collective-permute-start.16
  91.6 0.8 copy.63.refs_23_.order
  92.4 0.8 copy.59.refs_20_
  93.3 0.8 copy.60.refs_21_
  94.1 1.3 collective-permute-done.13.refs_12_
  95.4 1.3 collective-permute-start.17
  96.7 3.6 %collective-permute-done.14.refs_13_ = bf16[128,256]{1,0:T(8,128)(2,1)S(1)} collective-permute-done((bf16[128,256]{1,0:T(8,128)(2,1)}, bf16[128,256]{1,0:T(8,128)(2,1)S(1)}, u32[]{:S(2)}, u32[]{:S(2)}) %collective-permute-start.14) | collective-permute-done | bytes 65568 | tf_op jit(solution)/shard_map/ppermute | solution.py:380
  101.0 1.3 collective-permute-start.18
  102.9 1.3 collective-permute-start.19
  104.8 1.3 collective-permute-start.20
  106.9 2.8 %collective-permute-done.18.refs_17_ = bf16[128,256]{1,0:T(8,128)(2,1)S(1)} collective-permute-done((bf16[128,256]{1,0:T(8,128)(2,1)}, bf16[128,256]{1,0:T(8,128)(2,1)S(1)}, u32[]{:S(2)}, u32[]{:S(2)}) %collective-permute-start.18) | collective-permute-done | bytes 65568 | tf_op jit(solution)/shard_map/ppermute | solution.py:380
  109.7 2.1 %collective-permute-done.19.refs_18_ = bf16[128,256]{1,0:T(8,128)(2,1)S(1)} collective-permute-done((bf16[128,256]{1,0:T(8,128)(2,1)}, bf16[128,256]{1,0:T(8,128)(2,1)S(1)}, u32[]{:S(2)}, u32[]{:S(2)}) %collective-permute-start.19) | collective-permute-done | bytes 65568 | tf_op jit(solution)/shard_map/ppermute | solution.py:380
  111.7 1.3 collective-permute-done.20.refs_19_
  113.0 0.9 copy-done.15
  113.9 0.9 copy-done.17
  114.8 0.9 copy-done.19
  115.7 0.9 copy-done.21
  116.6 0.8 copy-done.23
  117.4 0.8 copy-done.25
  118.3 0.8 copy-done.27
  119.1 0.8 copy-done.29
  120.0 0.8 copy-done.31
  120.8 0.8 copy-done.33
  121.6 14.3 %attend.1.h0 = bf16[512,512]{1,0:T(8,128)(2,1)S(1)} custom-call(s32[4,4]{1,0:T(4,128)S(1)} %convert_reduce_fusion.2.begin, s32[4,4]{1,0:T(4,128)S(1)} %broadcast_select_fusion.end, bf16[4,128,128]{2,1,0:T(8,128)(2,1)S(1)} %copy-done.15, bf16[4,128,128]{2,1,0:T(8,128)(2,1)S(1)} %copy-done.17, bf16[4,128,128]{2,1,0:T(8,128)(2,1)S(1)} %copy-done.19, ...), custom_call_target="tpu_custom_call" | custom-call | flops 2147483648 | bytes 2097152 | tf_op jit(solution)/shard_map/attend/pallas_call | solution.py:157
  136.1 1.8 %collective-permute-done.21.h1 = bf16[512,512]{1,0:T(8,128)(2,1)S(1)} collective-permute-done((bf16[512,512]{1,0:T(8,128)(2,1)S(1)}, bf16[512,512]{1,0:T(8,128)(2,1)S(1)}, u32[]{:S(2)}, u32[]{:S(2)}) %collective-permute-start.21) | collective-permute-done | bytes 524320 | tf_op jit(solution)/shard_map/ppermute | solution.py:303
  137.9 2.2 %copy-done.2 = bf16[512,4096]{1,0:T(8,128)(2,1)S(1)} copy-done((bf16[512,4096]{1,0:T(8,128)(2,1)S(1)}, bf16[512,4096]{1,0:T(8,128)(2,1)}, u32[]{:S(2)}) %copy-start.2) | copy-done | bytes 4194328
  140.1 1.3 project.3
  142.0 1.3 project.2
  143.3 1.6 collective-permute-start.23
  145.0 2.4 %keep.1.kept = f32[512,1024]{1,0:T(8,128)S(1)} custom-call(s32[2]{0:T(128)S(1)} %pad_add_fusion.ids, s32[512,1]{1,0:T(8,128)S(1)} %copy.63.refs_23_.order, bf16[512,1024]{1,0:T(8,128)(2,1)S(1)} %copy-done.6, bf16[512,512]{1,0:T(8,128)(2,1)S(1)} %attend.1.h0, bf16[512,512]{1,0:T(8,128)(2,1)S(1)} %collective-permute-done.21.h1, ...), custom_call_target="tpu_custom_call" | custom-call | flops 1610612736 | bytes 5242880 | tf_op jit(solution)/shard_map/keep/pallas_call | solution.py:225
  147.3 8.9 %collective-permute-done.24.received = bf16[256,1024]{1,0:T(8,128)(2,1)S(1)} collective-permute-done((bf16[256,1024]{1,0:T(8,128)(2,1)S(1)}, bf16[256,1024]{1,0:T(8,128)(2,1)S(1)}, u32[]{:S(2)}, u32[]{:S(2)}) %collective-permute-start.24) | collective-permute-done | bytes 524320 | tf_op jit(solution)/shard_map/ppermute | solution.py:303
  156.3 1.0 finish.2
  157.3 9.4 %collective-permute-done.23.received = bf16[256,1024]{1,0:T(8,128)(2,1)S(1)} collective-permute-done((bf16[256,1024]{1,0:T(8,128)(2,1)S(1)}, bf16[256,1024]{1,0:T(8,128)(2,1)S(1)}, u32[]{:S(2)}, u32[]{:S(2)}) %collective-permute-start.23) | collective-permute-done | bytes 524320 | tf_op jit(solution)/shard_map/ppermute | solution.py:303
  166.7 1.0 finish.3
  167.7 5.9 %psum.7 = f32[2,512]{1,0:T(2,128)S(1)} all-reduce(f32[2,512]{1,0:T(2,128)S(1)} %pad_maximum_fusion.2), channel_id=1, replica_groups=mesh['parts'=2,'dp'=4,'tensor'=4] {'tensor'}, use_global_device_ids=true, to_apply=%region_4.5 | all-reduce | flops 1024 | bytes 8192 | tf_op jit(solution)/shard_map/psum | solution.py:407
  (119 shorter events, 15.0 us)
Async XLA Ops:
  0.6 55.2 %collective-permute-start = (bf16[512,1024]{1,0:T(8,128)(2,1)}, bf16[512,1024]{1,0:T(8,128)(2,1)}, u32[]{:S(2)}, u32[]{:S(2)}) collective-permute-start(bf16[512,1024]{1,0:T(8,128)(2,1)} %own.1), channel_id=1, source_target_pairs={{0,1},{1,0},{2,3},{3,2},{4,5},{5,4},{6,7},{7,6},{8,9},{9,8},{10,11... | collective-permute-start | bytes 3145736 | tf_op jit(solution)/shard_map/ppermute | solution.py:303
  2.8 46.5 %collective-permute-start.1 = (bf16[128,1024]{1,0:T(8,128)(2,1)}, bf16[128,1024]{1,0:T(8,128)(2,1)}, u32[]{:S(2)}, u32[]{:S(2)}) collective-permute-start(bf16[128,1024]{1,0:T(8,128)(2,1)} %get-tuple-element.37.r0), channel_id=1, source_target_pairs={{0,2},{1,3},{2,0},{3,1},{4,6},{5,7},{6,4},{7,5},{8,10},{9,11},{10,... | collective-permute-start | bytes 786440 | tf_op jit(solution)/shard_map/ppermute | solution.py:303
  4.3 48.4 %collective-permute-start.3 = (bf16[128,1024]{1,0:T(8,128)(2,1)}, bf16[128,1024]{1,0:T(8,128)(2,1)}, u32[]{:S(2)}, u32[]{:S(2)}) collective-permute-start(bf16[128,1024]{1,0:T(8,128)(2,1)} %get-tuple-element.36.r0), channel_id=1, source_target_pairs={{0,2},{1,3},{2,0},{3,1},{4,6},{5,7},{6,4},{7,5},{8,10},{9,11},{10,... | collective-permute-start | bytes 786440 | tf_op jit(solution)/shard_map/ppermute | solution.py:303
  4.9 49.2 %collective-permute-start.5 = (bf16[128,1024]{1,0:T(8,128)(2,1)}, bf16[128,1024]{1,0:T(8,128)(2,1)}, u32[]{:S(2)}, u32[]{:S(2)}) collective-permute-start(bf16[128,1024]{1,0:T(8,128)(2,1)} %get-tuple-element.35.r0), channel_id=1, source_target_pairs={{0,2},{1,3},{2,0},{3,1},{4,6},{5,7},{6,4},{7,5},{8,10},{9,11},{10,... | collective-permute-start | bytes 786440 | tf_op jit(solution)/shard_map/ppermute | solution.py:303
  14.2 17.6 %copy-start.41 = (s32[1,4]{1,0:T(1,128)S(1)}, s32[1,4]{1,0:T(1,128)}, u32[]{:S(2)}) copy-start(s32[1,4]{1,0:T(1,128)} %param.13) | copy-start | bytes 52
  14.2 17.8 %copy-start.39 = (s32[512]{0:T(512)S(1)}, s32[512]{0:T(512)}, u32[]{:S(2)}) copy-start(s32[512]{0:T(512)} %param.15) | copy-start | bytes 6148
  14.2 17.8 %copy-start.40 = (s32[512]{0:T(512)S(1)}, s32[512]{0:T(512)}, u32[]{:S(2)}) copy-start(s32[512]{0:T(512)} %param.14) | copy-start | bytes 6148
  29.8 27.9 %copy-start.4 = (bf16[4096,128]{1,0:T(8,128)(2,1)S(1)}, bf16[4096,128]{1,0:T(8,128)(2,1)}, u32[]{:S(2)}) copy-start(bf16[4096,128]{1,0:T(8,128)(2,1)} %wk.7) | copy-start | bytes 3145732
  31.7 106.2 %collective-permute-start.22 = (bf16[512,2048]{1,0:T(8,128)(2,1)}, bf16[512,2048]{1,0:T(8,128)(2,1)S(1)}, u32[]{:S(2)}, u32[]{:S(2)}) collective-permute-start(bf16[512,2048]{1,0:T(8,128)(2,1)} %bitcast.20), channel_id=1, source_target_pairs={{0,1},{1,0},{2,3},{3,2},{4,5},{5,4},{6,7},{7,6},{8,9},{9,8},{10,11... | collective-permute-start | bytes 6291464 | tf_op jit(solution)/shard_map/ppermute | solution.py:303
  32.5 18.0 %copy-start.35 = (s32[512]{0:T(512)}, s32[512]{0:T(512)S(1)}, u32[]{:S(2)}) copy-start(s32[512]{0:T(512)S(1)} %get-tuple-element.29) | copy-start | bytes 6148
  43.7 6.8 %copy-start.34 = (s32[4,512]{1,0:T(4,128)}, s32[4,512]{1,0:T(4,128)S(1)}, u32[]{:S(2)}) copy-start(s32[4,512]{1,0:T(4,128)S(1)} %gather_fusion) | copy-start | bytes 24580
  49.3 6.5 %collective-permute-start.7 = (bf16[128,1024]{1,0:T(8,128)(2,1)S(1)}, bf16[128,1024]{1,0:T(8,128)(2,1)}, u32[]{:S(2)}, u32[]{:S(2)}) collective-permute-start(bf16[128,1024]{1,0:T(8,128)(2,1)S(1)} %get-tuple-element.34.r0), channel_id=1, source_target_pairs={{0,2},{1,3},{2,0},{3,1},{4,6},{5,7},{6,4},{7,5},{8,10},{9,11},{10,... | collective-permute-start | bytes 786440 | tf_op jit(solution)/shard_map/ppermute | solution.py:303
  52.7 5.0 %collective-permute-start.2 = (bf16[128,1024]{1,0:T(8,128)(2,1)}, bf16[128,1024]{1,0:T(8,128)(2,1)}, u32[]{:S(2)}, u32[]{:S(2)}) collective-permute-start(bf16[128,1024]{1,0:T(8,128)(2,1)} %collective-permute-done.1.r2), channel_id=1, source_target_pairs={{0,1},{1,0},{2,3},{3,2},{4,5},{5,4},{6,7},{7,6},{8,9},{9,8},{10,11... | collective-permute-start | bytes 786440 | tf_op jit(solution)/shard_map/ppermute | solution.py:303
  54.1 14.3 %collective-permute-start.4 = (bf16[128,1024]{1,0:T(8,128)(2,1)}, bf16[128,1024]{1,0:T(8,128)(2,1)S(1)}, u32[]{:S(2)}, u32[]{:S(2)}) collective-permute-start(bf16[128,1024]{1,0:T(8,128)(2,1)} %collective-permute-done.3.r2), channel_id=1, source_target_pairs={{0,1},{1,0},{2,3},{3,2},{4,5},{5,4},{6,7},{7,6},{8,9},{9,8},{10,11... | collective-permute-start | bytes 786440 | tf_op jit(solution)/shard_map/ppermute | solution.py:303
  55.8 17.2 %collective-permute-start.6 = (bf16[128,1024]{1,0:T(8,128)(2,1)}, bf16[128,1024]{1,0:T(8,128)(2,1)S(1)}, u32[]{:S(2)}, u32[]{:S(2)}) collective-permute-start(bf16[128,1024]{1,0:T(8,128)(2,1)} %collective-permute-done.5.r2), channel_id=1, source_target_pairs={{0,1},{1,0},{2,3},{3,2},{4,5},{5,4},{6,7},{7,6},{8,9},{9,8},{10,11... | collective-permute-start | bytes 786440 | tf_op jit(solution)/shard_map/ppermute | solution.py:303
  55.8 21.7 %collective-permute-start.8 = (bf16[128,1024]{1,0:T(8,128)(2,1)}, bf16[128,1024]{1,0:T(8,128)(2,1)S(1)}, u32[]{:S(2)}, u32[]{:S(2)}) collective-permute-start(bf16[128,1024]{1,0:T(8,128)(2,1)} %collective-permute-done.7.r2), channel_id=1, source_target_pairs={{0,1},{1,0},{2,3},{3,2},{4,5},{5,4},{6,7},{7,6},{8,9},{9,8},{10,11... | collective-permute-start | bytes 786440 | tf_op jit(solution)/shard_map/ppermute | solution.py:303
  56.3 12.0 %copy-start.9 = (f32[128,128]{1,0:T(8,128)S(1)}, f32[128,128]{1,0:T(8,128)}, u32[]{:S(2)}) copy-start(f32[128,128]{1,0:T(8,128)} %get-tuple-element.39.sin) | copy-start | bytes 196612
  56.3 12.1 %copy-start.10 = (f32[128,128]{1,0:T(8,128)S(1)}, f32[128,128]{1,0:T(8,128)}, u32[]{:S(2)}) copy-start(f32[128,128]{1,0:T(8,128)} %get-tuple-element.54.cos) | copy-start | bytes 196612
  57.7 2.2 %copy-start = (bf16[4096,512]{1,0:T(8,128)(2,1)S(1)}, bf16[4096,512]{1,0:T(8,128)(2,1)}, u32[]{:S(2)}) copy-start(bf16[4096,512]{1,0:T(8,128)(2,1)} %wq.7) | copy-start | bytes 12582916
  59.9 1.2 copy-start.5
  61.1 0.8 copy-start.11
  61.9 0.8 copy-start.12
  62.8 0.7 copy-start.13
  63.4 5.0 %copy-start.1 = (bf16[4096,512]{1,0:T(8,128)(2,1)S(1)}, bf16[4096,512]{1,0:T(8,128)(2,1)}, u32[]{:S(2)}) copy-start(bf16[4096,512]{1,0:T(8,128)(2,1)} %wq.7) | copy-start | bytes 12582916
  66.9 9.3 %copy-start.14 = (bf16[4,128,128]{2,1,0:T(8,128)(2,1)}, bf16[4,128,128]{2,1,0:T(8,128)(2,1)S(1)}, u32[]{:S(2)}) copy-start(bf16[4,128,128]{2,1,0:T(8,128)(2,1)S(1)} %get-tuple-element.14.refs_0_) | copy-start | bytes 393220
  66.9 6.1 %copy-start.7 = (f32[128,128]{1,0:T(8,128)S(1)}, f32[128,128]{1,0:T(8,128)}, u32[]{:S(2)}) copy-start(f32[128,128]{1,0:T(8,128)} %get-tuple-element.40.sin) | copy-start | bytes 196612
  66.9 6.1 %copy-start.8 = (f32[128,128]{1,0:T(8,128)S(1)}, f32[128,128]{1,0:T(8,128)}, u32[]{:S(2)}) copy-start(f32[128,128]{1,0:T(8,128)} %get-tuple-element.53.cos) | copy-start | bytes 196612
  66.9 15.7 %collective-permute-start.9 = (bf16[128,256]{1,0:T(8,128)(2,1)}, bf16[128,256]{1,0:T(8,128)(2,1)S(1)}, u32[]{:S(2)}, u32[]{:S(2)}) collective-permute-start(bf16[128,256]{1,0:T(8,128)(2,1)} %get-tuple-element.18.refs_4_), channel_id=1, source_target_pairs={{0,4},{4,8},{8,12},{1,5},{5,9},{9,13},{2,6},{6,10},{10,14},{3,7},{... | collective-permute-start | bytes 196616 | tf_op jit(solution)/shard_map/ppermute | solution.py:380
  71.6 9.1 %copy-start.16 = (bf16[4,128,128]{2,1,0:T(8,128)(2,1)}, bf16[4,128,128]{2,1,0:T(8,128)(2,1)S(1)}, u32[]{:S(2)}) copy-start(bf16[4,128,128]{2,1,0:T(8,128)(2,1)S(1)} %get-tuple-element.15.refs_1_) | copy-start | bytes 393220
  71.6 13.0 %collective-permute-start.10 = (bf16[128,256]{1,0:T(8,128)(2,1)}, bf16[128,256]{1,0:T(8,128)(2,1)S(1)}, u32[]{:S(2)}, u32[]{:S(2)}) collective-permute-start(bf16[128,256]{1,0:T(8,128)(2,1)} %get-tuple-element.19.refs_5_), channel_id=1, source_target_pairs={{0,4},{4,8},{8,12},{1,5},{5,9},{9,13},{2,6},{6,10},{10,14},{3,7},{... | collective-permute-start | bytes 196616 | tf_op jit(solution)/shard_map/ppermute | solution.py:380
  76.3 14.6 %copy-start.18 = (bf16[4,128,128]{2,1,0:T(8,128)(2,1)}, bf16[4,128,128]{2,1,0:T(8,128)(2,1)S(1)}, u32[]{:S(2)}) copy-start(bf16[4,128,128]{2,1,0:T(8,128)(2,1)S(1)} %get-tuple-element.16.refs_2_) | copy-start | bytes 393220
  76.3 14.6 %copy-start.36 = (s32[4,4]{1,0:T(4,128)S(1)}, s32[4,4]{1,0:T(4,128)}, u32[]{:S(2)}) copy-start(s32[4,4]{1,0:T(4,128)} %convert_reduce_fusion.1) | copy-start | bytes 196
  76.3 10.2 %collective-permute-start.11 = (bf16[128,256]{1,0:T(8,128)(2,1)}, bf16[128,256]{1,0:T(8,128)(2,1)S(1)}, u32[]{:S(2)}, u32[]{:S(2)}) collective-permute-start(bf16[128,256]{1,0:T(8,128)(2,1)} %get-tuple-element.20.refs_6_), channel_id=1, source_target_pairs={{0,4},{4,8},{8,12},{1,5},{5,9},{9,13},{2,6},{6,10},{10,14},{3,7},{... | collective-permute-start | bytes 196616 | tf_op jit(solution)/shard_map/ppermute | solution.py:380
  80.7 0.7 copy-start.20
  81.3 8.2 %collective-permute-start.12 = (bf16[128,256]{1,0:T(8,128)(2,1)}, bf16[128,256]{1,0:T(8,128)(2,1)S(1)}, u32[]{:S(2)}, u32[]{:S(2)}) collective-permute-start(bf16[128,256]{1,0:T(8,128)(2,1)} %get-tuple-element.21.refs_7_), channel_id=1, source_target_pairs={{0,4},{4,8},{8,12},{1,5},{5,9},{9,13},{2,6},{6,10},{10,14},{3,7},{... | collective-permute-start | bytes 196616 | tf_op jit(solution)/shard_map/ppermute | solution.py:380
  82.7 0.6 copy-start.22
  83.3 12.2 %collective-permute-start.13 = (bf16[128,256]{1,0:T(8,128)(2,1)}, bf16[128,256]{1,0:T(8,128)(2,1)S(1)}, u32[]{:S(2)}, u32[]{:S(2)}) collective-permute-start(bf16[128,256]{1,0:T(8,128)(2,1)} %get-tuple-element.18.refs_4_), channel_id=1, source_target_pairs={{0,8},{4,12},{1,9},{5,13},{2,10},{6,14},{3,11},{7,15},{16,24},{20,... | collective-permute-start | bytes 196616 | tf_op jit(solution)/shard_map/ppermute | solution.py:380
  84.6 0.6 copy-start.24
  85.2 15.1 %collective-permute-start.14 = (bf16[128,256]{1,0:T(8,128)(2,1)}, bf16[128,256]{1,0:T(8,128)(2,1)S(1)}, u32[]{:S(2)}, u32[]{:S(2)}) collective-permute-start(bf16[128,256]{1,0:T(8,128)(2,1)} %get-tuple-element.19.refs_5_), channel_id=1, source_target_pairs={{0,8},{4,12},{1,9},{5,13},{2,10},{6,14},{3,11},{7,15},{16,24},{20,... | collective-permute-start | bytes 196616 | tf_op jit(solution)/shard_map/ppermute | solution.py:380
  87.1 15.1 %collective-permute-start.15 = (bf16[128,256]{1,0:T(8,128)(2,1)}, bf16[128,256]{1,0:T(8,128)(2,1)S(1)}, u32[]{:S(2)}, u32[]{:S(2)}) collective-permute-start(bf16[128,256]{1,0:T(8,128)(2,1)} %get-tuple-element.20.refs_6_), channel_id=1, source_target_pairs={{0,8},{4,12},{1,9},{5,13},{2,10},{6,14},{3,11},{7,15},{16,24},{20,... | collective-permute-start | bytes 196616 | tf_op jit(solution)/shard_map/ppermute | solution.py:380
  89.6 14.6 %collective-permute-start.16 = (bf16[128,256]{1,0:T(8,128)(2,1)}, bf16[128,256]{1,0:T(8,128)(2,1)S(1)}, u32[]{:S(2)}, u32[]{:S(2)}) collective-permute-start(bf16[128,256]{1,0:T(8,128)(2,1)} %get-tuple-element.21.refs_7_), channel_id=1, source_target_pairs={{0,8},{4,12},{1,9},{5,13},{2,10},{6,14},{3,11},{7,15},{16,24},{20,... | collective-permute-start | bytes 196616 | tf_op jit(solution)/shard_map/ppermute | solution.py:380
  95.4 11.4 %collective-permute-start.17 = (bf16[128,256]{1,0:T(8,128)(2,1)}, bf16[128,256]{1,0:T(8,128)(2,1)S(1)}, u32[]{:S(2)}, u32[]{:S(2)}) collective-permute-start(bf16[128,256]{1,0:T(8,128)(2,1)} %get-tuple-element.18.refs_4_), channel_id=1, source_target_pairs={{0,12},{1,13},{2,14},{3,15},{16,28},{17,29},{18,30},{19,31}} | collective-permute-start | bytes 196616 | tf_op jit(solution)/shard_map/ppermute | solution.py:380
  101.0 8.7 %collective-permute-start.18 = (bf16[128,256]{1,0:T(8,128)(2,1)}, bf16[128,256]{1,0:T(8,128)(2,1)S(1)}, u32[]{:S(2)}, u32[]{:S(2)}) collective-permute-start(bf16[128,256]{1,0:T(8,128)(2,1)} %get-tuple-element.19.refs_5_), channel_id=1, source_target_pairs={{0,12},{1,13},{2,14},{3,15},{16,28},{17,29},{18,30},{19,31}} | collective-permute-start | bytes 196616 | tf_op jit(solution)/shard_map/ppermute | solution.py:380
  102.9 8.8 %collective-permute-start.19 = (bf16[128,256]{1,0:T(8,128)(2,1)}, bf16[128,256]{1,0:T(8,128)(2,1)S(1)}, u32[]{:S(2)}, u32[]{:S(2)}) collective-permute-start(bf16[128,256]{1,0:T(8,128)(2,1)} %get-tuple-element.20.refs_6_), channel_id=1, source_target_pairs={{0,12},{1,13},{2,14},{3,15},{16,28},{17,29},{18,30},{19,31}} | collective-permute-start | bytes 196616 | tf_op jit(solution)/shard_map/ppermute | solution.py:380
  104.2 0.6 copy-start.32
  104.8 8.2 %collective-permute-start.20 = (bf16[128,256]{1,0:T(8,128)(2,1)}, bf16[128,256]{1,0:T(8,128)(2,1)S(1)}, u32[]{:S(2)}, u32[]{:S(2)}) collective-permute-start(bf16[128,256]{1,0:T(8,128)(2,1)} %get-tuple-element.21.refs_7_), channel_id=1, source_target_pairs={{0,12},{1,13},{2,14},{3,15},{16,28},{17,29},{18,30},{19,31}} | collective-permute-start | bytes 196616 | tf_op jit(solution)/shard_map/ppermute | solution.py:380
  113.0 0.9 copy-start.15
  113.9 0.9 copy-start.17
  114.8 0.9 copy-start.19
  115.7 0.9 copy-start.21
  116.6 0.8 copy-start.23
  117.4 0.8 copy-start.25
  118.3 0.8 copy-start.27
  119.1 0.8 copy-start.29
  120.0 0.8 copy-start.31
  120.8 0.8 copy-start.33
  135.9 2.0 %collective-permute-start.21 = (bf16[512,512]{1,0:T(8,128)(2,1)S(1)}, bf16[512,512]{1,0:T(8,128)(2,1)S(1)}, u32[]{:S(2)}, u32[]{:S(2)}) collective-permute-start(bf16[512,512]{1,0:T(8,128)(2,1)S(1)} %attend.1.h0), channel_id=1, source_target_pairs={{0,1},{1,0},{2,3},{3,2},{4,5},{5,4},{6,7},{7,6},{8,9},{9,8},{10,11... | collective-permute-start | bytes 1572872 | tf_op jit(solution)/shard_map/ppermute | solution.py:303
  137.9 2.2 %copy-start.2 = (bf16[512,4096]{1,0:T(8,128)(2,1)S(1)}, bf16[512,4096]{1,0:T(8,128)(2,1)}, u32[]{:S(2)}) copy-start(bf16[512,4096]{1,0:T(8,128)(2,1)} %w0.5) | copy-start | bytes 12582916
  141.4 3.5 %copy-start.37 = (bf16[1024]{0:T(1024)(128)(2,1)S(1)}, bf16[1024]{0:T(1024)(128)(2,1)}, u32[]{:S(2)}) copy-start(bf16[1024]{0:T(1024)(128)(2,1)} %param.22) | copy-start | bytes 6148
  141.4 3.5 %copy-start.38 = (bf16[1024]{0:T(1024)(128)(2,1)S(1)}, bf16[1024]{0:T(1024)(128)(2,1)}, u32[]{:S(2)}) copy-start(bf16[1024]{0:T(1024)(128)(2,1)} %param.23) | copy-start | bytes 6148
  141.4 3.6 %copy-start.3 = (bf16[512,4096]{1,0:T(8,128)(2,1)S(1)}, bf16[512,4096]{1,0:T(8,128)(2,1)}, u32[]{:S(2)}) copy-start(bf16[512,4096]{1,0:T(8,128)(2,1)} %w0.5) | copy-start | bytes 12582916
  141.4 3.5 %copy-start.6 = (bf16[512,1024]{1,0:T(8,128)(2,1)S(1)}, bf16[512,1024]{1,0:T(8,128)(2,1)}, u32[]{:S(2)}) copy-start(bf16[512,1024]{1,0:T(8,128)(2,1)} %own.1) | copy-start | bytes 3145732
  141.4 14.8 %collective-permute-start.24 = (bf16[256,1024]{1,0:T(8,128)(2,1)S(1)}, bf16[256,1024]{1,0:T(8,128)(2,1)S(1)}, u32[]{:S(2)}, u32[]{:S(2)}) collective-permute-start(bf16[256,1024]{1,0:T(8,128)(2,1)S(1)} %project.3), channel_id=1, source_target_pairs={{0,2},{1,3},{2,0},{3,1},{4,6},{5,7},{6,4},{7,5},{8,10},{9,11},{10,... | collective-permute-start | bytes 1572872 | tf_op jit(solution)/shard_map/ppermute | solution.py:303
  143.3 23.4 %collective-permute-start.23 = (bf16[256,1024]{1,0:T(8,128)(2,1)S(1)}, bf16[256,1024]{1,0:T(8,128)(2,1)S(1)}, u32[]{:S(2)}, u32[]{:S(2)}) collective-permute-start(bf16[256,1024]{1,0:T(8,128)(2,1)S(1)} %project.2), channel_id=1, source_target_pairs={{0,2},{1,3},{2,0},{3,1},{4,6},{5,7},{6,4},{7,5},{8,10},{9,11},{10,... | collective-permute-start | bytes 1572872 | tf_op jit(solution)/shard_map/ppermute | solution.py:303
  (3 other events, 1.9 us)

commit v2 on v1

v2 whole, which is shorter than its diff:
```python
import functools
import math

import jax
import jax.numpy as jnp
from jax import lax
from jax.experimental import pallas as pl
from jax.experimental.pallas import tpu as pltpu
from jax.sharding import PartitionSpec as P

MODEL_WIDTH = 4096
HEAD_WIDTH = 128
NORM_EPS = 1e-05
ROPE_BASE = 500000.0

SEG_SPAN = 64
POS_SPAN = 1024
POS_DIGIT = 128
DIGIT_ROWS = 16

QUERY_BLOCK = 128
KEY_BLOCK = 256
MASKED = -1e30

VMEM = pltpu.VMEM
EARLY_MIB = 16
TOKEN = jax.ShapeDtypeStruct((8, 128), jnp.float32)


def params(limit_mib):
    return pltpu.CompilerParams(vmem_limit_bytes=limit_mib * 2**20)


def cost(flops, bytes_accessed):
    return pl.CostEstimate(flops=flops, bytes_accessed=bytes_accessed, transcendentals=0)


def whole():
    return pl.BlockSpec(memory_space=VMEM)


def far_memory():
    return pl.BlockSpec(memory_space=pltpu.HBM)


def prep_kernel(loads, seg, pos, digits, cos, sin):
    lines, lanes = seg.shape
    row = lanes * lax.broadcasted_iota(jnp.int32, seg.shape, 0) + lax.broadcasted_iota(jnp.int32, seg.shape, 1)
    dest = jnp.zeros(seg.shape, jnp.int32)
    total = 0
    for e in range(loads.shape[1]):
        total = total + loads[0, e]
        dest += jnp.where(row >= total, 1, 0)
    low_pos = lax.bitwise_and(pos[...], POS_DIGIT - 1)
    high_pos = lax.shift_right_logical(pos[...], POS_DIGIT.bit_length() - 1)
    digits[...] = jnp.zeros(digits.shape, digits.dtype)
    for j, digit in enumerate((low_pos, high_pos, seg[...], dest)):
        line = jnp.concatenate([digit[i : i + 1, :] for i in range(lines)], 1)
        digits[j : j + 1, :] = line.astype(jnp.float32).astype(digits.dtype)
    at = pos[...].astype(jnp.float32)
    half = HEAD_WIDTH // 2
    lane = lax.broadcasted_iota(jnp.int32, (lanes, HEAD_WIDTH), 1)
    low = lane < half
    power = jnp.where(low, lane, lane - half).astype(jnp.float32)
    inverse = jnp.exp(power * (-2.0 * math.log(ROPE_BASE) / HEAD_WIDTH))
    for i in range(lines):
        column = jnp.broadcast_to(at[i : i + 1, :], (lanes, lanes)).T
        angle = column * inverse
        span = slice(i * lanes, (i + 1) * lanes)
        sine = jnp.sin(angle)
        cos[span, :] = jnp.cos(angle)
        sin[span, :] = jnp.where(low, -sine, sine)


def prep(row_loads, seg, pos):
    lines, lanes = seg.shape
    rows = lines * lanes
    table = jax.ShapeDtypeStruct((rows, HEAD_WIDTH), jnp.float32)
    return pl.pallas_call(
        prep_kernel,
        out_shape=(jax.ShapeDtypeStruct((DIGIT_ROWS, rows), jnp.bfloat16), table, table),
        in_specs=[pl.BlockSpec(memory_space=pltpu.SMEM), whole(), whole()],
        out_specs=(whole(), whole(), whole()),
        compiler_params=params(6),
        cost_estimate=cost(2 * 10**9, 4 * 10**7),
        name="prep",
    )(row_loads, seg, pos)


def gained(piece, gain, number):
    x = piece[...].astype(jnp.float32)
    width = x.shape[1]
    factor = gain[:, pl.ds(pl.multiple_of(number * width, width), width)].astype(jnp.float32)
    return jnp.sum(x * x, -1, keepdims=True), (x * factor).astype(jnp.bfloat16)


def weight_copies(weights, to, sem, ids, width):
    copies = []
    for i, number in enumerate(ids):
        at = 0
        rows = pl.ds(pl.multiple_of(number * width, width), width)
        for weight in weights:
            columns = pl.ds(at, weight.shape[1])
            copies.append(pltpu.make_async_copy(weight.at[rows, :], to.at[i, :, columns], sem.at[len(copies)]))
            at += weight.shape[1]
    return copies


def start(copies):
    for copy in copies:
        copy.start()


def wait(copies):
    for copy in copies:
        copy.wait()


def early_kernel(own, r0, r1, gain, wq, wk, wv, acc, squares, far_weights, token, held, sem):
    del token
    width = r0.shape[1]
    t = own[0]
    near = weight_copies((wq, wk, wv), held, sem.at[0], (t, lax.bitwise_xor(t, 1)), width)
    far = weight_copies(
        (wq, wk, wv), far_weights, sem.at[1], (lax.bitwise_xor(t, 2), lax.bitwise_xor(t, 3)), width
    )
    start(near)
    start(far)
    square0, x0 = gained(r0, gain, t)
    wait(near[:3])
    acc[...] = jnp.dot(x0, held[0], preferred_element_type=jnp.float32)
    square1, x1 = gained(r1, gain, lax.bitwise_xor(t, 1))
    wait(near[3:])
    acc[...] += jnp.dot(x1, held[1], preferred_element_type=jnp.float32)
    squares[...] = square0 + square1
    wait(far)


def early(own, r0, r1, gain, wq, wk, wv):
    rows, width = r0.shape
    columns = wq.shape[1] + wk.shape[1] + wv.shape[1]
    half = (2, width, columns)
    return pl.pallas_call(
        early_kernel,
        out_shape=(
            jax.ShapeDtypeStruct((rows, columns), jnp.float32),
            jax.ShapeDtypeStruct((rows, 1), jnp.float32),
            jax.ShapeDtypeStruct(half, jnp.bfloat16),
            TOKEN,
        ),
        in_specs=[pl.BlockSpec(memory_space=pltpu.SMEM)] + [whole()] * 3 + [far_memory()] * 3,
        out_specs=(whole(), whole(), whole(), far_memory()),
        scratch_shapes=[VMEM(half, jnp.bfloat16), pltpu.SemaphoreType.DMA((2, 6))],
        compiler_params=params(12),
        cost_estimate=cost(4 * rows * width * columns, 8 * width * columns),
        name="early",
    )(own, r0, r1, gain, wq, wk, wv)


def digit_lines(rows):
    return [(i, min(2 * HEAD_WIDTH, rows - i)) for i in range(0, rows, 2 * HEAD_WIDTH)]


def late_kernel(at, own, before, acc, squares, r2, r3, gain, weights, cos, sin, digits, q_out, kv_out, token):
    del before, token
    rows = r2.shape[0]
    span = slice(at, at + rows)
    square2, x2 = gained(r2, gain, lax.bitwise_xor(own[0], 2))
    total = acc[span, :] + jnp.dot(x2, weights[0], preferred_element_type=jnp.float32)
    square3, x3 = gained(r3, gain, lax.bitwise_xor(own[0], 3))
    total += jnp.dot(x3, weights[1], preferred_element_type=jnp.float32)
    total *= lax.rsqrt((squares[span, :] + square2 + square3) / MODEL_WIDTH + NORM_EPS)
    cosine, sine = cos[span, :], sin[span, :]
    n_head = q_out.shape[0]

    def rope(x):
        return (x * cosine + pltpu.roll(x, HEAD_WIDTH // 2, 1) * sine).astype(jnp.bfloat16)

    for h in range(n_head):
        q_out[h] = rope(total[:, h * HEAD_WIDTH : (h + 1) * HEAD_WIDTH])
    kv_out[:rows, :HEAD_WIDTH] = rope(total[:, n_head * HEAD_WIDTH : (n_head + 1) * HEAD_WIDTH])
    kv_out[:rows, HEAD_WIDTH:] = total[:, (n_head + 1) * HEAD_WIDTH :].astype(jnp.bfloat16)
    for i, (line, count) in enumerate(digit_lines(rows)):
        to = rows + i * DIGIT_ROWS
        kv_out[to : to + DIGIT_ROWS, :count] = digits[:, at + line : at + line + count]


def late(at, own, before, acc, squares, r2, r3, gain, weights, cos, sin, digits):
    rows, width = r2.shape
    columns = acc.shape[1]
    heads = columns // HEAD_WIDTH - 2
    return pl.pallas_call(
        functools.partial(late_kernel, at),
        out_shape=(
            jax.ShapeDtypeStruct((heads, rows, HEAD_WIDTH), jnp.bfloat16),
            jax.ShapeDtypeStruct((rows + DIGIT_ROWS * len(digit_lines(rows)), 2 * HEAD_WIDTH), jnp.bfloat16),
            TOKEN,
        ),
        in_specs=[pl.BlockSpec(memory_space=pltpu.SMEM), far_memory()] + [whole()] * 9,
        out_specs=(whole(), whole(), far_memory()),
        compiler_params=params(8),
        cost_estimate=cost(4 * rows * width * columns, 4 * width * columns),
        name="late",
    )(own, before, acc, squares, r2, r3, gain, weights, cos, sin, digits)


def pick_rows(order, x):
    rows = x.shape[0]
    pick = (order == lax.broadcasted_iota(jnp.int32, (rows, rows), 0)).astype(jnp.bfloat16)
    return lax.dot_general(pick, x, (((0,), (0,)), ((), ())), preferred_element_type=jnp.float32)


def attend_kernel(sizes, pieces, first, last, me, *refs):
    refs = list(refs)

    def take(count):
        taken = refs[:count]
        del refs[:count]
        return taken

    q_in = take(len(sizes))
    kv_in = take(len(pieces))
    if not first:
        m_in, l_in, acc_in, own_keys = take(4)
    if last:
        order, out, heads, m_s, l_s, acc_s = take(6)
    else:
        m_out, l_out, acc_out, own_keys_out, m_s, l_s, acc_s = take(7)
    q_all, kv_all, keys, keys_s, sem = refs
    n_head, rows, _ = q_all.shape
    n_query = rows // QUERY_BLOCK
    n_key = kv_all.shape[0] // KEY_BLOCK
    lanes = keys.shape[1]
    row = 0
    for (d, size), source in zip(pieces, kv_in, strict=True):
        for i, (line, count) in enumerate(digit_lines(size)):
            at = size + i * DIGIT_ROWS
            digit = source[at : at + DIGIT_ROWS, :count].astype(jnp.float32).astype(jnp.int32)
            doc = digit[3:4] * SEG_SPAN + digit[2:3]
            key = doc * POS_SPAN + digit[1:2] * POS_DIGIT + digit[0:1]
            key = jnp.where(d <= me[0], key, -1)
            for j in range(0, count, lanes):
                to = (row + line + j) // lanes
                keys[to : to + 1, :] = key[:, j : j + lanes]
        row += size
    own_line = row // lanes
    if first:
        own_line = 0
    else:
        keys[own_line : own_line + n_query, :] = own_keys[...]
    copy = pltpu.make_async_copy(keys, keys_s, sem)
    copy.start()
    if not last:
        own_keys_out[...] = keys[:n_query, :]
    for c, size in enumerate(sizes):
        at = sum(sizes[:c])
        q_all[:, at : at + size, :] = q_in[c][...]
    row = 0
    for (_, size), source in zip(pieces, kv_in, strict=True):
        kv_all[row : row + size, :] = source[:size, :]
        row += size
    copy.wait()
    scale = 1.4426950408889634 / HEAD_WIDTH**0.5
    stacked = n_head * QUERY_BLOCK
    lines = KEY_BLOCK // lanes

    def block(qb, _):
        at = pl.ds(pl.multiple_of(qb * QUERY_BLOCK, QUERY_BLOCK), QUERY_BLOCK)
        flat = pl.ds(pl.multiple_of(qb * stacked, stacked), stacked)
        q = q_all[:, at, :].reshape(stacked, HEAD_WIDTH)
        high = jnp.broadcast_to(keys[pl.ds(own_line + qb, 1), :], (QUERY_BLOCK, lanes)).T
        low = high - lax.bitwise_and(high, POS_SPAN - 1)
        high, low = (jnp.concatenate([x] * lines, 1) for x in (high, low))
        lowest = keys_s[own_line + qb, 0]
        lowest = lowest - lax.bitwise_and(lowest, POS_SPAN - 1)
        highest = lax.bitwise_or(keys_s[own_line + qb, lanes - 1], POS_SPAN - 1)
        if first:
            m_s[...] = jnp.full(m_s.shape, MASKED, jnp.float32)
            l_s[...] = jnp.zeros(l_s.shape, jnp.float32)
            acc_s[...] = jnp.zeros(acc_s.shape, jnp.float32)
        else:
            m_s[...] = m_in[flat, :]
            l_s[...] = l_in[flat, :]
            acc_s[...] = acc_in[flat, :]

        def keys_of(index, _):
            @pl.when((keys_s[index * lines + lines - 1, lanes - 1] >= lowest) & (keys_s[index * lines, 0] <= highest))
            def _():
                span = pl.ds(pl.multiple_of(index * KEY_BLOCK, KEY_BLOCK), KEY_BLOCK)
                k = kv_all[span, :HEAD_WIDTH]
                v = kv_all[span, HEAD_WIDTH:]
                s = lax.dot_general(q, k, (((1,), (1,)), ((), ())), preferred_element_type=jnp.float32)
                ids = jnp.concatenate([keys[pl.ds(index * lines + i, 1), :] for i in range(lines)], 1)
                allowed = (ids <= high) & (ids >= low)
                s = jnp.where(allowed[None], (s * scale).reshape(n_head, QUERY_BLOCK, KEY_BLOCK), MASKED)
                s = s.reshape(stacked, KEY_BLOCK)
                m_old = m_s[...]
                m_new = jnp.maximum(m_old, jnp.max(s, -1, keepdims=True))
                alpha = jnp.exp2(m_old - m_new)
                p = [
                    jnp.exp2(s[:, i : i + HEAD_WIDTH] - m_new) for i in range(0, KEY_BLOCK, HEAD_WIDTH)
                ]
                m_s[...] = m_new
                l_s[...] = l_s[...] * alpha + functools.reduce(jnp.add, p)
                p = jnp.concatenate(p, 1).astype(jnp.bfloat16)
                acc_s[...] = acc_s[...] * alpha + jnp.dot(p, v, preferred_element_type=jnp.float32)

            return 0

        lax.fori_loop(0, n_key, keys_of, 0)
        if last:
            done = (acc_s[...] / jnp.sum(l_s[...], -1, keepdims=True)).astype(jnp.bfloat16)
            for h in range(n_head):
                heads[at, h * HEAD_WIDTH : (h + 1) * HEAD_WIDTH] = done[h * QUERY_BLOCK : (h + 1) * QUERY_BLOCK]
        else:
            m_out[flat, :] = m_s[...]
            l_out[flat, :] = l_s[...]
            acc_out[flat, :] = acc_s[...]
        return 0

    lax.fori_loop(0, n_query, block, 0)
    if last:
        out[...] = pick_rows(order[...], heads[...]).astype(jnp.bfloat16)


def attend(me, q_parts, pieces, kv_parts, state, order):
    first, last = state is None, order is not None
    n_head = q_parts[0].shape[0]
    sizes = tuple(q.shape[1] for q in q_parts)
    rows = sum(sizes)
    n_key = sum(size for _, size in pieces)
    n_query = rows // QUERY_BLOCK
    stacked = n_head * QUERY_BLOCK
    key_lines = (n_key // QUERY_BLOCK + (0 if first else n_query), QUERY_BLOCK)
    running = jax.ShapeDtypeStruct((n_head * rows, HEAD_WIDTH), jnp.float32)
    inputs = [*q_parts, *kv_parts] + ([] if first else list(state)) + ([order] if last else [])
    if last:
        out_shape = jax.ShapeDtypeStruct((rows, n_head * HEAD_WIDTH), jnp.bfloat16)
        out_specs = whole()
    else:
        out_shape = (running,) * 3 + (jax.ShapeDtypeStruct((n_query, QUERY_BLOCK), jnp.int32),)
        out_specs = (whole(),) * 4
    return pl.pallas_call(
        functools.partial(attend_kernel, sizes, tuple(pieces), first, last),
        out_shape=out_shape,
        in_specs=[pl.BlockSpec(memory_space=pltpu.SMEM)] + [whole()] * len(inputs),
        out_specs=out_specs,
        scratch_shapes=([VMEM((rows, n_head * HEAD_WIDTH), jnp.bfloat16)] if last else [])
        + [VMEM((stacked, HEAD_WIDTH), jnp.float32)] * 3
        + [
            VMEM((n_head, rows, HEAD_WIDTH), jnp.bfloat16),
            VMEM((n_key, 2 * HEAD_WIDTH), jnp.bfloat16),
            VMEM(key_lines, jnp.int32),
            pltpu.SMEM(key_lines, jnp.int32),
            pltpu.SemaphoreType.DMA(()),
        ],
        compiler_params=params(12 + n_key // 512),
        cost_estimate=cost(4 * rows * n_key * n_head * HEAD_WIDTH, 4 * rows * n_head * HEAD_WIDTH),
        name="attend",
    )(me, *inputs)


def columns_kernel(own, w_out, token_in, near, far, send_near, send_far, token, sem):
    del token_in, token
    width = near.shape[1]
    copies = []
    for i, (bits, to) in enumerate(((3, send_far), (1, send_near), (2, far), (0, near))):
        at = pl.ds(pl.multiple_of(lax.bitwise_xor(own[0], bits) * width, width), width)
        copies.append(pltpu.make_async_copy(w_out.at[:, at], to, sem.at[i]))
    start(copies)
    wait(copies)


def columns(own, w_out, token, width):
    block = jax.ShapeDtypeStruct((w_out.shape[0], width), w_out.dtype)
    return pl.pallas_call(
        columns_kernel,
        out_shape=(block,) * 4 + (TOKEN,),
        in_specs=[pl.BlockSpec(memory_space=pltpu.SMEM), far_memory(), far_memory()],
        out_specs=(whole(),) * 4 + (far_memory(),),
        scratch_shapes=[pltpu.SemaphoreType.DMA((4,))],
        compiler_params=params(6),
        cost_estimate=cost(1, 4 * w_out.size),
        name="columns",
    )(own, w_out, token)


def project_kernel(h0, h1, w0, w1, out):
    total = jnp.dot(h0[...], w0[...], preferred_element_type=jnp.float32)
    total += jnp.dot(h1[...], w1[...], preferred_element_type=jnp.float32)
    out[...] = total.astype(out.dtype)


def project(h0, h1, w0, w1, part, n_part):
    rows, depth = h0.shape
    width = w0.shape[1]
    step = rows // n_part
    return pl.pallas_call(
        project_kernel,
        grid=(1,),
        in_specs=[
            pl.BlockSpec((step, depth), lambda i: (part, 0)),
            pl.BlockSpec((step, depth), lambda i: (part, 0)),
            pl.BlockSpec((depth, width), lambda i: (0, 0)),
            pl.BlockSpec((depth, width), lambda i: (0, 0)),
        ],
        out_specs=pl.BlockSpec((step, width), lambda i: (0, 0)),
        out_shape=jax.ShapeDtypeStruct((step, width), jnp.bfloat16),
        compiler_params=params(10),
        cost_estimate=cost(4 * step * depth * width, 4 * depth * width),
        name="project",
    )(h0, h1, w0, w1)


def keep_kernel(order, own, h0, h1, w0, w1, out):
    total = jnp.dot(h0[...], w0[...], preferred_element_type=jnp.float32)
    total += jnp.dot(h1[...], w1[...], preferred_element_type=jnp.float32)
    out[...] = total + pick_rows(order[...], own[...])


def keep(order, own, h0, h1, w0, w1):
    rows, width = own.shape
    depth = h0.shape[1]
    return pl.pallas_call(
        keep_kernel,
        out_shape=jax.ShapeDtypeStruct((rows, width), jnp.float32),
        in_specs=[whole()] * 6,
        out_specs=whole(),
        compiler_params=params(12),
        cost_estimate=cost(2 * rows * (2 * depth + rows) * width, 4 * depth * width + 6 * rows * width),
        name="keep",
    )(order, own, h0, h1, w0, w1)


def finish_kernel(kept, received, gain, head, *refs):
    hidden_out, sums = refs[-2:]
    hidden = (kept[...] + received[...].astype(jnp.float32)).astype(jnp.bfloat16)
    hidden_out[...] = hidden
    x = hidden.astype(jnp.float32)
    weighted = x * (gain[...] * head[...])
    squared = x * x
    for i, terms in enumerate((squared, weighted)):
        lanes = functools.reduce(
            jnp.add, [terms[:, j : j + 128] for j in range(0, terms.shape[1], 128)]
        )
        sums[i : i + 1, :] = jnp.sum(lanes.T, 0, keepdims=True)


def finish(kept, received, gain, head, part, n_part, hidden):
    rows, width = kept.shape
    step = rows // n_part
    specs = [
        pl.BlockSpec((step, width), lambda i: (part, 0)),
        pl.BlockSpec((step, width), lambda i: (0, 0)),
        pl.BlockSpec((1, width), lambda i: (0, 0)),
        pl.BlockSpec((1, width), lambda i: (0, 0)),
    ]
    args = [kept, received, gain, head]
    aliases = {}
    if hidden is not None:
        specs.append(pl.BlockSpec(memory_space=pl.ANY))
        args.append(hidden)
        aliases = {4: 0}
    return pl.pallas_call(
        finish_kernel,
        grid=(1,),
        in_specs=specs,
        out_specs=(
            pl.BlockSpec((step, width), lambda i: (part, 0)),
            pl.BlockSpec((2, step), lambda i: (0, 0)),
        ),
        out_shape=(
            jax.ShapeDtypeStruct((rows, width), jnp.bfloat16),
            jax.ShapeDtypeStruct((2, step), jnp.float32),
        ),
        input_output_aliases=aliases,
        compiler_params=params(8),
        cost_estimate=cost(6 * step * width, 8 * step * width),
        name="finish",
    )(*args)


def flip(x, bit):
    count = lax.axis_size("tensor")
    return lax.ppermute(x, "tensor", [(i, i ^ bit) for i in range(count)])


def chunk_sizes(rows, n_dp):
    if n_dp > 8 or rows % 128:
        return (rows,)
    return (rows // 2, rows // 2)


def on_device(
    hidden_in,
    row_loads,
    seg_ids,
    pos_ids,
    prompt_order,
    attn_gain,
    w_query,
    key_matrix,
    value_matrix,
    w_out,
    final_gain,
    value_head,
):
    n_dp = lax.axis_size("dp")
    me = lax.axis_index("dp")
    t = lax.axis_index("tensor")
    rows, width = hidden_in.shape
    sizes = chunk_sizes(rows, n_dp)
    n_part = 2

    own = [hidden_in[sum(sizes[:c]) : sum(sizes[: c + 1])] for c in range(len(sizes))]
    across = [flip(x, 2) for x in own]
    pair = flip(hidden_in, 1)

    lines = rows // QUERY_BLOCK
    digits, cos, sin = prep(
        row_loads, seg_ids.reshape(lines, QUERY_BLOCK), pos_ids.reshape(lines, QUERY_BLOCK)
    )
    gain = attn_gain.reshape(1, -1)
    t_own = t.astype(jnp.int32).reshape(1)
    acc, squares, far_weights, token = early(
        t_own, hidden_in, pair, gain, w_query, key_matrix, value_matrix
    )

    q_parts, kv_parts = [], [[] for _ in range(n_dp)]
    for c in range(len(sizes)):
        if c > 0:
            for d in range(1, n_dp):
                kv_parts[d][-1], token = lax.optimization_barrier((kv_parts[d][-1], token))
        received, token = lax.optimization_barrier((across[c], token))
        diagonal = flip(received, 1)
        q, kv, token = late(
            sum(sizes[:c]), t_own, token, acc, squares, received, diagonal, gain, far_weights, cos, sin, digits
        )
        q_parts.append(q)
        kv_parts[0].append(kv)
        for d in range(1, n_dp):
            kv_parts[d].append(lax.ppermute(kv, "dp", [(i, (i + d) % n_dp) for i in range(n_dp)]))
        if c == 0:
            near, far, send_near, send_far, token = columns(t_own, w_out, token, width)
            near_other, far_other = flip(send_near, 1), flip(send_far, 1)

    order = prompt_order.reshape(1, rows)
    me_own = me.astype(jnp.int32).reshape(1)
    numbers = range(len(sizes))
    soon = [(0, c) for c in numbers] + [(d, c) for d in range(1, n_dp) for c in numbers[:-1]]
    then = [(d, numbers[-1]) for d in range(1, n_dp)]
    if len(sizes) == 1:
        soon, then = soon + then, []
    state = None
    for some in (soon, then):
        if some:
            pieces = [(d, sizes[c]) for d, c in some]
            last = some is then or not then
            state = attend(
                me_own, q_parts, pieces, [kv_parts[d][c] for d, c in some], state, order if last else None
            )
    heads = state
    heads_other = flip(heads, 1)
    sent = [
        flip(project(heads, heads_other, far, far_other, j, n_part), 2) for j in range(n_part)
    ]
    kept = keep(order, hidden_in, heads, heads_other, near, near_other)
    final = final_gain.astype(jnp.float32).reshape(1, width)
    head = value_head.astype(jnp.float32).reshape(1, width)
    hidden, sums = None, []
    for j in range(n_part):
        hidden, part = finish(kept, sent[j], final, head, j, n_part, hidden)
        sums.append(part)
    square, product = lax.psum(jnp.concatenate(sums, 1), "tensor")
    return hidden, product * lax.rsqrt(square / MODEL_WIDTH + NORM_EPS)


def solution(mesh):
    return jax.shard_map(
        on_device,
        mesh=mesh,
        in_specs=(
            P(("parts", "dp"), "tensor"),
            P(("parts", "dp"), None),
            P(("parts", "dp")),
            P(("parts", "dp")),
            P(("parts", "dp"), None),
            P(),
            P(None, "tensor"),
            P(None, "tensor"),
            P(None, "tensor"),
            P("tensor", None),
            P("tensor"),
            P("tensor"),
        ),
        out_specs=(P(("parts", "dp"), "tensor"), P(("parts", "dp"))),
        check_vma=False,
    )
```

time: 176 us -> 101 us (0.57)
  the two profiles are of different devices: /device:TPU:28 before, /device:TPU:9 now
where the time goes in v2:
time: 101 us; the launch traced here: 99.5 us
  waiting for transfers between devices  33.6 us (33%)
  Pallas kernels  27.8 us (28%)
  local copies, waits for them, and re-layouts  16 us (16%)
  starting transfers between devices  14.7 us (15%)
  blocking collectives  5.95 us (6%)
    ppermute x10, waiting for transfers between devices, flip(): return lax.ppermute(x, 'tensor', [(i, i ^ bit) for i in range(count)])  24.9 us
    unnamed x46, local copies, waits for them, and re-layouts  13.2 us
    pallas_call x2, Pallas kernels, attend(): pl.pallas_call(functools.partial(attend_kernel, sizes, tuple(pieces), fir...  12.5 us
    ppermute x6, waiting for transfers between devices, on_device(): lax.ppermute(kv, 'dp', [(i, (i + d) % n_dp) for i in range(n_dp)])  8.65 us
    ppermute x10, starting transfers between devices, flip(): return lax.ppermute(x, 'tensor', [(i, i ^ bit) for i in range(count)])  7.43 us
    ppermute x6, starting transfers between devices, on_device(): lax.ppermute(kv, 'dp', [(i, (i + d) % n_dp) for i in range(n_dp)])  7.31 us
    psum x1, blocking collectives, on_device(): square, product = lax.psum(jnp.concatenate(sums, 1), 'tensor')  5.95 us
    pallas_call x1, Pallas kernels, early(): pl.pallas_call(early_kernel, out_shape=(jax.ShapeDtypeStruct((rows, colum...  3.68 us
  transfers between devices with their start and end apart: 16, of which 7 were waited for; matrix products, arithmetic and copies ran while one was open for 3% of the time, Pallas kernels for 27%

profile of v2, /device:TPU:9, one launch (start us, length us, event | category | flops | bytes accessed | tf_op | source)
XLA Modules:
  0.0 99.5 jit_solution(16464051861579627870)
XLA Ops:
  0.6 0.7 collective-permute-start.1
  1.4 2.1 %fusion.3 = (bf16[256,1024]{1,0:T(8,128)(2,1)}, bf16[256,1024]{1,0:T(8,128)(2,1)S(1)}) fusion(bf16[512,1024]{1,0:T(8,128)(2,1)} %own.1), kind=kLoop, calls=%fused_computation.5 | loop fusion | bytes 2097152 | tf_op jit(solution)/shard_map/slice | solution.py:515
  3.5 1.2 %collective-permute-start = (bf16[256,1024]{1,0:T(8,128)(2,1)S(1)}, bf16[256,1024]{1,0:T(8,128)(2,1)S(1)}, u32[]{:S(2)}, u32[]{:S(2)}) collective-permute-start(bf16[256,1024]{1,0:T(8,128)(2,1)S(1)} %get-tuple-element.73), channel_id=1, source_target_pairs={{0,2},{1,3},{2,0},{3,1},{4,6},{5,7},{6,4},{7,5},{8,10},{9,11},{10,... | collective-permute-start | bytes 1572872 | tf_op jit(solution)/shard_map/ppermute | solution.py:485
  4.7 0.7 reshape.37.gain
  5.4 0.0 collective-permute-done.1.r1
  5.4 0.0 copy-start
  5.4 1.2 %copy-done = bf16[512,1024]{1,0:T(8,128)(2,1)S(1)} copy-done((bf16[512,1024]{1,0:T(8,128)(2,1)S(1)}, bf16[512,1024]{1,0:T(8,128)(2,1)}, u32[]{:S(2)}) %copy-start) | copy-done | bytes 1048600
  6.6 2.2 %copy-done.3 = bf16[4096,512]{1,0:T(8,128)(2,1)S(1)} copy-done((bf16[4096,512]{1,0:T(8,128)(2,1)S(1)}, bf16[4096,512]{1,0:T(8,128)(2,1)}, u32[]{:S(2)}) %copy-start.3) | copy-done | bytes 4194328
  8.8 1.2 %copy-done.4 = bf16[4096,128]{1,0:T(8,128)(2,1)S(1)} copy-done((bf16[4096,128]{1,0:T(8,128)(2,1)S(1)}, bf16[4096,128]{1,0:T(8,128)(2,1)}, u32[]{:S(2)}) %copy-start.4) | copy-done | bytes 1048600
  10.0 1.2 %copy-done.5 = bf16[4096,128]{1,0:T(8,128)(2,1)S(1)} copy-done((bf16[4096,128]{1,0:T(8,128)(2,1)S(1)}, bf16[4096,128]{1,0:T(8,128)(2,1)}, u32[]{:S(2)}) %copy-start.5) | copy-done | bytes 1048600
  11.3 3.7 %early.1 = (f32[512,768]{1,0:T(8,128)S(1)}, f32[512,1]{1,0:T(8,128)S(1)}, bf16[2,1024,768]{2,1,0:T(8,128)(2,1)S(1)}, f32[8,128]{1,0:T(8,128)S(1)}) custom-call(s32[1]{0:T(128)} %bitcast.1.own, bf16[512,1024]{1,0:T(8,128)(2,1)S(1)} %copy-done, bf16[512,1024]{1,0:T(8,128)(2,1)S(1)} %collective-permute-done.1.r1, bf16[1,4096]{1,0:T(2,128)(2,1)S(1)} %reshape.37.gain, ...), custom_call_target="tpu_custom_call" | custom-call | flops 1610612736 | bytes 6291456 | tf_op jit(solution)/shard_map/early/pallas_call | solution.py:143
  14.9 2.0 %collective-permute-done.r2 = bf16[256,1024]{1,0:T(8,128)(2,1)S(1)} collective-permute-done((bf16[256,1024]{1,0:T(8,128)(2,1)S(1)}, bf16[256,1024]{1,0:T(8,128)(2,1)S(1)}, u32[]{:S(2)}, u32[]{:S(2)}) %collective-permute-start) | collective-permute-done | bytes 524320 | tf_op jit(solution)/shard_map/ppermute | solution.py:485
  17.0 0.8 collective-permute-start.2
  17.8 1.2 %collective-permute-start.3 = (bf16[256,1024]{1,0:T(8,128)(2,1)}, bf16[256,1024]{1,0:T(8,128)(2,1)S(1)}, u32[]{:S(2)}, u32[]{:S(2)}) collective-permute-start(bf16[256,1024]{1,0:T(8,128)(2,1)} %get-tuple-element.72), channel_id=1, source_target_pairs={{0,2},{1,3},{2,0},{3,1},{4,6},{5,7},{6,4},{7,5},{8,10},{9,11},{10,... | collective-permute-start | bytes 1572872 | tf_op jit(solution)/shard_map/ppermute | solution.py:485
  19.0 0.0 copy-done.20
  19.0 1.6 %prep.1 = (bf16[16,512]{1,0:T(8,128)(2,1)S(1)}, f32[512,128]{1,0:T(8,128)S(1)}, f32[512,128]{1,0:T(8,128)S(1)}) custom-call(s32[1,4]{1,0:T(1,128)S(1)} %copy-done.20, s32[4,128]{1,0:T(4,128)S(1)} %bitcast.11, s32[4,128]{1,0:T(4,128)S(1)} %bitcast.12), custom_call_target="tpu_custom_call" | custom-call | flops 2000000000 | bytes 40000000 | tf_op jit(solution)/shard_map/prep/pallas_call | solution.py:79
  20.6 0.0 collective-permute-done.2.r3
  20.6 0.0 copy-start.2
  20.6 1.3 %late.2 = (bf16[4,256,128]{2,1,0:T(8,128)(2,1)S(1)}, bf16[272,256]{1,0:T(8,128)(2,1)S(1)}, f32[8,128]{1,0:T(8,128)S(1)}) custom-call(s32[1]{0:T(128)} %bitcast.1.own, f32[8,128]{1,0:T(8,128)S(1)} %get-tuple-element.38.before, f32[512,768]{1,0:T(8,128)S(1)} %get-tuple-element.39.acc, f32[512,1]{1,0:T(8,128)S(1)} %get-tuple-element.40.squares, ...), custom_call_target="tpu_custom_call" | custom-call | flops 805306368 | bytes 3145728 | tf_op jit(solution)/shard_map/late/pallas_call | solution.py:192
  21.9 1.3 %collective-permute-start.6 = (bf16[272,256]{1,0:T(8,128)(2,1)S(1)}, bf16[272,256]{1,0:T(8,128)(2,1)S(1)}, u32[]{:S(2)}, u32[]{:S(2)}) collective-permute-start(bf16[272,256]{1,0:T(8,128)(2,1)S(1)} %get-tuple-element.47.refs_2_), channel_id=1, source_target_pairs={{0,4},{4,8},{8,12},{12,0},{1,5},{5,9},{9,13},{13,1},{2,6},{6,10},{... | collective-permute-start | bytes 417800 | tf_op jit(solution)/shard_map/ppermute | solution.py:542
  23.2 1.1 %collective-permute-start.5 = (bf16[272,256]{1,0:T(8,128)(2,1)S(1)}, bf16[272,256]{1,0:T(8,128)(2,1)S(1)}, u32[]{:S(2)}, u32[]{:S(2)}) collective-permute-start(bf16[272,256]{1,0:T(8,128)(2,1)S(1)} %get-tuple-element.47.refs_2_), channel_id=1, source_target_pairs={{0,8},{4,12},{8,0},{12,4},{1,9},{5,13},{9,1},{13,5},{2,10},{6,14},... | collective-permute-start | bytes 417800 | tf_op jit(solution)/shard_map/ppermute | solution.py:542
  24.3 1.4 %collective-permute-start.4 = (bf16[272,256]{1,0:T(8,128)(2,1)S(1)}, bf16[272,256]{1,0:T(8,128)(2,1)S(1)}, u32[]{:S(2)}, u32[]{:S(2)}) collective-permute-start(bf16[272,256]{1,0:T(8,128)(2,1)S(1)} %get-tuple-element.47.refs_2_), channel_id=1, source_target_pairs={{0,12},{4,0},{8,4},{12,8},{1,13},{5,1},{9,5},{13,9},{2,14},{6,2},{... | collective-permute-start | bytes 417800 | tf_op jit(solution)/shard_map/ppermute | solution.py:542
  25.7 1.6 %columns.1 = (bf16[512,1024]{1,0:T(8,128)(2,1)S(1)}, bf16[512,1024]{1,0:T(8,128)(2,1)S(1)}, bf16[512,1024]{1,0:T(8,128)(2,1)S(1)}, bf16[512,1024]{1,0:T(8,128)(2,1)}, f32[8,128]{1,0:T(8,128)S(1)}) custom-call(s32[1]{0:T(128)} %bitcast.1.own, bf16[512,4096]{1,0:T(8,128)(2,1)S(1)} %copy-done.2, f32[8,128]{1,0:T(8,128)S(1)} %get-tuple-element.48.token_in), custom_call_target="tpu_custom_call" | custom-call | flops 1 | bytes 8388608 | tf_op jit(solution)/shard_map/columns/pallas_call | solution.py:376
  27.3 0.0 collective-permute-done.6.refs_4_
  27.3 0.7 copy-done.12
  28.0 6.9 %collective-permute-done.5.refs_5_ = bf16[272,256]{1,0:T(8,128)(2,1)S(1)} collective-permute-done((bf16[272,256]{1,0:T(8,128)(2,1)S(1)}, bf16[272,256]{1,0:T(8,128)(2,1)S(1)}, u32[]{:S(2)}, u32[]{:S(2)}) %collective-permute-start.5) | collective-permute-done | bytes 139296 | tf_op jit(solution)/shard_map/ppermute | solution.py:542
  35.0 0.7 copy-done.14
  35.6 1.7 %collective-permute-done.4.refs_6_ = bf16[272,256]{1,0:T(8,128)(2,1)S(1)} collective-permute-done((bf16[272,256]{1,0:T(8,128)(2,1)S(1)}, bf16[272,256]{1,0:T(8,128)(2,1)S(1)}, u32[]{:S(2)}, u32[]{:S(2)}) %collective-permute-start.4) | collective-permute-done | bytes 139296 | tf_op jit(solution)/shard_map/ppermute | solution.py:542
  37.3 0.7 copy-done.16
  38.0 0.0 collective-permute-done.3.r2
  38.0 0.5 collective-permute-start.7
  38.5 0.1 collective-permute-start.13
  38.6 1.5 %collective-permute-done.7.r3 = bf16[256,1024]{1,0:T(8,128)(2,1)S(1)} collective-permute-done((bf16[256,1024]{1,0:T(8,128)(2,1)S(1)}, bf16[256,1024]{1,0:T(8,128)(2,1)S(1)}, u32[]{:S(2)}, u32[]{:S(2)}) %collective-permute-start.7) | collective-permute-done | bytes 524320 | tf_op jit(solution)/shard_map/ppermute | solution.py:485
  40.0 1.9 %late.3 = (bf16[4,256,128]{2,1,0:T(8,128)(2,1)S(1)}, bf16[272,256]{1,0:T(8,128)(2,1)}, f32[8,128]{1,0:T(8,128)}) custom-call(s32[1]{0:T(128)} %bitcast.1.own, f32[8,128]{1,0:T(8,128)S(1)} %get-tuple-element.53.before, f32[512,768]{1,0:T(8,128)S(1)} %get-tuple-element.39.acc, f32[512,1]{1,0:T(8,128)S(1)} %get-tuple-element.40.squares, ...), custom_call_target="tpu_custom_call" | custom-call | flops 805306368 | bytes 3145728 | tf_op jit(solution)/shard_map/late/pallas_call | solution.py:192
  42.0 0.7 copy-done.6
  42.7 0.0 collective-permute-start.8
  42.7 2.0 %collective-permute-start.9 = (bf16[272,256]{1,0:T(8,128)(2,1)}, bf16[272,256]{1,0:T(8,128)(2,1)}, u32[]{:S(2)}, u32[]{:S(2)}) collective-permute-start(bf16[272,256]{1,0:T(8,128)(2,1)} %get-tuple-element.56.refs_3_), channel_id=1, source_target_pairs={{0,8},{4,12},{8,0},{12,4},{1,9},{5,13},{9,1},{13,5},{2,10},{6,14},... | collective-permute-start | bytes 417800 | tf_op jit(solution)/shard_map/ppermute | solution.py:542
  44.7 1.5 %collective-permute-start.10 = (bf16[272,256]{1,0:T(8,128)(2,1)}, bf16[272,256]{1,0:T(8,128)(2,1)}, u32[]{:S(2)}, u32[]{:S(2)}) collective-permute-start(bf16[272,256]{1,0:T(8,128)(2,1)} %get-tuple-element.56.refs_3_), channel_id=1, source_target_pairs={{0,12},{4,0},{8,4},{12,8},{1,13},{5,1},{9,5},{13,9},{2,14},{6,2},{... | collective-permute-start | bytes 417800 | tf_op jit(solution)/shard_map/ppermute | solution.py:542
  46.2 1.2 %collective-permute-start.12 = (bf16[512,1024]{1,0:T(8,128)(2,1)}, bf16[512,1024]{1,0:T(8,128)(2,1)S(1)}, u32[]{:S(2)}, u32[]{:S(2)}) collective-permute-start(bf16[512,1024]{1,0:T(8,128)(2,1)} %copy-done.9), channel_id=1, source_target_pairs={{0,1},{1,0},{2,3},{3,2},{4,5},{5,4},{6,7},{7,6},{8,9},{9,8},{10,11... | collective-permute-start | bytes 3145736 | tf_op jit(solution)/shard_map/ppermute | solution.py:485
  47.4 0.9 copy-done.7
  48.3 0.9 copy-done.11
  49.3 0.9 copy-done.13
  50.2 0.9 copy-done.15
  51.1 0.9 copy-done.17
  52.0 7.8 %attend.2 = (f32[2048,128]{1,0:T(8,128)S(1)}, f32[2048,128]{1,0:T(8,128)S(1)}, f32[2048,128]{1,0:T(8,128)S(1)}, s32[4,128]{1,0:T(4,128)S(1)}) custom-call(s32[1]{0:T(128)} %bitcast.me, bf16[4,256,128]{2,1,0:T(8,128)(2,1)S(1)} %get-tuple-element.46.refs_0_, bf16[4,256,128]{2,1,0:T(8,128)(2,1)S(1)} %copy-done.7, bf16[272,256]{1,0:T(8,128)(2,1)S(1)} %copy-done.11, ...), custom_call_target="tpu_custom_call" | custom-call | flops 1342177280 | bytes 1048576 | tf_op jit(solution)/shard_map/attend/pallas_call | solution.py:343
  59.8 0.0 collective-permute-done.8.refs_2_
  59.8 0.0 collective-permute-done.9.refs_3_
  59.8 0.0 collective-permute-done.10.refs_4_
  59.8 4.7 %attend.3.h0 = bf16[512,512]{1,0:T(8,128)(2,1)S(1)} custom-call(s32[1]{0:T(128)} %bitcast.me, bf16[4,256,128]{2,1,0:T(8,128)(2,1)S(1)} %get-tuple-element.46.refs_0_, bf16[4,256,128]{2,1,0:T(8,128)(2,1)S(1)} %copy-done.7, bf16[272,256]{1,0:T(8,128)(2,1)S(1)} %collective-permute-done.8.refs_2_, bf16[272,256]{1,0:T(8,128)(2,1)} %collective-permute-done.9.refs_3_, ...), custom_call_target="tpu_custom_call" | custom-call | flops 805306368 | bytes 1048576 | tf_op jit(solution)/shard_map/attend/pallas_call | solution.py:343
  64.6 0.1 collective-permute-start.11
  64.6 0.0 collective-permute-done.13.w1
  64.7 1.9 %collective-permute-done.11.h1 = bf16[512,512]{1,0:T(8,128)(2,1)S(1)} collective-permute-done((bf16[512,512]{1,0:T(8,128)(2,1)S(1)}, bf16[512,512]{1,0:T(8,128)(2,1)S(1)}, u32[]{:S(2)}, u32[]{:S(2)}) %collective-permute-start.11) | collective-permute-done | bytes 524320 | tf_op jit(solution)/shard_map/ppermute | solution.py:485
  66.5 0.7 project.3
  67.3 0.3 collective-permute-start.15
  67.6 0.7 project.2
  68.3 1.3 %collective-permute-start.14 = (bf16[256,1024]{1,0:T(8,128)(2,1)S(1)}, bf16[256,1024]{1,0:T(8,128)(2,1)S(1)}, u32[]{:S(2)}, u32[]{:S(2)}) collective-permute-start(bf16[256,1024]{1,0:T(8,128)(2,1)S(1)} %project.2), channel_id=1, source_target_pairs={{0,2},{1,3},{2,0},{3,1},{4,6},{5,7},{6,4},{7,5},{8,10},{9,11},{10,... | collective-permute-start | bytes 1572872 | tf_op jit(solution)/shard_map/ppermute | solution.py:485
  69.6 0.0 collective-permute-done.12.w1
  69.7 1.8 %keep.1.kept = f32[512,1024]{1,0:T(8,128)S(1)} custom-call(s32[1,512]{1,0:T(1,128)S(1)} %copy-done.8, bf16[512,1024]{1,0:T(8,128)(2,1)S(1)} %copy-done.1, bf16[512,512]{1,0:T(8,128)(2,1)S(1)} %attend.3.h0, bf16[512,512]{1,0:T(8,128)(2,1)S(1)} %collective-permute-done.11.h1, bf16[512,1024]{1,0:T(8,128)(2,1)S(1)} %get-tuple-element.64.w0, ...), custom_call_target="tpu_custom_call" | custom-call | flops 1610612736 | bytes 5242880 | tf_op jit(solution)/shard_map/keep/pallas_call | solution.py:424
  71.5 9.3 %collective-permute-done.15.received = bf16[256,1024]{1,0:T(8,128)(2,1)S(1)} collective-permute-done((bf16[256,1024]{1,0:T(8,128)(2,1)S(1)}, bf16[256,1024]{1,0:T(8,128)(2,1)S(1)}, u32[]{:S(2)}, u32[]{:S(2)}) %collective-permute-start.15) | collective-permute-done | bytes 524320 | tf_op jit(solution)/shard_map/ppermute | solution.py:485
  80.7 1.0 finish.2
  81.7 10.2 %collective-permute-done.14.received = bf16[256,1024]{1,0:T(8,128)(2,1)S(1)} collective-permute-done((bf16[256,1024]{1,0:T(8,128)(2,1)S(1)}, bf16[256,1024]{1,0:T(8,128)(2,1)S(1)}, u32[]{:S(2)}, u32[]{:S(2)}) %collective-permute-start.14) | collective-permute-done | bytes 524320 | tf_op jit(solution)/shard_map/ppermute | solution.py:485
  92.0 1.0 finish.3
  92.9 6.0 %psum.7 = f32[2,512]{1,0:T(2,128)S(1)} all-reduce(f32[2,512]{1,0:T(2,128)S(1)} %pad_maximum_fusion), channel_id=1, replica_groups=mesh['parts'=2,'dp'=4,'tensor'=4] {'tensor'}, use_global_device_ids=true, to_apply=%region_0.0 | all-reduce | flops 1024 | bytes 8192 | tf_op jit(solution)/shard_map/psum | solution.py:574
  98.9 0.6 fusion.2
  (33 shorter events, 0.1 us)
Async XLA Ops:
  0.6 4.7 %collective-permute-start.1 = (bf16[512,1024]{1,0:T(8,128)(2,1)}, bf16[512,1024]{1,0:T(8,128)(2,1)S(1)}, u32[]{:S(2)}, u32[]{:S(2)}) collective-permute-start(bf16[512,1024]{1,0:T(8,128)(2,1)} %own.1), channel_id=1, source_target_pairs={{0,1},{1,0},{2,3},{3,2},{4,5},{5,4},{6,7},{7,6},{8,9},{9,8},{10,11... | collective-permute-start | bytes 3145736 | tf_op jit(solution)/shard_map/ppermute | solution.py:485
  3.5 13.5 %collective-permute-start = (bf16[256,1024]{1,0:T(8,128)(2,1)S(1)}, bf16[256,1024]{1,0:T(8,128)(2,1)S(1)}, u32[]{:S(2)}, u32[]{:S(2)}) collective-permute-start(bf16[256,1024]{1,0:T(8,128)(2,1)S(1)} %get-tuple-element.73), channel_id=1, source_target_pairs={{0,2},{1,3},{2,0},{3,1},{4,6},{5,7},{6,4},{7,5},{8,10},{9,11},{10,... | collective-permute-start | bytes 1572872 | tf_op jit(solution)/shard_map/ppermute | solution.py:485
  5.4 1.2 %copy-start = (bf16[512,1024]{1,0:T(8,128)(2,1)S(1)}, bf16[512,1024]{1,0:T(8,128)(2,1)}, u32[]{:S(2)}) copy-start(bf16[512,1024]{1,0:T(8,128)(2,1)} %own.1) | copy-start | bytes 3145732
  6.6 2.2 %copy-start.3 = (bf16[4096,512]{1,0:T(8,128)(2,1)S(1)}, bf16[4096,512]{1,0:T(8,128)(2,1)}, u32[]{:S(2)}) copy-start(bf16[4096,512]{1,0:T(8,128)(2,1)} %wq.1) | copy-start | bytes 12582916
  8.8 1.2 %copy-start.4 = (bf16[4096,128]{1,0:T(8,128)(2,1)S(1)}, bf16[4096,128]{1,0:T(8,128)(2,1)}, u32[]{:S(2)}) copy-start(bf16[4096,128]{1,0:T(8,128)(2,1)} %wk.1) | copy-start | bytes 3145732
  10.0 1.2 %copy-start.5 = (bf16[4096,128]{1,0:T(8,128)(2,1)S(1)}, bf16[4096,128]{1,0:T(8,128)(2,1)}, u32[]{:S(2)}) copy-start(bf16[4096,128]{1,0:T(8,128)(2,1)} %wv.1) | copy-start | bytes 3145732
  11.3 7.8 %copy-start.18 = (s32[512]{0:T(512)S(1)}, s32[512]{0:T(512)}, u32[]{:S(2)}) copy-start(s32[512]{0:T(512)} %param.14) | copy-start | bytes 6148
  11.3 7.8 %copy-start.19 = (s32[512]{0:T(512)S(1)}, s32[512]{0:T(512)}, u32[]{:S(2)}) copy-start(s32[512]{0:T(512)} %param.15) | copy-start | bytes 6148
  11.3 7.8 %copy-start.20 = (s32[1,4]{1,0:T(1,128)S(1)}, s32[1,4]{1,0:T(1,128)}, u32[]{:S(2)}) copy-start(s32[1,4]{1,0:T(1,128)} %loads.1) | copy-start | bytes 52
  17.0 3.6 %collective-permute-start.2 = (bf16[256,1024]{1,0:T(8,128)(2,1)S(1)}, bf16[256,1024]{1,0:T(8,128)(2,1)S(1)}, u32[]{:S(2)}, u32[]{:S(2)}) collective-permute-start(bf16[256,1024]{1,0:T(8,128)(2,1)S(1)} %collective-permute-done.r2), channel_id=1, source_target_pairs={{0,1},{1,0},{2,3},{3,2},{4,5},{5,4},{6,7},{7,6},{8,9},{9,8},{10,11... | collective-permute-start | bytes 1572872 | tf_op jit(solution)/shard_map/ppermute | solution.py:485
  17.8 20.2 %collective-permute-start.3 = (bf16[256,1024]{1,0:T(8,128)(2,1)}, bf16[256,1024]{1,0:T(8,128)(2,1)S(1)}, u32[]{:S(2)}, u32[]{:S(2)}) collective-permute-start(bf16[256,1024]{1,0:T(8,128)(2,1)} %get-tuple-element.72), channel_id=1, source_target_pairs={{0,2},{1,3},{2,0},{3,1},{4,6},{5,7},{6,4},{7,5},{8,10},{9,11},{10,... | collective-permute-start | bytes 1572872 | tf_op jit(solution)/shard_map/ppermute | solution.py:485
  20.6 5.1 %copy-start.2 = (bf16[512,4096]{1,0:T(8,128)(2,1)S(1)}, bf16[512,4096]{1,0:T(8,128)(2,1)}, u32[]{:S(2)}) copy-start(bf16[512,4096]{1,0:T(8,128)(2,1)} %w_out.1) | copy-start | bytes 12582916
  21.9 16.6 %copy-start.10 = (bf16[272,256]{1,0:T(8,128)(2,1)}, bf16[272,256]{1,0:T(8,128)(2,1)S(1)}, u32[]{:S(2)}) copy-start(bf16[272,256]{1,0:T(8,128)(2,1)S(1)} %get-tuple-element.47.refs_2_) | copy-start | bytes 417796
  21.9 5.4 %collective-permute-start.6 = (bf16[272,256]{1,0:T(8,128)(2,1)S(1)}, bf16[272,256]{1,0:T(8,128)(2,1)S(1)}, u32[]{:S(2)}, u32[]{:S(2)}) collective-permute-start(bf16[272,256]{1,0:T(8,128)(2,1)S(1)} %get-tuple-element.47.refs_2_), channel_id=1, source_target_pairs={{0,4},{4,8},{8,12},{12,0},{1,5},{5,9},{9,13},{13,1},{2,6},{6,10},{... | collective-permute-start | bytes 417800 | tf_op jit(solution)/shard_map/ppermute | solution.py:542
  23.2 11.7 %collective-permute-start.5 = (bf16[272,256]{1,0:T(8,128)(2,1)S(1)}, bf16[272,256]{1,0:T(8,128)(2,1)S(1)}, u32[]{:S(2)}, u32[]{:S(2)}) collective-permute-start(bf16[272,256]{1,0:T(8,128)(2,1)S(1)} %get-tuple-element.47.refs_2_), channel_id=1, source_target_pairs={{0,8},{4,12},{8,0},{12,4},{1,9},{5,13},{9,1},{13,5},{2,10},{6,14},... | collective-permute-start | bytes 417800 | tf_op jit(solution)/shard_map/ppermute | solution.py:542
  24.3 13.0 %collective-permute-start.4 = (bf16[272,256]{1,0:T(8,128)(2,1)S(1)}, bf16[272,256]{1,0:T(8,128)(2,1)S(1)}, u32[]{:S(2)}, u32[]{:S(2)}) collective-permute-start(bf16[272,256]{1,0:T(8,128)(2,1)S(1)} %get-tuple-element.47.refs_2_), channel_id=1, source_target_pairs={{0,12},{4,0},{8,4},{12,8},{1,13},{5,1},{9,5},{13,9},{2,14},{6,2},{... | collective-permute-start | bytes 417800 | tf_op jit(solution)/shard_map/ppermute | solution.py:542
  27.3 10.0 %copy-start.9 = (bf16[512,1024]{1,0:T(8,128)(2,1)}, bf16[512,1024]{1,0:T(8,128)(2,1)S(1)}, u32[]{:S(2)}) copy-start(bf16[512,1024]{1,0:T(8,128)(2,1)S(1)} %get-tuple-element.65) | copy-start | bytes 3145732
  27.3 0.7 copy-start.12
  35.0 0.7 copy-start.14
  37.3 0.7 copy-start.16
  38.0 2.0 %collective-permute-start.7 = (bf16[256,1024]{1,0:T(8,128)(2,1)S(1)}, bf16[256,1024]{1,0:T(8,128)(2,1)S(1)}, u32[]{:S(2)}, u32[]{:S(2)}) collective-permute-start(bf16[256,1024]{1,0:T(8,128)(2,1)S(1)} %collective-permute-done.3.r2), channel_id=1, source_target_pairs={{0,1},{1,0},{2,3},{3,2},{4,5},{5,4},{6,7},{7,6},{8,9},{9,8},{10,11... | collective-permute-start | bytes 1572872 | tf_op jit(solution)/shard_map/ppermute | solution.py:485
  38.5 26.2 %collective-permute-start.13 = (bf16[512,1024]{1,0:T(8,128)(2,1)}, bf16[512,1024]{1,0:T(8,128)(2,1)S(1)}, u32[]{:S(2)}, u32[]{:S(2)}) collective-permute-start(bf16[512,1024]{1,0:T(8,128)(2,1)} %get-tuple-element.67), channel_id=1, source_target_pairs={{0,1},{1,0},{2,3},{3,2},{4,5},{5,4},{6,7},{7,6},{8,9},{9,8},{10,11... | collective-permute-start | bytes 3145736 | tf_op jit(solution)/shard_map/ppermute | solution.py:485
  42.0 0.7 copy-start.6
  42.7 17.1 %copy-start.8 = (s32[1,512]{1,0:T(1,128)S(1)}, s32[1,512]{1,0:T(1,128)}, u32[]{:S(2)}) copy-start(s32[1,512]{1,0:T(1,128)} %order.1) | copy-start | bytes 6148
  42.7 17.1 %collective-permute-start.8 = (bf16[272,256]{1,0:T(8,128)(2,1)}, bf16[272,256]{1,0:T(8,128)(2,1)S(1)}, u32[]{:S(2)}, u32[]{:S(2)}) collective-permute-start(bf16[272,256]{1,0:T(8,128)(2,1)} %get-tuple-element.56.refs_3_), channel_id=1, source_target_pairs={{0,4},{4,8},{8,12},{12,0},{1,5},{5,9},{9,13},{13,1},{2,6},{6,10},{... | collective-permute-start | bytes 417800 | tf_op jit(solution)/shard_map/ppermute | solution.py:542
  42.7 17.1 %collective-permute-start.9 = (bf16[272,256]{1,0:T(8,128)(2,1)}, bf16[272,256]{1,0:T(8,128)(2,1)}, u32[]{:S(2)}, u32[]{:S(2)}) collective-permute-start(bf16[272,256]{1,0:T(8,128)(2,1)} %get-tuple-element.56.refs_3_), channel_id=1, source_target_pairs={{0,8},{4,12},{8,0},{12,4},{1,9},{5,13},{9,1},{13,5},{2,10},{6,14},... | collective-permute-start | bytes 417800 | tf_op jit(solution)/shard_map/ppermute | solution.py:542
  44.7 15.1 %collective-permute-start.10 = (bf16[272,256]{1,0:T(8,128)(2,1)}, bf16[272,256]{1,0:T(8,128)(2,1)}, u32[]{:S(2)}, u32[]{:S(2)}) collective-permute-start(bf16[272,256]{1,0:T(8,128)(2,1)} %get-tuple-element.56.refs_3_), channel_id=1, source_target_pairs={{0,12},{4,0},{8,4},{12,8},{1,13},{5,1},{9,5},{13,9},{2,14},{6,2},{... | collective-permute-start | bytes 417800 | tf_op jit(solution)/shard_map/ppermute | solution.py:542
  46.2 23.5 %collective-permute-start.12 = (bf16[512,1024]{1,0:T(8,128)(2,1)}, bf16[512,1024]{1,0:T(8,128)(2,1)S(1)}, u32[]{:S(2)}, u32[]{:S(2)}) collective-permute-start(bf16[512,1024]{1,0:T(8,128)(2,1)} %copy-done.9), channel_id=1, source_target_pairs={{0,1},{1,0},{2,3},{3,2},{4,5},{5,4},{6,7},{7,6},{8,9},{9,8},{10,11... | collective-permute-start | bytes 3145736 | tf_op jit(solution)/shard_map/ppermute | solution.py:485
  47.4 0.9 copy-start.7
  48.3 0.9 copy-start.11
  49.3 0.9 copy-start.13
  50.2 0.9 copy-start.15
  51.1 0.9 copy-start.17
  64.6 2.0 %collective-permute-start.11 = (bf16[512,512]{1,0:T(8,128)(2,1)S(1)}, bf16[512,512]{1,0:T(8,128)(2,1)S(1)}, u32[]{:S(2)}, u32[]{:S(2)}) collective-permute-start(bf16[512,512]{1,0:T(8,128)(2,1)S(1)} %attend.3.h0), channel_id=1, source_target_pairs={{0,1},{1,0},{2,3},{3,2},{4,5},{5,4},{6,7},{7,6},{8,9},{9,8},{10,11... | collective-permute-start | bytes 1572872 | tf_op jit(solution)/shard_map/ppermute | solution.py:485
  66.5 3.1 %copy-start.21 = (bf16[1024]{0:T(1024)(128)(2,1)S(1)}, bf16[1024]{0:T(1024)(128)(2,1)}, u32[]{:S(2)}) copy-start(bf16[1024]{0:T(1024)(128)(2,1)} %param.22) | copy-start | bytes 6148
  66.5 3.1 %copy-start.22 = (bf16[1024]{0:T(1024)(128)(2,1)S(1)}, bf16[1024]{0:T(1024)(128)(2,1)}, u32[]{:S(2)}) copy-start(bf16[1024]{0:T(1024)(128)(2,1)} %param.23) | copy-start | bytes 6148
  66.5 3.1 %copy-start.1 = (bf16[512,1024]{1,0:T(8,128)(2,1)S(1)}, bf16[512,1024]{1,0:T(8,128)(2,1)}, u32[]{:S(2)}) copy-start(bf16[512,1024]{1,0:T(8,128)(2,1)} %own.1) | copy-start | bytes 3145732
  67.3 13.4 %collective-permute-start.15 = (bf16[256,1024]{1,0:T(8,128)(2,1)S(1)}, bf16[256,1024]{1,0:T(8,128)(2,1)S(1)}, u32[]{:S(2)}, u32[]{:S(2)}) collective-permute-start(bf16[256,1024]{1,0:T(8,128)(2,1)S(1)} %project.3), channel_id=1, source_target_pairs={{0,2},{1,3},{2,0},{3,1},{4,6},{5,7},{6,4},{7,5},{8,10},{9,11},{10,... | collective-permute-start | bytes 1572872 | tf_op jit(solution)/shard_map/ppermute | solution.py:485
  68.3 23.6 %collective-permute-start.14 = (bf16[256,1024]{1,0:T(8,128)(2,1)S(1)}, bf16[256,1024]{1,0:T(8,128)(2,1)S(1)}, u32[]{:S(2)}, u32[]{:S(2)}) collective-permute-start(bf16[256,1024]{1,0:T(8,128)(2,1)S(1)} %project.2), channel_id=1, source_target_pairs={{0,2},{1,3},{2,0},{3,1},{4,6},{5,7},{6,4},{7,5},{8,10},{9,11},{10,... | collective-permute-start | bytes 1572872 | tf_op jit(solution)/shard_map/ppermute | solution.py:485

commit v3 on v2

--- a/solution.py
+++ b/solution.py
@@ -17,6 +17,7 @@
 POS_SPAN = 1024
 POS_DIGIT = 128
 DIGIT_ROWS = 16
+N_PART = 2
 
 QUERY_BLOCK = 128
 KEY_BLOCK = 256
@@ -161,9 +162,34 @@
     return [(i, min(2 * HEAD_WIDTH, rows - i)) for i in range(0, rows, 2 * HEAD_WIDTH)]
 
 
-def late_kernel(at, own, before, acc, squares, r2, r3, gain, weights, cos, sin, digits, q_out, kv_out, token):
-    del before, token
+def keys_of(digits, back, own):
+    digit = digits.astype(jnp.float32).astype(jnp.int32)
+    doc = digit[3:4] * SEG_SPAN + digit[2:3]
+    key = doc * POS_SPAN + digit[1:2] * POS_DIGIT + digit[0:1]
+    return jnp.where(back <= own[2], key, -1)
+
+
+def unpack(pieces, sources, own, kv_all, keys):
+    lanes = keys.shape[1]
+    row = 0
+    for (back, size), source in zip(pieces, sources, strict=True):
+        kv_all[row : row + size, :] = source[:size, :]
+        for i, (line, count) in enumerate(digit_lines(size)):
+            at = size + i * DIGIT_ROWS
+            key = keys_of(source[at : at + DIGIT_ROWS, :count], back, own)
+            for j in range(0, count, lanes):
+                to = (row + line + j) // lanes
+                keys[to : to + 1, :] = key[:, j : j + lanes]
+        row += size
+
+
+def late_kernel(at, pieces, own, before, acc, squares, r2, r3, gain, weights, cos, sin, digits, *refs):
+    del before
+    refs = list(refs)
     rows = r2.shape[0]
+    n_old = sum(1 for back, _ in pieces if back == 0)
+    q_old, kv_old = refs[:n_old], refs[n_old : n_old + len(pieces)]
+    q_out, kv_out, *outs = refs[n_old + len(pieces) :]
     span = slice(at, at + rows)
     square2, x2 = gained(r2, gain, lax.bitwise_xor(own[0], 2))
     total = acc[span, :] + jnp.dot(x2, weights[0], preferred_element_type=jnp.float32)
@@ -176,32 +202,51 @@
     def rope(x):
         return (x * cosine + pltpu.roll(x, HEAD_WIDTH // 2, 1) * sine).astype(jnp.bfloat16)
 
+    here = slice(at, at + rows) if q_out.shape[1] > rows else slice(0, rows)
     for h in range(n_head):
-        q_out[h] = rope(total[:, h * HEAD_WIDTH : (h + 1) * HEAD_WIDTH])
+        q_out[h, here, :] = rope(total[:, h * HEAD_WIDTH : (h + 1) * HEAD_WIDTH])
     kv_out[:rows, :HEAD_WIDTH] = rope(total[:, n_head * HEAD_WIDTH : (n_head + 1) * HEAD_WIDTH])
     kv_out[:rows, HEAD_WIDTH:] = total[:, (n_head + 1) * HEAD_WIDTH :].astype(jnp.bfloat16)
     for i, (line, count) in enumerate(digit_lines(rows)):
         to = rows + i * DIGIT_ROWS
         kv_out[to : to + DIGIT_ROWS, :count] = digits[:, at + line : at + line + count]
-
-
-def late(at, own, before, acc, squares, r2, r3, gain, weights, cos, sin, digits):
+    if len(outs) > 1:
+        kv_all, keys, _ = outs
+        row = 0
+        for q in q_old:
+            q_out[:, row : row + q.shape[1], :] = q[...]
+            row += q.shape[1]
+        sources = [*kv_old[:n_old], kv_out, *kv_old[n_old:]]
+        unpack([*pieces[:n_old], (0, rows), *pieces[n_old:]], sources, own, kv_all, keys)
+
+
+def late(at, own, before, acc, squares, r2, r3, gain, weights, cos, sin, digits, last, q_old, pieces, kv_old):
     rows, width = r2.shape
     columns = acc.shape[1]
     heads = columns // HEAD_WIDTH - 2
-    return pl.pallas_call(
-        functools.partial(late_kernel, at),
+    n_key = rows + sum(size for _, size in pieces)
+    more, specs = (), ()
+    if last:
+        more = (
+            jax.ShapeDtypeStruct((n_key, 2 * HEAD_WIDTH), jnp.bfloat16),
+            jax.ShapeDtypeStruct((n_key // QUERY_BLOCK, QUERY_BLOCK), jnp.int32),
+        )
+        specs = (whole(), whole())
+    return pl.pallas_call(
+        functools.partial(late_kernel, at, tuple(pieces)),
         out_shape=(
-            jax.ShapeDtypeStruct((heads, rows, HEAD_WIDTH), jnp.bfloat16),
+            jax.ShapeDtypeStruct((heads, at + rows if last else rows, HEAD_WIDTH), jnp.bfloat16),
             jax.ShapeDtypeStruct((rows + DIGIT_ROWS * len(digit_lines(rows)), 2 * HEAD_WIDTH), jnp.bfloat16),
+            *more,
             TOKEN,
         ),
-        in_specs=[pl.BlockSpec(memory_space=pltpu.SMEM), far_memory()] + [whole()] * 9,
-        out_specs=(whole(), whole(), far_memory()),
-        compiler_params=params(8),
+        in_specs=[pl.BlockSpec(memory_space=pltpu.SMEM), far_memory()]
+        + [whole()] * (9 + len(q_old) + len(kv_old)),
+        out_specs=(whole(), whole(), *specs, far_memory()),
+        compiler_params=params(10),
         cost_estimate=cost(4 * rows * width * columns, 4 * width * columns),
         name="late",
-    )(own, before, acc, squares, r2, r3, gain, weights, cos, sin, digits)
+    )(own, before, acc, squares, r2, r3, gain, weights, cos, sin, digits, *q_old, *kv_old)
 
 
 def pick_rows(order, x):
@@ -210,7 +255,7 @@
     return lax.dot_general(pick, x, (((0,), (0,)), ((), ())), preferred_element_type=jnp.float32)
 
 
-def attend_kernel(sizes, pieces, first, last, me, *refs):
+def attend_kernel(pieces, last, own, q_all, *refs):
     refs = list(refs)
 
     def take(count):
@@ -218,47 +263,24 @@
         del refs[:count]
         return taken
 
-    q_in = take(len(sizes))
-    kv_in = take(len(pieces))
-    if not first:
-        m_in, l_in, acc_in, own_keys = take(4)
-    if last:
-        order, out, heads, m_s, l_s, acc_s = take(6)
-    else:
-        m_out, l_out, acc_out, own_keys_out, m_s, l_s, acc_s = take(7)
-    q_all, kv_all, keys, keys_s, sem = refs
     n_head, rows, _ = q_all.shape
     n_query = rows // QUERY_BLOCK
+    if last:
+        m_in, l_in, acc_in, own_keys = take(4)
+        kv_in = take(len(pieces))
+        _, order, out, *parts = take(3 + N_PART)
+        heads, kv_all, keys = take(3)
+        unpack(pieces, kv_in, own, kv_all, keys)
+        own_line = kv_all.shape[0] // QUERY_BLOCK
+        keys[own_line : own_line + n_query, :] = own_keys[:n_query, :]
+    else:
+        kv_all, keys, m_out, l_out, acc_out, _ = take(6)
+        own_line = 0
+    m_s, l_s, acc_s, keys_s, sem = refs
     n_key = kv_all.shape[0] // KEY_BLOCK
     lanes = keys.shape[1]
-    row = 0
-    for (d, size), source in zip(pieces, kv_in, strict=True):
-        for i, (line, count) in enumerate(digit_lines(size)):
-            at = size + i * DIGIT_ROWS
-            digit = source[at : at + DIGIT_ROWS, :count].astype(jnp.float32).astype(jnp.int32)
-            doc = digit[3:4] * SEG_SPAN + digit[2:3]
-            key = doc * POS_SPAN + digit[1:2] * POS_DIGIT + digit[0:1]
-            key = jnp.where(d <= me[0], key, -1)
-            for j in range(0, count, lanes):
-                to = (row + line + j) // lanes
-                keys[to : to + 1, :] = key[:, j : j + lanes]
-        row += size
-    own_line = row // lanes
-    if first:
-        own_line = 0
-    else:
-        keys[own_line : own_line + n_query, :] = own_keys[...]
     copy = pltpu.make_async_copy(keys, keys_s, sem)
     copy.start()
-    if not last:
-        own_keys_out[...] = keys[:n_query, :]
-    for c, size in enumerate(sizes):
-        at = sum(sizes[:c])
-        q_all[:, at : at + size, :] = q_in[c][...]
-    row = 0
-    for (_, size), source in zip(pieces, kv_in, strict=True):
-        kv_all[row : row + size, :] = source[:size, :]
-        row += size
     copy.wait()
     scale = 1.4426950408889634 / HEAD_WIDTH**0.5
     stacked = n_head * QUERY_BLOCK
@@ -274,7 +296,7 @@
         lowest = keys_s[own_line + qb, 0]
         lowest = lowest - lax.bitwise_and(lowest, POS_SPAN - 1)
         highest = lax.bitwise_or(keys_s[own_line + qb, lanes - 1], POS_SPAN - 1)
-        if first:
+        if not last:
             m_s[...] = jnp.full(m_s.shape, MASKED, jnp.float32)
             l_s[...] = jnp.zeros(l_s.shape, jnp.float32)
             acc_s[...] = jnp.zeros(acc_s.shape, jnp.float32)
@@ -283,7 +305,7 @@
             l_s[...] = l_in[flat, :]
             acc_s[...] = acc_in[flat, :]
 
-        def keys_of(index, _):
+        def some_keys(index, _):
             @pl.when((keys_s[index * lines + lines - 1, lanes - 1] >= lowest) & (keys_s[index * lines, 0] <= highest))
             def _():
                 span = pl.ds(pl.multiple_of(index * KEY_BLOCK, KEY_BLOCK), KEY_BLOCK)
@@ -307,7 +329,7 @@
 
             return 0
 
-        lax.fori_loop(0, n_key, keys_of, 0)
+        lax.fori_loop(0, n_key, some_keys, 0)
         if last:
             done = (acc_s[...] / jnp.sum(l_s[...], -1, keepdims=True)).astype(jnp.bfloat16)
             for h in range(n_head):
@@ -320,99 +342,93 @@
 
     lax.fori_loop(0, n_query, block, 0)
     if last:
-        out[...] = pick_rows(order[...], heads[...]).astype(jnp.bfloat16)
-
-
-def attend(me, q_parts, pieces, kv_parts, state, order):
-    first, last = state is None, order is not None
-    n_head = q_parts[0].shape[0]
-    sizes = tuple(q.shape[1] for q in q_parts)
-    rows = sum(sizes)
+        picked = pick_rows(order[...], heads[...]).astype(jnp.bfloat16)
+        out[...] = picked
+        for i, part in enumerate(parts):
+            part[...] = picked[i * part.shape[0] : (i + 1) * part.shape[0], :]
+
+
+def attend(own, q_all, kv_all, keys):
+    n_head, rows, _ = q_all.shape
+    stacked = n_head * QUERY_BLOCK
+    n_key = kv_all.shape[0]
+    running = jax.ShapeDtypeStruct((n_head * rows, HEAD_WIDTH), jnp.float32)
+    return pl.pallas_call(
+        functools.partial(attend_kernel, (), False),
+        out_shape=(running,) * 3 + (TOKEN,),
+        in_specs=[pl.BlockSpec(memory_space=pltpu.SMEM)] + [whole()] * 3,
+        out_specs=(whole(),) * 3 + (far_memory(),),
+        scratch_shapes=[VMEM((stacked, HEAD_WIDTH), jnp.float32)] * 3
+        + [pltpu.SMEM(keys.shape, jnp.int32), pltpu.SemaphoreType.DMA(())],
+        compiler_params=params(12),
+        cost_estimate=cost(4 * rows * n_key * n_head * HEAD_WIDTH, 4 * rows * n_head * HEAD_WIDTH),
+        name="attend",
+    )(own, q_all, kv_all, keys)
+
+
+def attend_rest(own, q_all, state, own_keys, pieces, kv_parts, token, order):
+    n_head, rows, _ = q_all.shape
+    stacked = n_head * QUERY_BLOCK
     n_key = sum(size for _, size in pieces)
-    n_query = rows // QUERY_BLOCK
-    stacked = n_head * QUERY_BLOCK
-    key_lines = (n_key // QUERY_BLOCK + (0 if first else n_query), QUERY_BLOCK)
-    running = jax.ShapeDtypeStruct((n_head * rows, HEAD_WIDTH), jnp.float32)
-    inputs = [*q_parts, *kv_parts] + ([] if first else list(state)) + ([order] if last else [])
-    if last:
-        out_shape = jax.ShapeDtypeStruct((rows, n_head * HEAD_WIDTH), jnp.bfloat16)
-        out_specs = whole()
-    else:
-        out_shape = (running,) * 3 + (jax.ShapeDtypeStruct((n_query, QUERY_BLOCK), jnp.int32),)
-        out_specs = (whole(),) * 4
-    return pl.pallas_call(
-        functools.partial(attend_kernel, sizes, tuple(pieces), first, last),
-        out_shape=out_shape,
-        in_specs=[pl.BlockSpec(memory_space=pltpu.SMEM)] + [whole()] * len(inputs),
-        out_specs=out_specs,
-        scratch_shapes=([VMEM((rows, n_head * HEAD_WIDTH), jnp.bfloat16)] if last else [])
-        + [VMEM((stacked, HEAD_WIDTH), jnp.float32)] * 3
-        + [
-            VMEM((n_head, rows, HEAD_WIDTH), jnp.bfloat16),
+    key_lines = ((n_key + rows) // QUERY_BLOCK, QUERY_BLOCK)
+    return pl.pallas_call(
+        functools.partial(attend_kernel, tuple(pieces), True),
+        out_shape=tuple(
+            jax.ShapeDtypeStruct((size, n_head * HEAD_WIDTH), jnp.bfloat16)
+            for size in [rows] + [rows // N_PART] * N_PART
+        ),
+        in_specs=[pl.BlockSpec(memory_space=pltpu.SMEM)]
+        + [whole()] * (5 + len(pieces))
+        + [far_memory(), whole()],
+        out_specs=(whole(),) * (1 + N_PART),
+        scratch_shapes=[
+            VMEM((rows, n_head * HEAD_WIDTH), jnp.bfloat16),
             VMEM((n_key, 2 * HEAD_WIDTH), jnp.bfloat16),
             VMEM(key_lines, jnp.int32),
-            pltpu.SMEM(key_lines, jnp.int32),
-            pltpu.SemaphoreType.DMA(()),
-        ],
+        ]
+        + [VMEM((stacked, HEAD_WIDTH), jnp.float32)] * 3
+        + [pltpu.SMEM(key_lines, jnp.int32), pltpu.SemaphoreType.DMA(())],
         compiler_params=params(12 + n_key // 512),
         cost_estimate=cost(4 * rows * n_key * n_head * HEAD_WIDTH, 4 * rows * n_head * HEAD_WIDTH),
-        name="attend",
-    )(me, *inputs)
-
-
-def columns_kernel(own, w_out, token_in, near, far, send_near, send_far, token, sem):
+        name="attend_rest",
+    )(own, q_all, *state, own_keys, *kv_parts, token, order)
+
+
+def columns_kernel(own, w_out, token_in, near, send_near, far, beside, token, sem):
     del token_in, token
-    width = near.shape[1]
+    depth, width = near.shape
+    half = depth // 2
     copies = []
-    for i, (bits, to) in enumerate(((3, send_far), (1, send_near), (2, far), (0, near))):
+    for bits, first, to in (
+        (2, own[1] * half, far),
+        (3, own[1] * half, beside),
+        (1, 0, send_near),
+        (0, 0, near),
+    ):
+        rows = pl.ds(pl.multiple_of(first, half), to.shape[0])
         at = pl.ds(pl.multiple_of(lax.bitwise_xor(own[0], bits) * width, width), width)
-        copies.append(pltpu.make_async_copy(w_out.at[:, at], to, sem.at[i]))
+        copies.append(pltpu.make_async_copy(w_out.at[rows, at], to, sem.at[len(copies)]))
     start(copies)
     wait(copies)
 
 
 def columns(own, w_out, token, width):
-    block = jax.ShapeDtypeStruct((w_out.shape[0], width), w_out.dtype)
+    rows = w_out.shape[0]
+    blocks = [jax.ShapeDtypeStruct((size, width), w_out.dtype) for size in (rows, rows, rows // 2, rows // 2)]
     return pl.pallas_call(
         columns_kernel,
-        out_shape=(block,) * 4 + (TOKEN,),
+        out_shape=(*blocks, TOKEN),
         in_specs=[pl.BlockSpec(memory_space=pltpu.SMEM), far_memory(), far_memory()],
         out_specs=(whole(),) * 4 + (far_memory(),),
-        scratch_shapes=[pltpu.SemaphoreType.DMA((4,))],
+        scratch_shapes=[pltpu.SemaphoreType.DMA((5,))],
         compiler_params=params(6),
         cost_estimate=cost(1, 4 * w_out.size),
         name="columns",
     )(own, w_out, token)
 
 
-def project_kernel(h0, h1, w0, w1, out):
-    total = jnp.dot(h0[...], w0[...], preferred_element_type=jnp.float32)
-    total += jnp.dot(h1[...], w1[...], preferred_element_type=jnp.float32)
-    out[...] = total.astype(out.dtype)
-
-
-def project(h0, h1, w0, w1, part, n_part):
-    rows, depth = h0.shape
-    width = w0.shape[1]
-    step = rows // n_part
-    return pl.pallas_call(
-        project_kernel,
-        grid=(1,),
-        in_specs=[
-            pl.BlockSpec((step, depth), lambda i: (part, 0)),
-            pl.BlockSpec((step, depth), lambda i: (part, 0)),
-            pl.BlockSpec((depth, width), lambda i: (0, 0)),
-            pl.BlockSpec((depth, width), lambda i: (0, 0)),
-        ],
-        out_specs=pl.BlockSpec((step, width), lambda i: (0, 0)),
-        out_shape=jax.ShapeDtypeStruct((step, width), jnp.bfloat16),
-        compiler_params=params(10),
-        cost_estimate=cost(4 * step * depth * width, 4 * depth * width),
-        name="project",
-    )(h0, h1, w0, w1)
-
-
-def keep_kernel(order, own, h0, h1, w0, w1, out):
+def keep_kernel(order, own, h0, h1, w0, w1, out, token):
+    del token
     total = jnp.dot(h0[...], w0[...], preferred_element_type=jnp.float32)
     total += jnp.dot(h1[...], w1[...], preferred_element_type=jnp.float32)
     out[...] = total + pick_rows(order[...], own[...])
@@ -423,18 +439,24 @@
     depth = h0.shape[1]
     return pl.pallas_call(
         keep_kernel,
-        out_shape=jax.ShapeDtypeStruct((rows, width), jnp.float32),
+        out_shape=(jax.ShapeDtypeStruct((rows, width), jnp.float32), TOKEN),
         in_specs=[whole()] * 6,
-        out_specs=whole(),
+        out_specs=(whole(), far_memory()),
         compiler_params=params(12),
         cost_estimate=cost(2 * rows * (2 * depth + rows) * width, 4 * depth * width + 6 * rows * width),
         name="keep",
     )(order, own, h0, h1, w0, w1)
 
 
-def finish_kernel(kept, received, gain, head, *refs):
-    hidden_out, sums = refs[-2:]
-    hidden = (kept[...] + received[...].astype(jnp.float32)).astype(jnp.bfloat16)
+def finish_kernel(own, kept, h2, h3, gain, head, *refs):
+    (w2, other2, w3, other3), (hidden_out, sums) = refs[:4], refs[-2:]
+    half = w2.shape[0]
+    mine = pl.ds(pl.multiple_of(own[1] * half, half), half)
+    others = pl.ds(pl.multiple_of((1 - own[1]) * half, half), half)
+    total = kept[...]
+    for h, columns, weight in ((h2, mine, w2), (h3, mine, w3), (h2, others, other2), (h3, others, other3)):
+        total += jnp.dot(h[:, columns], weight[...], preferred_element_type=jnp.float32)
+    hidden = total.astype(jnp.bfloat16)
     hidden_out[...] = hidden
     x = hidden.astype(jnp.float32)
     weighted = x * (gain[...] * head[...])
@@ -446,21 +468,25 @@
         sums[i : i + 1, :] = jnp.sum(lanes.T, 0, keepdims=True)
 
 
-def finish(kept, received, gain, head, part, n_part, hidden):
+def finish(own, kept, h2, h3, gain, head, weights, token, part, hidden):
     rows, width = kept.shape
-    step = rows // n_part
+    step, depth = h2.shape
     specs = [
+        pl.BlockSpec(memory_space=pltpu.SMEM),
         pl.BlockSpec((step, width), lambda i: (part, 0)),
-        pl.BlockSpec((step, width), lambda i: (0, 0)),
+        pl.BlockSpec((step, depth), lambda i: (0, 0)),
+        pl.BlockSpec((step, depth), lambda i: (0, 0)),
         pl.BlockSpec((1, width), lambda i: (0, 0)),
         pl.BlockSpec((1, width), lambda i: (0, 0)),
+        *(pl.BlockSpec(w.shape, lambda i: (0, 0)) for w in weights),
     ]
-    args = [kept, received, gain, head]
+    specs.append(far_memory())
+    args = [own, kept, h2, h3, gain, head, *weights, token]
     aliases = {}
     if hidden is not None:
+        aliases = {len(args): 0}
         specs.append(pl.BlockSpec(memory_space=pl.ANY))
         args.append(hidden)
-        aliases = {4: 0}
     return pl.pallas_call(
         finish_kernel,
         grid=(1,),
@@ -474,8 +500,8 @@
             jax.ShapeDtypeStruct((2, step), jnp.float32),
         ),
         input_output_aliases=aliases,
-        compiler_params=params(8),
-        cost_estimate=cost(6 * step * width, 8 * step * width),
+        compiler_params=params(14),
+        cost_estimate=cost(4 * step * depth * width, 8 * step * width),
         name="finish",
     )(*args)
 
@@ -485,8 +511,12 @@
     return lax.ppermute(x, "tensor", [(i, i ^ bit) for i in range(count)])
 
 
+def swap_parts(x):
+    return lax.ppermute(x, "parts", [(0, 1), (1, 0)])
+
+
 def chunk_sizes(rows, n_dp):
-    if n_dp > 8 or rows % 128:
+    if n_dp > 8 or rows % 256:
         return (rows,)
     return (rows // 2, rows // 2)
 
@@ -510,7 +540,6 @@
     t = lax.axis_index("tensor")
     rows, width = hidden_in.shape
     sizes = chunk_sizes(rows, n_dp)
-    n_part = 2
 
     own = [hidden_in[sum(sizes[:c]) : sum(sizes[: c + 1])] for c in range(len(sizes))]
     across = [flip(x, 2) for x in own]
@@ -521,58 +550,86 @@
         row_loads, seg_ids.reshape(lines, QUERY_BLOCK), pos_ids.reshape(lines, QUERY_BLOCK)
     )
     gain = attn_gain.reshape(1, -1)
-    t_own = t.astype(jnp.int32).reshape(1)
+    t_own = jnp.stack([t, lax.axis_index("parts"), me]).astype(jnp.int32)
     acc, squares, far_weights, token = early(
         t_own, hidden_in, pair, gain, w_query, key_matrix, value_matrix
     )
 
+    near, send_near, far2, far3, token = columns(t_own, w_out, token, width)
+    near_other = flip(send_near, 1)
+
     q_parts, kv_parts = [], [[] for _ in range(n_dp)]
     for c in range(len(sizes)):
+        received, token = lax.optimization_barrier((across[c], token))
+        if c == len(sizes) - 1:
+            far2, far3, token = lax.optimization_barrier((far2, far3, token))
+            far2, far3 = flip(far2, 2), flip(far3, 3)
         if c > 0:
             for d in range(1, n_dp):
                 kv_parts[d][-1], token = lax.optimization_barrier((kv_parts[d][-1], token))
-        received, token = lax.optimization_barrier((across[c], token))
+        received, token = lax.optimization_barrier((received, token))
         diagonal = flip(received, 1)
-        q, kv, token = late(
-            sum(sizes[:c]), t_own, token, acc, squares, received, diagonal, gain, far_weights, cos, sin, digits
+        if c > 0:
+            near_other, token = lax.optimization_barrier((near_other, token))
+        last = c == len(sizes) - 1
+        soon = [(0, i) for i in range(c)] + [(d, i) for d in range(1, n_dp) for i in range(c)] if last else []
+        q, kv, *side, token = late(
+            sum(sizes[:c]),
+            t_own,
+            token,
+            acc,
+            squares,
+            received,
+            diagonal,
+            gain,
+            far_weights,
+            cos,
+            sin,
+            digits,
+            last,
+            q_parts if last else [],
+            [(d, sizes[i]) for d, i in soon],
+            [kv_parts[d][i] for d, i in soon],
         )
         q_parts.append(q)
         kv_parts[0].append(kv)
         for d in range(1, n_dp):
             kv_parts[d].append(lax.ppermute(kv, "dp", [(i, (i + d) % n_dp) for i in range(n_dp)]))
-        if c == 0:
-            near, far, send_near, send_far, token = columns(t_own, w_out, token, width)
-            near_other, far_other = flip(send_near, 1), flip(send_far, 1)
 
     order = prompt_order.reshape(1, rows)
-    me_own = me.astype(jnp.int32).reshape(1)
-    numbers = range(len(sizes))
-    soon = [(0, c) for c in numbers] + [(d, c) for d in range(1, n_dp) for c in numbers[:-1]]
-    then = [(d, numbers[-1]) for d in range(1, n_dp)]
-    if len(sizes) == 1:
-        soon, then = soon + then, []
-    state = None
-    for some in (soon, then):
-        if some:
-            pieces = [(d, sizes[c]) for d, c in some]
-            last = some is then or not then
-            state = attend(
-                me_own, q_parts, pieces, [kv_parts[d][c] for d, c in some], state, order if last else None
-            )
-    heads = state
+    q_all, (kv_all, keys) = q, side
+    *state, token = attend(t_own, q_all, kv_all, keys)
+    far3, token = lax.optimization_barrier((far3, token))
+    other3 = swap_parts(far3)
+    heads, *parts = attend_rest(
+        t_own,
+        q_all,
+        state,
+        keys,
+        [(d, sizes[-1]) for d in range(1, n_dp)],
+        [kv_parts[d][-1] for d in range(1, n_dp)],
+        token,
+        order,
+    )
+    heads2 = [flip(parts[0], 2)]
+    rest, far2, other3 = lax.optimization_barrier((parts[1], far2, other3))
+    heads2.append(flip(rest, 2))
+    other2 = swap_parts(far2)
+    weights = (far2, other2, far3, other3)
     heads_other = flip(heads, 1)
-    sent = [
-        flip(project(heads, heads_other, far, far_other, j, n_part), 2) for j in range(n_part)
-    ]
-    kept = keep(order, hidden_in, heads, heads_other, near, near_other)
+    kept, token = keep(order, hidden_in, heads, heads_other, near, near_other)
+    heads2[0], token = lax.optimization_barrier((heads2[0], token))
+    heads3 = [flip(x, 1) for x in heads2]
     final = final_gain.astype(jnp.float32).reshape(1, width)
     head = value_head.astype(jnp.float32).reshape(1, width)
-    hidden, sums = None, []
-    for j in range(n_part):
-        hidden, part = finish(kept, sent[j], final, head, j, n_part, hidden)
-        sums.append(part)
-    square, product = lax.psum(jnp.concatenate(sums, 1), "tensor")
-    return hidden, product * lax.rsqrt(square / MODEL_WIDTH + NORM_EPS)
+    hidden, values = None, []
+    for j in range(N_PART):
+        hidden, sums = finish(
+            t_own, kept, heads2[j], heads3[j], final, head, weights, token, j, hidden
+        )
+        square, product = sums + flip(sums, 1) + (flip(sums, 2) + flip(sums, 3))
+        values.append(product * lax.rsqrt(square / MODEL_WIDTH + NORM_EPS))
+    return hidden, jnp.concatenate(values)
 
 
 def solution(mesh):

time: 101 us -> 90.7 us (0.90); the launches traced: 99.5 us -> 90.4 us
  starting transfers between devices: 14.7 us -> 23.8 us
  local copies, waits for them, and re-layouts: 16 us -> 8.23 us
  blocking collectives: 5.95 us -> 0 us
  Pallas kernels: 27.8 us -> 25.2 us
  waiting for transfers between devices: 33.6 us -> 31.7 us
    ppermute x10 -> x19, waiting for transfers between devices: 24.9 us -> 17.5 us  [flip(): return lax.ppermute(x, 'tensor', [(i, i ^ bit) for i in range(count)])]
    ppermute x10 -> x19, starting transfers between devices: 7.43 us -> 14.6 us  [flip(): return lax.ppermute(x, 'tensor', [(i, i ^ bit) for i in range(count)])]
    unnamed x46 -> x24, local copies, waits for them, and re-layouts: 13.2 us -> 6.25 us
    ppermute x0 -> x2, waiting for transfers between devices: none -> 6.87 us  [swap_parts(): return lax.ppermute(x, 'parts', [(0, 1), (1, 0)])]
    psum x1 -> x0, blocking collectives: 5.95 us -> none  [on_device(): square, product = lax.psum(jnp.concatenate(sums, 1), 'tensor')]
    pallas_call x8 -> x6, Pallas kernels: 20.5 us -> 15.2 us  [the longest x1 4.94 us: attend(): pl.pallas_call(functools.partial(attend_kernel, (), False), out_shape=(ru...]
    ppermute x0 -> x2, starting transfers between devices: none -> 2.48 us  [swap_parts(): return lax.ppermute(x, 'parts', [(0, 1), (1, 0)])]
    pallas_call x2, Pallas kernels: 1.96 us -> 4.15 us  [finish(): pl.pallas_call(finish_kernel, grid=(1,), in_specs=specs, out_specs=(pl.Bl...]
  transfers between devices with their start and end apart: 16 -> 27, of which waited for: 7 -> 12; matrix products, arithmetic and copies ran while one was open for 3% -> 2% of each run, Pallas kernels for 27% -> 28%
where the time goes in v3:
time: 90.7 us; the launch traced here: 90.4 us
  waiting for transfers between devices  31.7 us (35%)
  Pallas kernels  25.2 us (28%)
  starting transfers between devices  23.8 us (26%)
  local copies, waits for them, and re-layouts  8.23 us (9%)
    ppermute x19, waiting for transfers between devices, flip(): return lax.ppermute(x, 'tensor', [(i, i ^ bit) for i in range(count)])  17.5 us
    ppermute x19, starting transfers between devices, flip(): return lax.ppermute(x, 'tensor', [(i, i ^ bit) for i in range(count)])  14.6 us
    ppermute x6, waiting for transfers between devices, on_device(): lax.ppermute(kv, 'dp', [(i, (i + d) % n_dp) for i in range(n_dp)])  7.35 us
    ppermute x2, waiting for transfers between devices, swap_parts(): return lax.ppermute(x, 'parts', [(0, 1), (1, 0)])  6.87 us
    ppermute x6, starting transfers between devices, on_device(): lax.ppermute(kv, 'dp', [(i, (i + d) % n_dp) for i in range(n_dp)])  6.71 us
    unnamed x24, local copies, waits for them, and re-layouts  6.25 us
    pallas_call x1, Pallas kernels, attend(): pl.pallas_call(functools.partial(attend_kernel, (), False), out_shape=(ru...  4.94 us
    pallas_call x1, Pallas kernels, early(): pl.pallas_call(early_kernel, out_shape=(jax.ShapeDtypeStruct((rows, colum...  4.23 us
  transfers between devices with their start and end apart: 27, of which 12 were waited for; matrix products, arithmetic and copies ran while one was open for 2% of the time, Pallas kernels for 28%

profile of v3, /device:TPU:9, one launch (start us, length us, event | category | flops | bytes accessed | tf_op | source)
XLA Modules:
  0.0 90.4 jit_solution(10217189191720932266)
XLA Ops:
  0.6 0.7 collective-permute-start
  1.4 1.3 %fusion.6 = (bf16[256,1024]{1,0:T(8,128)(2,1)S(1)}, bf16[256,1024]{1,0:T(8,128)(2,1)S(1)}) fusion(bf16[512,1024]{1,0:T(8,128)(2,1)} %own.1), kind=kLoop, calls=%fused_computation.12 | loop fusion | bytes 2097152 | tf_op jit(solution)/shard_map/slice | solution.py:544
  2.6 1.3 %collective-permute-start.3 = (bf16[256,1024]{1,0:T(8,128)(2,1)S(1)}, bf16[256,1024]{1,0:T(8,128)(2,1)S(1)}, u32[]{:S(2)}, u32[]{:S(2)}) collective-permute-start(bf16[256,1024]{1,0:T(8,128)(2,1)S(1)} %get-tuple-element.114), channel_id=1, source_target_pairs={{0,2},{1,3},{2,0},{3,1},{4,6},{5,7},{6,4},{7,5},{8,10},{9,11},{10,... | collective-permute-start | bytes 1572872 | tf_op jit(solution)/shard_map/ppermute | solution.py:511
  3.9 0.7 reshape.35.gain
  4.6 0.1 pad_add_fusion.own
  4.7 0.0 collective-permute-done.r1
  4.7 1.4 %copy-done.1 = bf16[512,1024]{1,0:T(8,128)(2,1)S(1)} copy-done((bf16[512,1024]{1,0:T(8,128)(2,1)S(1)}, bf16[512,1024]{1,0:T(8,128)(2,1)}, u32[]{:S(2)}) %copy-start.1) | copy-done | bytes 1048600
  6.1 2.4 %copy-done.3 = bf16[4096,512]{1,0:T(8,128)(2,1)S(1)} copy-done((bf16[4096,512]{1,0:T(8,128)(2,1)S(1)}, bf16[4096,512]{1,0:T(8,128)(2,1)}, u32[]{:S(2)}) %copy-start.3) | copy-done | bytes 4194328
  8.5 1.2 %copy-done.4 = bf16[4096,128]{1,0:T(8,128)(2,1)S(1)} copy-done((bf16[4096,128]{1,0:T(8,128)(2,1)S(1)}, bf16[4096,128]{1,0:T(8,128)(2,1)}, u32[]{:S(2)}) %copy-start.4) | copy-done | bytes 1048600
  9.7 1.2 %copy-done.5 = bf16[4096,128]{1,0:T(8,128)(2,1)S(1)} copy-done((bf16[4096,128]{1,0:T(8,128)(2,1)S(1)}, bf16[4096,128]{1,0:T(8,128)(2,1)}, u32[]{:S(2)}) %copy-start.5) | copy-done | bytes 1048600
  10.9 4.2 %early.1 = (f32[512,768]{1,0:T(8,128)S(1)}, f32[512,1]{1,0:T(8,128)S(1)}, bf16[2,1024,768]{2,1,0:T(8,128)(2,1)S(1)}, f32[8,128]{1,0:T(8,128)S(1)}) custom-call(s32[3]{0:T(128)S(1)} %pad_add_fusion.own, bf16[512,1024]{1,0:T(8,128)(2,1)S(1)} %copy-done.1, bf16[512,1024]{1,0:T(8,128)(2,1)S(1)} %collective-permute-done.r1, bf16[1,4096]{1,0:T(2,128)(2,1)S(1)} %reshape.35.gain, ...), custom_call_target="tpu_custom_call" | custom-call | flops 1610612736 | bytes 6291456 | tf_op jit(solution)/shard_map/early/pallas_call | solution.py:144
  15.2 0.0 copy-start.7
  15.2 0.0 copy-start.8
  15.2 0.0 copy-start.9
  15.2 1.0 %columns.1 = (bf16[512,1024]{1,0:T(8,128)(2,1)S(1)}, bf16[512,1024]{1,0:T(8,128)(2,1)S(1)}, bf16[256,1024]{1,0:T(8,128)(2,1)S(1)}, bf16[256,1024]{1,0:T(8,128)(2,1)S(1)}, f32[8,128]{1,0:T(8,128)S(1)}) custom-call(s32[3]{0:T(128)S(1)} %pad_add_fusion.own, bf16[512,4096]{1,0:T(8,128)(2,1)S(1)} %copy-done, f32[8,128]{1,0:T(8,128)S(1)} %get-tuple-element.58.token_in), custom_call_target="tpu_custom_call" | custom-call | flops 1 | bytes 8388608 | tf_op jit(solution)/shard_map/columns/pallas_call | solution.py:418
  16.3 0.8 collective-permute-start.4
  17.0 1.2 %collective-permute-start.2 = (bf16[256,1024]{1,0:T(8,128)(2,1)S(1)}, bf16[256,1024]{1,0:T(8,128)(2,1)S(1)}, u32[]{:S(2)}, u32[]{:S(2)}) collective-permute-start(bf16[256,1024]{1,0:T(8,128)(2,1)S(1)} %get-tuple-element.115), channel_id=1, source_target_pairs={{0,2},{1,3},{2,0},{3,1},{4,6},{5,7},{6,4},{7,5},{8,10},{9,11},{10,... | collective-permute-start | bytes 1572872 | tf_op jit(solution)/shard_map/ppermute | solution.py:511
  18.3 0.3 collective-permute-start.1
  18.5 1.6 %prep.1 = (bf16[16,512]{1,0:T(8,128)(2,1)S(1)}, f32[512,128]{1,0:T(8,128)S(1)}, f32[512,128]{1,0:T(8,128)S(1)}) custom-call(s32[1,4]{1,0:T(1,128)S(1)} %copy-done.9, s32[4,128]{1,0:T(4,128)S(1)} %bitcast.13, s32[4,128]{1,0:T(4,128)S(1)} %bitcast.14), custom_call_target="tpu_custom_call" | custom-call | flops 2000000000 | bytes 40000000 | tf_op jit(solution)/shard_map/prep/pallas_call | solution.py:80
  20.1 1.8 %late.2 = (bf16[4,256,128]{2,1,0:T(8,128)(2,1)S(1)}, bf16[272,256]{1,0:T(8,128)(2,1)S(1)}, f32[8,128]{1,0:T(8,128)S(1)}) custom-call(s32[3]{0:T(128)S(1)} %pad_add_fusion.own, f32[8,128]{1,0:T(8,128)S(1)} %get-tuple-element.61.before, f32[512,768]{1,0:T(8,128)S(1)} %get-tuple-element.62.acc, f32[512,1]{1,0:T(8,128)S(1)} %get-tuple-element.63.squares, ...), custom_call_target="tpu_custom_call" | custom-call | flops 805306368 | bytes 3145728 | tf_op jit(solution)/shard_map/late/pallas_call | solution.py:235
  21.9 1.3 %collective-permute-start.7 = (bf16[272,256]{1,0:T(8,128)(2,1)S(1)}, bf16[272,256]{1,0:T(8,128)(2,1)S(1)}, u32[]{:S(2)}, u32[]{:S(2)}) collective-permute-start(bf16[272,256]{1,0:T(8,128)(2,1)S(1)} %get-tuple-element.71.refs_1_), channel_id=1, source_target_pairs={{0,4},{4,8},{8,12},{12,0},{1,5},{5,9},{9,13},{13,1},{2,6},{6,10},{... | collective-permute-start | bytes 417800 | tf_op jit(solution)/shard_map/ppermute | solution.py:597
  23.3 1.1 %collective-permute-start.6 = (bf16[272,256]{1,0:T(8,128)(2,1)S(1)}, bf16[272,256]{1,0:T(8,128)(2,1)S(1)}, u32[]{:S(2)}, u32[]{:S(2)}) collective-permute-start(bf16[272,256]{1,0:T(8,128)(2,1)S(1)} %get-tuple-element.71.refs_1_), channel_id=1, source_target_pairs={{0,8},{4,12},{8,0},{12,4},{1,9},{5,13},{9,1},{13,5},{2,10},{6,14},... | collective-permute-start | bytes 417800 | tf_op jit(solution)/shard_map/ppermute | solution.py:597
  24.4 1.4 %collective-permute-start.5 = (bf16[272,256]{1,0:T(8,128)(2,1)S(1)}, bf16[272,256]{1,0:T(8,128)(2,1)S(1)}, u32[]{:S(2)}, u32[]{:S(2)}) collective-permute-start(bf16[272,256]{1,0:T(8,128)(2,1)S(1)} %get-tuple-element.71.refs_1_), channel_id=1, source_target_pairs={{0,12},{4,0},{8,4},{12,8},{1,13},{5,1},{9,5},{13,9},{2,14},{6,2},{... | collective-permute-start | bytes 417800 | tf_op jit(solution)/shard_map/ppermute | solution.py:597
  25.8 4.8 %collective-permute-done.2.r2 = bf16[256,1024]{1,0:T(8,128)(2,1)S(1)} collective-permute-done((bf16[256,1024]{1,0:T(8,128)(2,1)S(1)}, bf16[256,1024]{1,0:T(8,128)(2,1)S(1)}, u32[]{:S(2)}, u32[]{:S(2)}) %collective-permute-start.2) | collective-permute-done | bytes 524320 | tf_op jit(solution)/shard_map/ppermute | solution.py:511
  30.6 4.5 %collective-permute-done.6.refs_3_ = bf16[272,256]{1,0:T(8,128)(2,1)S(1)} collective-permute-done((bf16[272,256]{1,0:T(8,128)(2,1)S(1)}, bf16[272,256]{1,0:T(8,128)(2,1)S(1)}, u32[]{:S(2)}, u32[]{:S(2)}) %collective-permute-start.6) | collective-permute-done | bytes 139296 | tf_op jit(solution)/shard_map/ppermute | solution.py:597
  35.1 2.3 %collective-permute-done.5.refs_4_ = bf16[272,256]{1,0:T(8,128)(2,1)S(1)} collective-permute-done((bf16[272,256]{1,0:T(8,128)(2,1)S(1)}, bf16[272,256]{1,0:T(8,128)(2,1)S(1)}, u32[]{:S(2)}, u32[]{:S(2)}) %collective-permute-start.5) | collective-permute-done | bytes 139296 | tf_op jit(solution)/shard_map/ppermute | solution.py:597
  37.4 0.5 collective-permute-start.8
  37.9 0.2 collective-permute-start.12
  38.1 1.2 %collective-permute-start.14 = (bf16[256,1024]{1,0:T(8,128)(2,1)S(1)}, bf16[256,1024]{1,0:T(8,128)(2,1)S(1)}, u32[]{:S(2)}, u32[]{:S(2)}) collective-permute-start(bf16[256,1024]{1,0:T(8,128)(2,1)S(1)} %get-tuple-element.101), channel_id=1, source_target_pairs={{0,2},{1,3},{2,0},{3,1},{4,6},{5,7},{6,4},{7,5},{8,10},{9,11},{10,... | collective-permute-start | bytes 1572872 | tf_op jit(solution)/shard_map/ppermute | solution.py:511
  39.3 0.2 collective-permute-done.8.r3
  39.4 1.9 %late.3 = (bf16[4,512,128]{2,1,0:T(8,128)(2,1)S(1)}, bf16[272,256]{1,0:T(8,128)(2,1)S(1)}, bf16[1280,256]{1,0:T(8,128)(2,1)S(1)}, s32[10,128]{1,0:T(8,128)S(1)}, f32[8,128]{1,0:T(8,128)}) custom-call(s32[3]{0:T(128)S(1)} %pad_add_fusion.own, f32[8,128]{1,0:T(8,128)S(1)} %get-tuple-element.80.before, f32[512,768]{1,0:T(8,128)S(1)} %get-tuple-element.62.acc, ...), custom_call_target="tpu_custom_call" | custom-call | flops 805306368 | bytes 3145728 | tf_op jit(solution)/shard_map/late/pallas_call | solution.py:235
  41.3 0.0 copy-start.6
  41.3 1.4 %collective-permute-start.10 = (bf16[272,256]{1,0:T(8,128)(2,1)S(1)}, bf16[272,256]{1,0:T(8,128)(2,1)S(1)}, u32[]{:S(2)}, u32[]{:S(2)}) collective-permute-start(bf16[272,256]{1,0:T(8,128)(2,1)S(1)} %get-tuple-element.92), channel_id=1, source_target_pairs={{0,8},{4,12},{8,0},{12,4},{1,9},{5,13},{9,1},{13,5},{2,10},{6,14},... | collective-permute-start | bytes 417800 | tf_op jit(solution)/shard_map/ppermute | solution.py:597
  42.7 1.5 %collective-permute-start.9 = (bf16[272,256]{1,0:T(8,128)(2,1)S(1)}, bf16[272,256]{1,0:T(8,128)(2,1)S(1)}, u32[]{:S(2)}, u32[]{:S(2)}) collective-permute-start(bf16[272,256]{1,0:T(8,128)(2,1)S(1)} %get-tuple-element.92), channel_id=1, source_target_pairs={{0,4},{4,8},{8,12},{12,0},{1,5},{5,9},{9,13},{13,1},{2,6},{6,10},{... | collective-permute-start | bytes 417800 | tf_op jit(solution)/shard_map/ppermute | solution.py:597
  44.2 4.9 %attend.1 = (f32[2048,128]{1,0:T(8,128)S(1)}, f32[2048,128]{1,0:T(8,128)S(1)}, f32[2048,128]{1,0:T(8,128)S(1)}, f32[8,128]{1,0:T(8,128)S(1)}) custom-call(s32[3]{0:T(128)S(1)} %pad_add_fusion.own, bf16[4,512,128]{2,1,0:T(8,128)(2,1)S(1)} %get-tuple-element.86.q_all, bf16[1280,256]{1,0:T(8,128)(2,1)S(1)} %get-tuple-element.87.refs_0_, ...), custom_call_target="tpu_custom_call" | custom-call | flops 1342177280 | bytes 1048576 | tf_op jit(solution)/shard_map/attend/pallas_call | solution.py:356
  49.1 0.0 copy-start.2
  49.1 3.0 %collective-permute-done.12.refs_2_ = bf16[256,1024]{1,0:T(8,128)(2,1)S(1)} collective-permute-done((bf16[256,1024]{1,0:T(8,128)(2,1)S(1)}, bf16[256,1024]{1,0:T(8,128)(2,1)S(1)}, u32[]{:S(2)}, u32[]{:S(2)}) %collective-permute-start.12) | collective-permute-done | bytes 524320 | tf_op jit(solution)/shard_map/ppermute | solution.py:511
  52.1 1.2 %collective-permute-start.15 = (bf16[256,1024]{1,0:T(8,128)(2,1)S(1)}, bf16[256,1024]{1,0:T(8,128)(2,1)S(1)}, u32[]{:S(2)}, u32[]{:S(2)}) collective-permute-start(bf16[256,1024]{1,0:T(8,128)(2,1)S(1)} %collective-permute-done.12.refs_2_), channel_id=1, source_target_pairs={{0,16},{16,0},{1,17},{17,1},{2,18},{18,2},{3,19},{19,3},{4,20},{20... | collective-permute-start | bytes 1572872 | tf_op jit(solution)/shard_map/ppermute | solution.py:515
  53.4 0.5 collective-permute-done.9.refs_4_
  53.9 3.8 %attend_rest.1 = (bf16[512,512]{1,0:T(8,128)(2,1)S(1)}, bf16[256,512]{1,0:T(8,128)(2,1)S(1)}, bf16[256,512]{1,0:T(8,128)(2,1)S(1)}) custom-call(s32[3]{0:T(128)S(1)} %pad_add_fusion.own, bf16[4,512,128]{2,1,0:T(8,128)(2,1)S(1)} %get-tuple-element.86.q_all, f32[2048,128]{1,0:T(8,128)S(1)} %get-tuple-element.89.refs_0_, ...), custom_call_target="tpu_custom_call" | custom-call | flops 805306368 | bytes 1048576 | tf_op jit(solution)/shard_map/attend_rest/pallas_call | solution.py:374
  57.7 0.0 copy-start.10
  57.7 0.0 copy-start.11
  57.7 0.6 collective-permute-start.13
  58.3 0.3 collective-permute-start.19
  58.6 3.8 %collective-permute-done.14.refs_0_ = bf16[256,1024]{1,0:T(8,128)(2,1)S(1)} collective-permute-done((bf16[256,1024]{1,0:T(8,128)(2,1)S(1)}, bf16[256,1024]{1,0:T(8,128)(2,1)S(1)}, u32[]{:S(2)}, u32[]{:S(2)}) %collective-permute-start.14) | collective-permute-done | bytes 524320 | tf_op jit(solution)/shard_map/ppermute | solution.py:511
  62.4 3.6 %collective-permute-done.15.refs_3_ = bf16[256,1024]{1,0:T(8,128)(2,1)S(1)} collective-permute-done((bf16[256,1024]{1,0:T(8,128)(2,1)S(1)}, bf16[256,1024]{1,0:T(8,128)(2,1)S(1)}, u32[]{:S(2)}, u32[]{:S(2)}) %collective-permute-start.15) | collective-permute-done | bytes 524320 | tf_op jit(solution)/shard_map/ppermute | solution.py:515
  65.9 1.2 %collective-permute-start.18 = (bf16[256,1024]{1,0:T(8,128)(2,1)S(1)}, bf16[256,1024]{1,0:T(8,128)(2,1)S(1)}, u32[]{:S(2)}, u32[]{:S(2)}) collective-permute-start(bf16[256,1024]{1,0:T(8,128)(2,1)S(1)} %collective-permute-done.14.refs_0_), channel_id=1, source_target_pairs={{0,16},{16,0},{1,17},{17,1},{2,18},{18,2},{3,19},{19,3},{4,20},{20... | collective-permute-start | bytes 1572872 | tf_op jit(solution)/shard_map/ppermute | solution.py:515
  67.2 0.3 collective-permute-start.16
  67.5 1.8 %keep.1 = (f32[512,1024]{1,0:T(8,128)S(1)}, f32[8,128]{1,0:T(8,128)S(1)}) custom-call(s32[1,512]{1,0:T(1,128)S(1)} %copy-done.6, bf16[512,1024]{1,0:T(8,128)(2,1)S(1)} %copy-done.2, bf16[512,512]{1,0:T(8,128)(2,1)S(1)} %get-tuple-element.96.h0, bf16[512,512]{1,0:T(8,128)(2,1)S(1)} %collective-permute-done.13.h1, bf16[512,1024]{1,0:T(8,128)(2,1)S(1)} %get-tuple-element.97.w0, ...), custom_call_target="tpu_custom_call" | custom-call | flops 1610612736 | bytes 5242880 | tf_op jit(solution)/shard_map/keep/pallas_call | solution.py:440
  69.3 1.1 %collective-permute-start.20 = (bf16[256,512]{1,0:T(8,128)(2,1)S(1)}, bf16[256,512]{1,0:T(8,128)(2,1)S(1)}, u32[]{:S(2)}, u32[]{:S(2)}) collective-permute-start(bf16[256,512]{1,0:T(8,128)(2,1)S(1)} %collective-permute-done.19.h2), channel_id=1, source_target_pairs={{0,1},{1,0},{2,3},{3,2},{4,5},{5,4},{6,7},{7,6},{8,9},{9,8},{10,11... | collective-permute-start | bytes 786440 | tf_op jit(solution)/shard_map/ppermute | solution.py:511
  70.4 4.1 %collective-permute-done.16.h2 = bf16[256,512]{1,0:T(8,128)(2,1)S(1)} collective-permute-done((bf16[256,512]{1,0:T(8,128)(2,1)S(1)}, bf16[256,512]{1,0:T(8,128)(2,1)S(1)}, u32[]{:S(2)}, u32[]{:S(2)}) %collective-permute-start.16) | collective-permute-done | bytes 262176 | tf_op jit(solution)/shard_map/ppermute | solution.py:511
  74.5 1.4 %collective-permute-start.17 = (bf16[256,512]{1,0:T(8,128)(2,1)S(1)}, bf16[256,512]{1,0:T(8,128)(2,1)S(1)}, u32[]{:S(2)}, u32[]{:S(2)}) collective-permute-start(bf16[256,512]{1,0:T(8,128)(2,1)S(1)} %collective-permute-done.16.h2), channel_id=1, source_target_pairs={{0,1},{1,0},{2,3},{3,2},{4,5},{5,4},{6,7},{7,6},{8,9},{9,8},{10,11... | collective-permute-start | bytes 786440 | tf_op jit(solution)/shard_map/ppermute | solution.py:511
  75.9 3.3 %collective-permute-done.18.refs_1_ = bf16[256,1024]{1,0:T(8,128)(2,1)S(1)} collective-permute-done((bf16[256,1024]{1,0:T(8,128)(2,1)S(1)}, bf16[256,1024]{1,0:T(8,128)(2,1)S(1)}, u32[]{:S(2)}, u32[]{:S(2)}) %collective-permute-start.18) | collective-permute-done | bytes 524320 | tf_op jit(solution)/shard_map/ppermute | solution.py:515
  79.2 2.1 %finish.2 = (bf16[512,1024]{1,0:T(8,128)(2,1)}, f32[2,256]{1,0:T(2,128)S(1)}) custom-call(s32[3]{0:T(128)S(1)} %pad_add_fusion.own, f32[512,1024]{1,0:T(8,128)S(1)} %get-tuple-element.99.kept, bf16[256,512]{1,0:T(8,128)(2,1)S(1)} %collective-permute-done.19.h2, bf16[256,512]{1,0:T(8,128)(2,1)S(1)} %collective-permute-done.20.h3, f32[1,1024]{1,0:T(1,128)S(1)} %bitcast.9, ...), custom_call_target="tpu_custom_call" | custom-call | flops 536870912 | bytes 2097152 | tf_op jit(solution)/shard_map/finish/pallas_call | solution.py:490
  81.3 1.0 %collective-permute-start.21 = (f32[2,256]{1,0:T(2,128)S(1)}, f32[2,256]{1,0:T(2,128)S(1)}, u32[]{:S(2)}, u32[]{:S(2)}) collective-permute-start(f32[2,256]{1,0:T(2,128)S(1)} %get-tuple-element.112), channel_id=1, source_target_pairs={{0,1},{1,0},{2,3},{3,2},{4,5},{5,4},{6,7},{7,6},{8,9},{9,8},{10,11... | collective-permute-start | bytes 6152 | tf_op jit(solution)/shard_map/ppermute | solution.py:511
  82.3 0.3 collective-permute-start.22
  82.6 1.3 %collective-permute-start.23 = (f32[2,256]{1,0:T(2,128)S(1)}, f32[2,256]{1,0:T(2,128)S(1)}, u32[]{:S(2)}, u32[]{:S(2)}) collective-permute-start(f32[2,256]{1,0:T(2,128)S(1)} %get-tuple-element.112), channel_id=1, source_target_pairs={{0,3},{1,2},{2,1},{3,0},{4,7},{5,6},{6,5},{7,4},{8,11},{9,10},{10,... | collective-permute-start | bytes 6152 | tf_op jit(solution)/shard_map/ppermute | solution.py:511
  84.0 2.1 %finish.3 = (bf16[512,1024]{1,0:T(8,128)(2,1)}, f32[2,256]{1,0:T(2,128)S(1)}) custom-call(s32[3]{0:T(128)S(1)} %pad_add_fusion.own, f32[512,1024]{1,0:T(8,128)S(1)} %get-tuple-element.99.kept, bf16[256,512]{1,0:T(8,128)(2,1)S(1)} %collective-permute-done.16.h2, bf16[256,512]{1,0:T(8,128)(2,1)S(1)} %collective-permute-done.17.h3, ...), custom_call_target="tpu_custom_call", output_to_operand_aliasing={{0}: (11, {})} | custom-call | flops 536870912 | bytes 2097152 | tf_op jit(solution)/shard_map/finish/pallas_call | solution.py:490
  86.0 0.2 collective-permute-start.24
  86.3 0.3 collective-permute-start.25
  86.6 1.6 %collective-permute-start.26 = (f32[2,256]{1,0:T(2,128)S(1)}, f32[2,256]{1,0:T(2,128)S(1)}, u32[]{:S(2)}, u32[]{:S(2)}) collective-permute-start(f32[2,256]{1,0:T(2,128)S(1)} %get-tuple-element.113), channel_id=1, source_target_pairs={{0,3},{1,2},{2,1},{3,0},{4,7},{5,6},{6,5},{7,4},{8,11},{9,10},{10,... | collective-permute-start | bytes 6152 | tf_op jit(solution)/shard_map/ppermute | solution.py:511
  88.2 0.5 collective-permute-done.25
  88.7 1.1 %collective-permute-done.26 = f32[2,256]{1,0:T(2,128)S(1)} collective-permute-done((f32[2,256]{1,0:T(2,128)S(1)}, f32[2,256]{1,0:T(2,128)S(1)}, u32[]{:S(2)}, u32[]{:S(2)}) %collective-permute-start.26) | collective-permute-done | bytes 2080 | tf_op jit(solution)/shard_map/ppermute | solution.py:511
  89.8 0.6 pad_maximum_fusion
  (34 shorter events, 0.1 us)
Async XLA Ops:
  0.6 4.1 %collective-permute-start = (bf16[512,1024]{1,0:T(8,128)(2,1)}, bf16[512,1024]{1,0:T(8,128)(2,1)S(1)}, u32[]{:S(2)}, u32[]{:S(2)}) collective-permute-start(bf16[512,1024]{1,0:T(8,128)(2,1)} %own.1), channel_id=1, source_target_pairs={{0,1},{1,0},{2,3},{3,2},{4,5},{5,4},{6,7},{7,6},{8,9},{9,8},{10,11... | collective-permute-start | bytes 3145736 | tf_op jit(solution)/shard_map/ppermute | solution.py:511
  2.6 13.6 %collective-permute-start.3 = (bf16[256,1024]{1,0:T(8,128)(2,1)S(1)}, bf16[256,1024]{1,0:T(8,128)(2,1)S(1)}, u32[]{:S(2)}, u32[]{:S(2)}) collective-permute-start(bf16[256,1024]{1,0:T(8,128)(2,1)S(1)} %get-tuple-element.114), channel_id=1, source_target_pairs={{0,2},{1,3},{2,0},{3,1},{4,6},{5,7},{6,4},{7,5},{8,10},{9,11},{10,... | collective-permute-start | bytes 1572872 | tf_op jit(solution)/shard_map/ppermute | solution.py:511
  4.7 10.5 %copy-start = (bf16[512,4096]{1,0:T(8,128)(2,1)S(1)}, bf16[512,4096]{1,0:T(8,128)(2,1)}, u32[]{:S(2)}) copy-start(bf16[512,4096]{1,0:T(8,128)(2,1)} %w_out.1) | copy-start | bytes 12582916
  4.7 1.4 %copy-start.1 = (bf16[512,1024]{1,0:T(8,128)(2,1)S(1)}, bf16[512,1024]{1,0:T(8,128)(2,1)}, u32[]{:S(2)}) copy-start(bf16[512,1024]{1,0:T(8,128)(2,1)} %own.1) | copy-start | bytes 3145732
  6.1 2.4 %copy-start.3 = (bf16[4096,512]{1,0:T(8,128)(2,1)S(1)}, bf16[4096,512]{1,0:T(8,128)(2,1)}, u32[]{:S(2)}) copy-start(bf16[4096,512]{1,0:T(8,128)(2,1)} %wq.1) | copy-start | bytes 12582916
  8.5 1.2 %copy-start.4 = (bf16[4096,128]{1,0:T(8,128)(2,1)S(1)}, bf16[4096,128]{1,0:T(8,128)(2,1)}, u32[]{:S(2)}) copy-start(bf16[4096,128]{1,0:T(8,128)(2,1)} %wk.1) | copy-start | bytes 3145732
  9.7 1.2 %copy-start.5 = (bf16[4096,128]{1,0:T(8,128)(2,1)S(1)}, bf16[4096,128]{1,0:T(8,128)(2,1)}, u32[]{:S(2)}) copy-start(bf16[4096,128]{1,0:T(8,128)(2,1)} %wv.1) | copy-start | bytes 3145732
  15.2 3.4 %copy-start.7 = (s32[512]{0:T(512)S(1)}, s32[512]{0:T(512)}, u32[]{:S(2)}) copy-start(s32[512]{0:T(512)} %param.14) | copy-start | bytes 6148
  15.2 3.4 %copy-start.8 = (s32[512]{0:T(512)S(1)}, s32[512]{0:T(512)}, u32[]{:S(2)}) copy-start(s32[512]{0:T(512)} %param.15) | copy-start | bytes 6148
  15.2 3.4 %copy-start.9 = (s32[1,4]{1,0:T(1,128)S(1)}, s32[1,4]{1,0:T(1,128)}, u32[]{:S(2)}) copy-start(s32[1,4]{1,0:T(1,128)} %loads.1) | copy-start | bytes 52
  16.3 3.9 %collective-permute-start.4 = (bf16[256,1024]{1,0:T(8,128)(2,1)S(1)}, bf16[256,1024]{1,0:T(8,128)(2,1)S(1)}, u32[]{:S(2)}, u32[]{:S(2)}) collective-permute-start(bf16[256,1024]{1,0:T(8,128)(2,1)S(1)} %collective-permute-done.3.r2), channel_id=1, source_target_pairs={{0,1},{1,0},{2,3},{3,2},{4,5},{5,4},{6,7},{7,6},{8,9},{9,8},{10,11... | collective-permute-start | bytes 1572872 | tf_op jit(solution)/shard_map/ppermute | solution.py:511
  17.0 13.6 %collective-permute-start.2 = (bf16[256,1024]{1,0:T(8,128)(2,1)S(1)}, bf16[256,1024]{1,0:T(8,128)(2,1)S(1)}, u32[]{:S(2)}, u32[]{:S(2)}) collective-permute-start(bf16[256,1024]{1,0:T(8,128)(2,1)S(1)} %get-tuple-element.115), channel_id=1, source_target_pairs={{0,2},{1,3},{2,0},{3,1},{4,6},{5,7},{6,4},{7,5},{8,10},{9,11},{10,... | collective-permute-start | bytes 1572872 | tf_op jit(solution)/shard_map/ppermute | solution.py:511
  18.3 21.0 %collective-permute-start.1 = (bf16[512,1024]{1,0:T(8,128)(2,1)S(1)}, bf16[512,1024]{1,0:T(8,128)(2,1)S(1)}, u32[]{:S(2)}, u32[]{:S(2)}) collective-permute-start(bf16[512,1024]{1,0:T(8,128)(2,1)S(1)} %get-tuple-element.59), channel_id=1, source_target_pairs={{0,1},{1,0},{2,3},{3,2},{4,5},{5,4},{6,7},{7,6},{8,9},{9,8},{10,11... | collective-permute-start | bytes 3145736 | tf_op jit(solution)/shard_map/ppermute | solution.py:511
  21.9 8.7 %collective-permute-start.7 = (bf16[272,256]{1,0:T(8,128)(2,1)S(1)}, bf16[272,256]{1,0:T(8,128)(2,1)S(1)}, u32[]{:S(2)}, u32[]{:S(2)}) collective-permute-start(bf16[272,256]{1,0:T(8,128)(2,1)S(1)} %get-tuple-element.71.refs_1_), channel_id=1, source_target_pairs={{0,4},{4,8},{8,12},{12,0},{1,5},{5,9},{9,13},{13,1},{2,6},{6,10},{... | collective-permute-start | bytes 417800 | tf_op jit(solution)/shard_map/ppermute | solution.py:597
  23.3 11.8 %collective-permute-start.6 = (bf16[272,256]{1,0:T(8,128)(2,1)S(1)}, bf16[272,256]{1,0:T(8,128)(2,1)S(1)}, u32[]{:S(2)}, u32[]{:S(2)}) collective-permute-start(bf16[272,256]{1,0:T(8,128)(2,1)S(1)} %get-tuple-element.71.refs_1_), channel_id=1, source_target_pairs={{0,8},{4,12},{8,0},{12,4},{1,9},{5,13},{9,1},{13,5},{2,10},{6,14},... | collective-permute-start | bytes 417800 | tf_op jit(solution)/shard_map/ppermute | solution.py:597
  24.4 13.0 %collective-permute-start.5 = (bf16[272,256]{1,0:T(8,128)(2,1)S(1)}, bf16[272,256]{1,0:T(8,128)(2,1)S(1)}, u32[]{:S(2)}, u32[]{:S(2)}) collective-permute-start(bf16[272,256]{1,0:T(8,128)(2,1)S(1)} %get-tuple-element.71.refs_1_), channel_id=1, source_target_pairs={{0,12},{4,0},{8,4},{12,8},{1,13},{5,1},{9,5},{13,9},{2,14},{6,2},{... | collective-permute-start | bytes 417800 | tf_op jit(solution)/shard_map/ppermute | solution.py:597
  37.4 2.0 %collective-permute-start.8 = (bf16[256,1024]{1,0:T(8,128)(2,1)S(1)}, bf16[256,1024]{1,0:T(8,128)(2,1)S(1)}, u32[]{:S(2)}, u32[]{:S(2)}) collective-permute-start(bf16[256,1024]{1,0:T(8,128)(2,1)S(1)} %collective-permute-done.2.r2), channel_id=1, source_target_pairs={{0,1},{1,0},{2,3},{3,2},{4,5},{5,4},{6,7},{7,6},{8,9},{9,8},{10,11... | collective-permute-start | bytes 1572872 | tf_op jit(solution)/shard_map/ppermute | solution.py:511
  37.9 14.2 %collective-permute-start.12 = (bf16[256,1024]{1,0:T(8,128)(2,1)S(1)}, bf16[256,1024]{1,0:T(8,128)(2,1)S(1)}, u32[]{:S(2)}, u32[]{:S(2)}) collective-permute-start(bf16[256,1024]{1,0:T(8,128)(2,1)S(1)} %get-tuple-element.93), channel_id=1, source_target_pairs={{0,3},{1,2},{2,1},{3,0},{4,7},{5,6},{6,5},{7,4},{8,11},{9,10},{10,... | collective-permute-start | bytes 1572872 | tf_op jit(solution)/shard_map/ppermute | solution.py:511
  38.1 24.3 %collective-permute-start.14 = (bf16[256,1024]{1,0:T(8,128)(2,1)S(1)}, bf16[256,1024]{1,0:T(8,128)(2,1)S(1)}, u32[]{:S(2)}, u32[]{:S(2)}) collective-permute-start(bf16[256,1024]{1,0:T(8,128)(2,1)S(1)} %get-tuple-element.101), channel_id=1, source_target_pairs={{0,2},{1,3},{2,0},{3,1},{4,6},{5,7},{6,4},{7,5},{8,10},{9,11},{10,... | collective-permute-start | bytes 1572872 | tf_op jit(solution)/shard_map/ppermute | solution.py:511
  41.3 12.6 %copy-start.6 = (s32[1,512]{1,0:T(1,128)S(1)}, s32[1,512]{1,0:T(1,128)}, u32[]{:S(2)}) copy-start(s32[1,512]{1,0:T(1,128)} %order.1) | copy-start | bytes 6148
  41.3 12.1 %collective-permute-start.10 = (bf16[272,256]{1,0:T(8,128)(2,1)S(1)}, bf16[272,256]{1,0:T(8,128)(2,1)S(1)}, u32[]{:S(2)}, u32[]{:S(2)}) collective-permute-start(bf16[272,256]{1,0:T(8,128)(2,1)S(1)} %get-tuple-element.92), channel_id=1, source_target_pairs={{0,8},{4,12},{8,0},{12,4},{1,9},{5,13},{9,1},{13,5},{2,10},{6,14},... | collective-permute-start | bytes 417800 | tf_op jit(solution)/shard_map/ppermute | solution.py:597
  42.7 10.7 %collective-permute-start.11 = (bf16[272,256]{1,0:T(8,128)(2,1)S(1)}, bf16[272,256]{1,0:T(8,128)(2,1)S(1)}, u32[]{:S(2)}, u32[]{:S(2)}) collective-permute-start(bf16[272,256]{1,0:T(8,128)(2,1)S(1)} %get-tuple-element.92), channel_id=1, source_target_pairs={{0,12},{4,0},{8,4},{12,8},{1,13},{5,1},{9,5},{13,9},{2,14},{6,2},{... | collective-permute-start | bytes 417800 | tf_op jit(solution)/shard_map/ppermute | solution.py:597
  42.7 11.2 %collective-permute-start.9 = (bf16[272,256]{1,0:T(8,128)(2,1)S(1)}, bf16[272,256]{1,0:T(8,128)(2,1)S(1)}, u32[]{:S(2)}, u32[]{:S(2)}) collective-permute-start(bf16[272,256]{1,0:T(8,128)(2,1)S(1)} %get-tuple-element.92), channel_id=1, source_target_pairs={{0,4},{4,8},{8,12},{12,0},{1,5},{5,9},{9,13},{13,1},{2,6},{6,10},{... | collective-permute-start | bytes 417800 | tf_op jit(solution)/shard_map/ppermute | solution.py:597
  49.1 18.3 %copy-start.2 = (bf16[512,1024]{1,0:T(8,128)(2,1)S(1)}, bf16[512,1024]{1,0:T(8,128)(2,1)}, u32[]{:S(2)}) copy-start(bf16[512,1024]{1,0:T(8,128)(2,1)} %own.1) | copy-start | bytes 3145732
  52.1 13.8 %collective-permute-start.15 = (bf16[256,1024]{1,0:T(8,128)(2,1)S(1)}, bf16[256,1024]{1,0:T(8,128)(2,1)S(1)}, u32[]{:S(2)}, u32[]{:S(2)}) collective-permute-start(bf16[256,1024]{1,0:T(8,128)(2,1)S(1)} %collective-permute-done.12.refs_2_), channel_id=1, source_target_pairs={{0,16},{16,0},{1,17},{17,1},{2,18},{18,2},{3,19},{19,3},{4,20},{20... | collective-permute-start | bytes 1572872 | tf_op jit(solution)/shard_map/ppermute | solution.py:515
  57.7 18.2 %copy-start.10 = (bf16[1024]{0:T(1024)(128)(2,1)S(1)}, bf16[1024]{0:T(1024)(128)(2,1)}, u32[]{:S(2)}) copy-start(bf16[1024]{0:T(1024)(128)(2,1)} %param.22) | copy-start | bytes 6148
  57.7 18.2 %copy-start.11 = (bf16[1024]{0:T(1024)(128)(2,1)S(1)}, bf16[1024]{0:T(1024)(128)(2,1)}, u32[]{:S(2)}) copy-start(bf16[1024]{0:T(1024)(128)(2,1)} %param.23) | copy-start | bytes 6148
  57.7 9.7 %collective-permute-start.13 = (bf16[512,512]{1,0:T(8,128)(2,1)S(1)}, bf16[512,512]{1,0:T(8,128)(2,1)S(1)}, u32[]{:S(2)}, u32[]{:S(2)}) collective-permute-start(bf16[512,512]{1,0:T(8,128)(2,1)S(1)} %get-tuple-element.96.h0), channel_id=1, source_target_pairs={{0,1},{1,0},{2,3},{3,2},{4,5},{5,4},{6,7},{7,6},{8,9},{9,8},{10,11... | collective-permute-start | bytes 1572872 | tf_op jit(solution)/shard_map/ppermute | solution.py:511
  58.3 11.0 %collective-permute-start.19 = (bf16[256,512]{1,0:T(8,128)(2,1)S(1)}, bf16[256,512]{1,0:T(8,128)(2,1)S(1)}, u32[]{:S(2)}, u32[]{:S(2)}) collective-permute-start(bf16[256,512]{1,0:T(8,128)(2,1)S(1)} %get-tuple-element.106), channel_id=1, source_target_pairs={{0,2},{1,3},{2,0},{3,1},{4,6},{5,7},{6,4},{7,5},{8,10},{9,11},{10,... | collective-permute-start | bytes 786440 | tf_op jit(solution)/shard_map/ppermute | solution.py:511
  65.9 13.3 %collective-permute-start.18 = (bf16[256,1024]{1,0:T(8,128)(2,1)S(1)}, bf16[256,1024]{1,0:T(8,128)(2,1)S(1)}, u32[]{:S(2)}, u32[]{:S(2)}) collective-permute-start(bf16[256,1024]{1,0:T(8,128)(2,1)S(1)} %collective-permute-done.14.refs_0_), channel_id=1, source_target_pairs={{0,16},{16,0},{1,17},{17,1},{2,18},{18,2},{3,19},{19,3},{4,20},{20... | collective-permute-start | bytes 1572872 | tf_op jit(solution)/shard_map/ppermute | solution.py:515
  67.2 7.4 %collective-permute-start.16 = (bf16[256,512]{1,0:T(8,128)(2,1)S(1)}, bf16[256,512]{1,0:T(8,128)(2,1)S(1)}, u32[]{:S(2)}, u32[]{:S(2)}) collective-permute-start(bf16[256,512]{1,0:T(8,128)(2,1)S(1)} %get-tuple-element.103), channel_id=1, source_target_pairs={{0,2},{1,3},{2,0},{3,1},{4,6},{5,7},{6,4},{7,5},{8,10},{9,11},{10,... | collective-permute-start | bytes 786440 | tf_op jit(solution)/shard_map/ppermute | solution.py:511
  69.3 6.6 %collective-permute-start.20 = (bf16[256,512]{1,0:T(8,128)(2,1)S(1)}, bf16[256,512]{1,0:T(8,128)(2,1)S(1)}, u32[]{:S(2)}, u32[]{:S(2)}) collective-permute-start(bf16[256,512]{1,0:T(8,128)(2,1)S(1)} %collective-permute-done.19.h2), channel_id=1, source_target_pairs={{0,1},{1,0},{2,3},{3,2},{4,5},{5,4},{6,7},{7,6},{8,9},{9,8},{10,11... | collective-permute-start | bytes 786440 | tf_op jit(solution)/shard_map/ppermute | solution.py:511
  74.5 9.4 %collective-permute-start.17 = (bf16[256,512]{1,0:T(8,128)(2,1)S(1)}, bf16[256,512]{1,0:T(8,128)(2,1)S(1)}, u32[]{:S(2)}, u32[]{:S(2)}) collective-permute-start(bf16[256,512]{1,0:T(8,128)(2,1)S(1)} %collective-permute-done.16.h2), channel_id=1, source_target_pairs={{0,1},{1,0},{2,3},{3,2},{4,5},{5,4},{6,7},{7,6},{8,9},{9,8},{10,11... | collective-permute-start | bytes 786440 | tf_op jit(solution)/shard_map/ppermute | solution.py:511
  81.3 5.3 %collective-permute-start.21 = (f32[2,256]{1,0:T(2,128)S(1)}, f32[2,256]{1,0:T(2,128)S(1)}, u32[]{:S(2)}, u32[]{:S(2)}) collective-permute-start(f32[2,256]{1,0:T(2,128)S(1)} %get-tuple-element.112), channel_id=1, source_target_pairs={{0,1},{1,0},{2,3},{3,2},{4,5},{5,4},{6,7},{7,6},{8,9},{9,8},{10,11... | collective-permute-start | bytes 6152 | tf_op jit(solution)/shard_map/ppermute | solution.py:511
  82.3 5.9 %collective-permute-start.22 = (f32[2,256]{1,0:T(2,128)S(1)}, f32[2,256]{1,0:T(2,128)S(1)}, u32[]{:S(2)}, u32[]{:S(2)}) collective-permute-start(f32[2,256]{1,0:T(2,128)S(1)} %get-tuple-element.112), channel_id=1, source_target_pairs={{0,2},{1,3},{2,0},{3,1},{4,6},{5,7},{6,4},{7,5},{8,10},{9,11},{10,... | collective-permute-start | bytes 6152 | tf_op jit(solution)/shard_map/ppermute | solution.py:511
  82.6 5.6 %collective-permute-start.23 = (f32[2,256]{1,0:T(2,128)S(1)}, f32[2,256]{1,0:T(2,128)S(1)}, u32[]{:S(2)}, u32[]{:S(2)}) collective-permute-start(f32[2,256]{1,0:T(2,128)S(1)} %get-tuple-element.112), channel_id=1, source_target_pairs={{0,3},{1,2},{2,1},{3,0},{4,7},{5,6},{6,5},{7,4},{8,11},{9,10},{10,... | collective-permute-start | bytes 6152 | tf_op jit(solution)/shard_map/ppermute | solution.py:511
  86.0 2.2 %collective-permute-start.24 = (f32[2,256]{1,0:T(2,128)S(1)}, f32[2,256]{1,0:T(2,128)S(1)}, u32[]{:S(2)}, u32[]{:S(2)}) collective-permute-start(f32[2,256]{1,0:T(2,128)S(1)} %get-tuple-element.113), channel_id=1, source_target_pairs={{0,1},{1,0},{2,3},{3,2},{4,5},{5,4},{6,7},{7,6},{8,9},{9,8},{10,11... | collective-permute-start | bytes 6152 | tf_op jit(solution)/shard_map/ppermute | solution.py:511
  86.3 2.4 %collective-permute-start.25 = (f32[2,256]{1,0:T(2,128)S(1)}, f32[2,256]{1,0:T(2,128)S(1)}, u32[]{:S(2)}, u32[]{:S(2)}) collective-permute-start(f32[2,256]{1,0:T(2,128)S(1)} %get-tuple-element.113), channel_id=1, source_target_pairs={{0,2},{1,3},{2,0},{3,1},{4,6},{5,7},{6,4},{7,5},{8,10},{9,11},{10,... | collective-permute-start | bytes 6152 | tf_op jit(solution)/shard_map/ppermute | solution.py:511
  86.6 3.2 %collective-permute-start.26 = (f32[2,256]{1,0:T(2,128)S(1)}, f32[2,256]{1,0:T(2,128)S(1)}, u32[]{:S(2)}, u32[]{:S(2)}) collective-permute-start(f32[2,256]{1,0:T(2,128)S(1)} %get-tuple-element.113), channel_id=1, source_target_pairs={{0,3},{1,2},{2,1},{3,0},{4,7},{5,6},{6,5},{7,4},{8,11},{9,10},{10,... | collective-permute-start | bytes 6152 | tf_op jit(solution)/shard_map/ppermute | solution.py:511

commit v4 on v3

--- a/solution.py
+++ b/solution.py
@@ -448,62 +448,69 @@
     )(order, own, h0, h1, w0, w1)
 
 
-def finish_kernel(own, kept, h2, h3, gain, head, *refs):
-    (w2, other2, w3, other3), (hidden_out, sums) = refs[:4], refs[-2:]
-    half = w2.shape[0]
-    mine = pl.ds(pl.multiple_of(own[1] * half, half), half)
-    others = pl.ds(pl.multiple_of((1 - own[1]) * half, half), half)
-    total = kept[...]
-    for h, columns, weight in ((h2, mine, w2), (h3, mine, w3), (h2, others, other2), (h3, others, other3)):
-        total += jnp.dot(h[:, columns], weight[...], preferred_element_type=jnp.float32)
-    hidden = total.astype(jnp.bfloat16)
-    hidden_out[...] = hidden
-    x = hidden.astype(jnp.float32)
-    weighted = x * (gain[...] * head[...])
-    squared = x * x
-    for i, terms in enumerate((squared, weighted)):
-        lanes = functools.reduce(
-            jnp.add, [terms[:, j : j + 128] for j in range(0, terms.shape[1], 128)]
-        )
-        sums[i : i + 1, :] = jnp.sum(lanes.T, 0, keepdims=True)
-
-
-def finish(own, kept, h2, h3, gain, head, weights, token, part, hidden):
+def shares(own, h):
+    half = h.shape[1] // 2
+    return tuple(pl.ds(pl.multiple_of(share * half, half), half) for share in (own[1], 1 - own[1]))
+
+
+def gather_kernel(own, kept, *refs):
+    *heads, w2, w3, other3, out = refs
+    rows = heads[0].shape[0]
+    for j in range(N_PART):
+        span = slice(j * rows, (j + 1) * rows)
+        h2, h3 = heads[j], heads[N_PART + j]
+        mine, others = shares(own, h2)
+        total = kept[span, :]
+        for h, columns, weight in ((h2, mine, w2), (h3, mine, w3), (h3, others, other3)):
+            total += jnp.dot(h[:, columns], weight[...], preferred_element_type=jnp.float32)
+        out[span, :] = total
+
+
+def gather(own, kept, heads2, heads3, w2, w3, other3):
     rows, width = kept.shape
-    step, depth = h2.shape
-    specs = [
-        pl.BlockSpec(memory_space=pltpu.SMEM),
-        pl.BlockSpec((step, width), lambda i: (part, 0)),
-        pl.BlockSpec((step, depth), lambda i: (0, 0)),
-        pl.BlockSpec((step, depth), lambda i: (0, 0)),
-        pl.BlockSpec((1, width), lambda i: (0, 0)),
-        pl.BlockSpec((1, width), lambda i: (0, 0)),
-        *(pl.BlockSpec(w.shape, lambda i: (0, 0)) for w in weights),
-    ]
-    specs.append(far_memory())
-    args = [own, kept, h2, h3, gain, head, *weights, token]
-    aliases = {}
-    if hidden is not None:
-        aliases = {len(args): 0}
-        specs.append(pl.BlockSpec(memory_space=pl.ANY))
-        args.append(hidden)
+    depth = heads2[0].shape[1]
+    return pl.pallas_call(
+        gather_kernel,
+        out_shape=jax.ShapeDtypeStruct((rows, width), jnp.float32),
+        in_specs=[pl.BlockSpec(memory_space=pltpu.SMEM)] + [whole()] * (4 + 2 * N_PART),
+        out_specs=whole(),
+        compiler_params=params(14),
+        cost_estimate=cost(3 * rows * depth * width, 8 * rows * width),
+        name="gather",
+    )(own, kept, *heads2, *heads3, w2, w3, other3)
+
+
+def finish_kernel(own, most, *refs):
+    *heads, other2, gain, head, hidden_out, sums = refs
+    rows = heads[0].shape[0]
+    weight = gain[...].astype(jnp.float32) * head[...].astype(jnp.float32)
+    for j, h in enumerate(heads):
+        span = slice(j * rows, (j + 1) * rows)
+        _, others = shares(own, h)
+        total = most[span, :] + jnp.dot(h[:, others], other2[...], preferred_element_type=jnp.float32)
+        hidden = total.astype(jnp.bfloat16)
+        hidden_out[span, :] = hidden
+        x = hidden.astype(jnp.float32)
+        for i, terms in enumerate((x * x, x * weight)):
+            lanes = functools.reduce(jnp.add, [terms[:, k : k + 128] for k in range(0, terms.shape[1], 128)])
+            sums[i : i + 1, span] = jnp.sum(lanes.T, 0, keepdims=True)
+
+
+def finish(own, most, heads2, other2, gain, head):
+    rows, width = most.shape
+    depth = heads2[0].shape[1]
     return pl.pallas_call(
         finish_kernel,
-        grid=(1,),
-        in_specs=specs,
-        out_specs=(
-            pl.BlockSpec((step, width), lambda i: (part, 0)),
-            pl.BlockSpec((2, step), lambda i: (0, 0)),
-        ),
         out_shape=(
             jax.ShapeDtypeStruct((rows, width), jnp.bfloat16),
-            jax.ShapeDtypeStruct((2, step), jnp.float32),
+            jax.ShapeDtypeStruct((2, rows), jnp.float32),
         ),
-        input_output_aliases=aliases,
+        in_specs=[pl.BlockSpec(memory_space=pltpu.SMEM)] + [whole()] * (4 + N_PART),
+        out_specs=(whole(), whole()),
         compiler_params=params(14),
-        cost_estimate=cost(4 * step * depth * width, 8 * step * width),
+        cost_estimate=cost(rows * depth * width, 8 * rows * width),
         name="finish",
-    )(*args)
+    )(own, most, *heads2, other2, gain, head)
 
 
 def flip(x, bit):
@@ -612,24 +619,20 @@
         order,
     )
     heads2 = [flip(parts[0], 2)]
-    rest, far2, other3 = lax.optimization_barrier((parts[1], far2, other3))
+    rest, far2 = lax.optimization_barrier((parts[1], far2))
     heads2.append(flip(rest, 2))
     other2 = swap_parts(far2)
-    weights = (far2, other2, far3, other3)
     heads_other = flip(heads, 1)
+    heads_other, other3 = lax.optimization_barrier((heads_other, other3))
     kept, token = keep(order, hidden_in, heads, heads_other, near, near_other)
     heads2[0], token = lax.optimization_barrier((heads2[0], token))
     heads3 = [flip(x, 1) for x in heads2]
-    final = final_gain.astype(jnp.float32).reshape(1, width)
-    head = value_head.astype(jnp.float32).reshape(1, width)
-    hidden, values = None, []
-    for j in range(N_PART):
-        hidden, sums = finish(
-            t_own, kept, heads2[j], heads3[j], final, head, weights, token, j, hidden
-        )
-        square, product = sums + flip(sums, 1) + (flip(sums, 2) + flip(sums, 3))
-        values.append(product * lax.rsqrt(square / MODEL_WIDTH + NORM_EPS))
-    return hidden, jnp.concatenate(values)
+    most = gather(t_own, kept, heads2, heads3, far2, far3, other3)
+    hidden, sums = finish(
+        t_own, most, heads2, other2, final_gain.reshape(1, width), value_head.reshape(1, width)
+    )
+    square, product = sums + flip(sums, 1) + (flip(sums, 2) + flip(sums, 3))
+    return hidden, product * lax.rsqrt(square / MODEL_WIDTH + NORM_EPS)
 
 
 def solution(mesh):

time: 90.7 us -> 86.9 us (0.958)
  waiting for transfers between devices: 31.7 us -> 27.7 us
  Pallas kernels: 25.2 us -> 24.1 us
  starting transfers between devices: 23.8 us -> 24.9 us
    ppermute x2, waiting for transfers between devices: 6.87 us -> 0.01 us  [swap_parts(): return lax.ppermute(x, 'parts', [(0, 1), (1, 0)])]
    ppermute x19 -> x16, waiting for transfers between devices: 17.5 us -> 20.4 us  [flip(): return lax.ppermute(x, 'tensor', [(i, i ^ bit) for i in range(count)])]
    ppermute x19 -> x16, starting transfers between devices: 14.6 us -> 15.7 us  [flip(): return lax.ppermute(x, 'tensor', [(i, i ^ bit) for i in range(count)])]
  transfers between devices with their start and end apart: 27 -> 24, of which waited for: 12 -> 12; matrix products, arithmetic and copies ran while one was open for 2% -> 2% of each run, Pallas kernels for 28% -> 25%
where the time goes in v4:
time: 86.9 us; the launch traced here: 86.6 us
  waiting for transfers between devices  27.7 us (32%)
  starting transfers between devices  24.9 us (29%)
  Pallas kernels  24.1 us (28%)
  local copies, waits for them, and re-layouts  8.24 us (9%)
    ppermute x16, waiting for transfers between devices, flip(): return lax.ppermute(x, 'tensor', [(i, i ^ bit) for i in range(count)])  20.4 us
    ppermute x16, starting transfers between devices, flip(): return lax.ppermute(x, 'tensor', [(i, i ^ bit) for i in range(count)])  15.7 us
    ppermute x6, waiting for transfers between devices, on_device(): lax.ppermute(kv, 'dp', [(i, (i + d) % n_dp) for i in range(n_dp)])  7.36 us
    ppermute x6, starting transfers between devices, on_device(): lax.ppermute(kv, 'dp', [(i, (i + d) % n_dp) for i in range(n_dp)])  6.71 us
    unnamed x24, local copies, waits for them, and re-layouts  6.25 us
    pallas_call x1, Pallas kernels, attend(): pl.pallas_call(functools.partial(attend_kernel, (), False), out_shape=(ru...  4.95 us
    pallas_call x1, Pallas kernels, early(): pl.pallas_call(early_kernel, out_shape=(jax.ShapeDtypeStruct((rows, colum...  4.23 us
    pallas_call x2, Pallas kernels, late(): pl.pallas_call(functools.partial(late_kernel, at, tuple(pieces)), out_sha...  3.68 us
  transfers between devices with their start and end apart: 24, of which 12 were waited for; matrix products, arithmetic and copies ran while one was open for 2% of the time, Pallas kernels for 25%

profile of v4, /device:TPU:9, one launch (start us, length us, event | category | flops | bytes accessed | tf_op | source)
XLA Modules:
  0.0 86.6 jit_solution(18313774617570501785)
XLA Ops:
  0.6 0.7 collective-permute-start
  1.4 1.3 %fusion.3 = (bf16[256,1024]{1,0:T(8,128)(2,1)S(1)}, bf16[256,1024]{1,0:T(8,128)(2,1)S(1)}) fusion(bf16[512,1024]{1,0:T(8,128)(2,1)} %own.1), kind=kLoop, calls=%fused_computation.6 | loop fusion | bytes 2097152 | tf_op jit(solution)/shard_map/slice | solution.py:551
  2.6 1.3 %collective-permute-start.3 = (bf16[256,1024]{1,0:T(8,128)(2,1)S(1)}, bf16[256,1024]{1,0:T(8,128)(2,1)S(1)}, u32[]{:S(2)}, u32[]{:S(2)}) collective-permute-start(bf16[256,1024]{1,0:T(8,128)(2,1)S(1)} %get-tuple-element.106), channel_id=1, source_target_pairs={{0,2},{1,3},{2,0},{3,1},{4,6},{5,7},{6,4},{7,5},{8,10},{9,11},{10,... | collective-permute-start | bytes 1572872 | tf_op jit(solution)/shard_map/ppermute | solution.py:518
  3.9 0.7 reshape.25.gain
  4.6 0.1 pad_add_fusion.own
  4.7 1.4 %copy-done.1 = bf16[512,1024]{1,0:T(8,128)(2,1)S(1)} copy-done((bf16[512,1024]{1,0:T(8,128)(2,1)S(1)}, bf16[512,1024]{1,0:T(8,128)(2,1)}, u32[]{:S(2)}) %copy-start.1) | copy-done | bytes 1048600
  6.1 2.4 %copy-done.3 = bf16[4096,512]{1,0:T(8,128)(2,1)S(1)} copy-done((bf16[4096,512]{1,0:T(8,128)(2,1)S(1)}, bf16[4096,512]{1,0:T(8,128)(2,1)}, u32[]{:S(2)}) %copy-start.3) | copy-done | bytes 4194328
  8.5 1.2 %copy-done.4 = bf16[4096,128]{1,0:T(8,128)(2,1)S(1)} copy-done((bf16[4096,128]{1,0:T(8,128)(2,1)S(1)}, bf16[4096,128]{1,0:T(8,128)(2,1)}, u32[]{:S(2)}) %copy-start.4) | copy-done | bytes 1048600
  9.7 1.2 %copy-done.5 = bf16[4096,128]{1,0:T(8,128)(2,1)S(1)} copy-done((bf16[4096,128]{1,0:T(8,128)(2,1)S(1)}, bf16[4096,128]{1,0:T(8,128)(2,1)}, u32[]{:S(2)}) %copy-start.5) | copy-done | bytes 1048600
  10.9 4.2 %early.1 = (f32[512,768]{1,0:T(8,128)S(1)}, f32[512,1]{1,0:T(8,128)S(1)}, bf16[2,1024,768]{2,1,0:T(8,128)(2,1)S(1)}, f32[8,128]{1,0:T(8,128)S(1)}) custom-call(s32[3]{0:T(128)S(1)} %pad_add_fusion.own, bf16[512,1024]{1,0:T(8,128)(2,1)S(1)} %copy-done.1, bf16[512,1024]{1,0:T(8,128)(2,1)S(1)} %collective-permute-done.r1, bf16[1,4096]{1,0:T(2,128)(2,1)S(1)} %reshape.25.gain, ...), custom_call_target="tpu_custom_call" | custom-call | flops 1610612736 | bytes 6291456 | tf_op jit(solution)/shard_map/early/pallas_call | solution.py:144
  15.2 0.0 copy-start.7
  15.2 0.0 copy-start.8
  15.2 0.0 copy-start.9
  15.2 1.0 %columns.1 = (bf16[512,1024]{1,0:T(8,128)(2,1)S(1)}, bf16[512,1024]{1,0:T(8,128)(2,1)S(1)}, bf16[256,1024]{1,0:T(8,128)(2,1)S(1)}, bf16[256,1024]{1,0:T(8,128)(2,1)S(1)}, f32[8,128]{1,0:T(8,128)S(1)}) custom-call(s32[3]{0:T(128)S(1)} %pad_add_fusion.own, bf16[512,4096]{1,0:T(8,128)(2,1)S(1)} %copy-done, f32[8,128]{1,0:T(8,128)S(1)} %get-tuple-element.54.token_in), custom_call_target="tpu_custom_call" | custom-call | flops 1 | bytes 8388608 | tf_op jit(solution)/shard_map/columns/pallas_call | solution.py:418
  16.2 0.1 collective-permute-done.3.r2
  16.2 0.8 collective-permute-start.4
  17.0 1.2 %collective-permute-start.2 = (bf16[256,1024]{1,0:T(8,128)(2,1)S(1)}, bf16[256,1024]{1,0:T(8,128)(2,1)S(1)}, u32[]{:S(2)}, u32[]{:S(2)}) collective-permute-start(bf16[256,1024]{1,0:T(8,128)(2,1)S(1)} %get-tuple-element.107), channel_id=1, source_target_pairs={{0,2},{1,3},{2,0},{3,1},{4,6},{5,7},{6,4},{7,5},{8,10},{9,11},{10,... | collective-permute-start | bytes 1572872 | tf_op jit(solution)/shard_map/ppermute | solution.py:518
  18.3 0.3 collective-permute-start.1
  18.5 1.6 %prep.1 = (bf16[16,512]{1,0:T(8,128)(2,1)S(1)}, f32[512,128]{1,0:T(8,128)S(1)}, f32[512,128]{1,0:T(8,128)S(1)}) custom-call(s32[1,4]{1,0:T(1,128)S(1)} %copy-done.9, s32[4,128]{1,0:T(4,128)S(1)} %bitcast.6, s32[4,128]{1,0:T(4,128)S(1)} %bitcast.7), custom_call_target="tpu_custom_call" | custom-call | flops 2000000000 | bytes 40000000 | tf_op jit(solution)/shard_map/prep/pallas_call | solution.py:80
  20.1 0.0 collective-permute-done.4.r3
  20.1 1.8 %late.2 = (bf16[4,256,128]{2,1,0:T(8,128)(2,1)S(1)}, bf16[272,256]{1,0:T(8,128)(2,1)S(1)}, f32[8,128]{1,0:T(8,128)S(1)}) custom-call(s32[3]{0:T(128)S(1)} %pad_add_fusion.own, f32[8,128]{1,0:T(8,128)S(1)} %get-tuple-element.57.before, f32[512,768]{1,0:T(8,128)S(1)} %get-tuple-element.58.acc, f32[512,1]{1,0:T(8,128)S(1)} %get-tuple-element.59.squares, ...), custom_call_target="tpu_custom_call" | custom-call | flops 805306368 | bytes 3145728 | tf_op jit(solution)/shard_map/late/pallas_call | solution.py:235
  21.9 1.3 %collective-permute-start.7 = (bf16[272,256]{1,0:T(8,128)(2,1)S(1)}, bf16[272,256]{1,0:T(8,128)(2,1)S(1)}, u32[]{:S(2)}, u32[]{:S(2)}) collective-permute-start(bf16[272,256]{1,0:T(8,128)(2,1)S(1)} %get-tuple-element.67.refs_1_), channel_id=1, source_target_pairs={{0,4},{4,8},{8,12},{12,0},{1,5},{5,9},{9,13},{13,1},{2,6},{6,10},{... | collective-permute-start | bytes 417800 | tf_op jit(solution)/shard_map/ppermute | solution.py:604
  23.3 1.1 %collective-permute-start.6 = (bf16[272,256]{1,0:T(8,128)(2,1)S(1)}, bf16[272,256]{1,0:T(8,128)(2,1)S(1)}, u32[]{:S(2)}, u32[]{:S(2)}) collective-permute-start(bf16[272,256]{1,0:T(8,128)(2,1)S(1)} %get-tuple-element.67.refs_1_), channel_id=1, source_target_pairs={{0,8},{4,12},{8,0},{12,4},{1,9},{5,13},{9,1},{13,5},{2,10},{6,14},... | collective-permute-start | bytes 417800 | tf_op jit(solution)/shard_map/ppermute | solution.py:604
  24.4 1.4 %collective-permute-start.5 = (bf16[272,256]{1,0:T(8,128)(2,1)S(1)}, bf16[272,256]{1,0:T(8,128)(2,1)S(1)}, u32[]{:S(2)}, u32[]{:S(2)}) collective-permute-start(bf16[272,256]{1,0:T(8,128)(2,1)S(1)} %get-tuple-element.67.refs_1_), channel_id=1, source_target_pairs={{0,12},{4,0},{8,4},{12,8},{1,13},{5,1},{9,5},{13,9},{2,14},{6,2},{... | collective-permute-start | bytes 417800 | tf_op jit(solution)/shard_map/ppermute | solution.py:604
  25.8 4.8 %collective-permute-done.2.r2 = bf16[256,1024]{1,0:T(8,128)(2,1)S(1)} collective-permute-done((bf16[256,1024]{1,0:T(8,128)(2,1)S(1)}, bf16[256,1024]{1,0:T(8,128)(2,1)S(1)}, u32[]{:S(2)}, u32[]{:S(2)}) %collective-permute-start.2) | collective-permute-done | bytes 524320 | tf_op jit(solution)/shard_map/ppermute | solution.py:518
  30.6 4.5 %collective-permute-done.6.refs_3_ = bf16[272,256]{1,0:T(8,128)(2,1)S(1)} collective-permute-done((bf16[272,256]{1,0:T(8,128)(2,1)S(1)}, bf16[272,256]{1,0:T(8,128)(2,1)S(1)}, u32[]{:S(2)}, u32[]{:S(2)}) %collective-permute-start.6) | collective-permute-done | bytes 139296 | tf_op jit(solution)/shard_map/ppermute | solution.py:604
  35.1 2.3 %collective-permute-done.5.refs_4_ = bf16[272,256]{1,0:T(8,128)(2,1)S(1)} collective-permute-done((bf16[272,256]{1,0:T(8,128)(2,1)S(1)}, bf16[272,256]{1,0:T(8,128)(2,1)S(1)}, u32[]{:S(2)}, u32[]{:S(2)}) %collective-permute-start.5) | collective-permute-done | bytes 139296 | tf_op jit(solution)/shard_map/ppermute | solution.py:604
  37.4 0.5 collective-permute-start.8
  37.9 0.2 collective-permute-start.12
  38.1 1.2 %collective-permute-start.16 = (bf16[256,1024]{1,0:T(8,128)(2,1)S(1)}, bf16[256,1024]{1,0:T(8,128)(2,1)S(1)}, u32[]{:S(2)}, u32[]{:S(2)}) collective-permute-start(bf16[256,1024]{1,0:T(8,128)(2,1)S(1)} %get-tuple-element.100), channel_id=1, source_target_pairs={{0,2},{1,3},{2,0},{3,1},{4,6},{5,7},{6,4},{7,5},{8,10},{9,11},{10,... | collective-permute-start | bytes 1572872 | tf_op jit(solution)/shard_map/ppermute | solution.py:518
  39.3 0.0 collective-permute-done.1.w1
  39.3 0.2 collective-permute-done.8.r3
  39.4 1.9 %late.3 = (bf16[4,512,128]{2,1,0:T(8,128)(2,1)S(1)}, bf16[272,256]{1,0:T(8,128)(2,1)S(1)}, bf16[1280,256]{1,0:T(8,128)(2,1)S(1)}, s32[10,128]{1,0:T(8,128)S(1)}, f32[8,128]{1,0:T(8,128)}) custom-call(s32[3]{0:T(128)S(1)} %pad_add_fusion.own, f32[8,128]{1,0:T(8,128)S(1)} %get-tuple-element.76.before, f32[512,768]{1,0:T(8,128)S(1)} %get-tuple-element.58.acc, ...), custom_call_target="tpu_custom_call" | custom-call | flops 805306368 | bytes 3145728 | tf_op jit(solution)/shard_map/late/pallas_call | solution.py:235
  41.3 0.0 copy-start.6
  41.3 1.4 %collective-permute-start.10 = (bf16[272,256]{1,0:T(8,128)(2,1)S(1)}, bf16[272,256]{1,0:T(8,128)(2,1)S(1)}, u32[]{:S(2)}, u32[]{:S(2)}) collective-permute-start(bf16[272,256]{1,0:T(8,128)(2,1)S(1)} %get-tuple-element.88), channel_id=1, source_target_pairs={{0,8},{4,12},{8,0},{12,4},{1,9},{5,13},{9,1},{13,5},{2,10},{6,14},... | collective-permute-start | bytes 417800 | tf_op jit(solution)/shard_map/ppermute | solution.py:604
  42.7 0.0 collective-permute-start.11
  42.7 1.5 %collective-permute-start.9 = (bf16[272,256]{1,0:T(8,128)(2,1)S(1)}, bf16[272,256]{1,0:T(8,128)(2,1)S(1)}, u32[]{:S(2)}, u32[]{:S(2)}) collective-permute-start(bf16[272,256]{1,0:T(8,128)(2,1)S(1)} %get-tuple-element.88), channel_id=1, source_target_pairs={{0,4},{4,8},{8,12},{12,0},{1,5},{5,9},{9,13},{13,1},{2,6},{6,10},{... | collective-permute-start | bytes 417800 | tf_op jit(solution)/shard_map/ppermute | solution.py:604
  44.2 4.9 %attend.1 = (f32[2048,128]{1,0:T(8,128)S(1)}, f32[2048,128]{1,0:T(8,128)S(1)}, f32[2048,128]{1,0:T(8,128)S(1)}, f32[8,128]{1,0:T(8,128)S(1)}) custom-call(s32[3]{0:T(128)S(1)} %pad_add_fusion.own, bf16[4,512,128]{2,1,0:T(8,128)(2,1)S(1)} %get-tuple-element.82.q_all, bf16[1280,256]{1,0:T(8,128)(2,1)S(1)} %get-tuple-element.83.refs_0_, ...), custom_call_target="tpu_custom_call" | custom-call | flops 1342177280 | bytes 1048576 | tf_op jit(solution)/shard_map/attend/pallas_call | solution.py:356
  49.2 0.0 copy-start.10
  49.2 0.0 copy-start.11
  49.2 0.0 copy-start.2
  49.2 2.9 %collective-permute-done.12.refs_5_ = bf16[256,1024]{1,0:T(8,128)(2,1)S(1)} collective-permute-done((bf16[256,1024]{1,0:T(8,128)(2,1)S(1)}, bf16[256,1024]{1,0:T(8,128)(2,1)S(1)}, u32[]{:S(2)}, u32[]{:S(2)}) %collective-permute-start.12) | collective-permute-done | bytes 524320 | tf_op jit(solution)/shard_map/ppermute | solution.py:518
  52.1 1.2 %collective-permute-start.14 = (bf16[256,1024]{1,0:T(8,128)(2,1)S(1)}, bf16[256,1024]{1,0:T(8,128)(2,1)S(1)}, u32[]{:S(2)}, u32[]{:S(2)}) collective-permute-start(bf16[256,1024]{1,0:T(8,128)(2,1)S(1)} %collective-permute-done.12.refs_5_), channel_id=1, source_target_pairs={{0,16},{16,0},{1,17},{17,1},{2,18},{18,2},{3,19},{19,3},{4,20},{20... | collective-permute-start | bytes 1572872 | tf_op jit(solution)/shard_map/ppermute | solution.py:522
  53.4 0.6 collective-permute-done.9.refs_4_
  53.9 3.3 %attend_rest.1 = (bf16[512,512]{1,0:T(8,128)(2,1)S(1)}, bf16[256,512]{1,0:T(8,128)(2,1)S(1)}, bf16[256,512]{1,0:T(8,128)(2,1)S(1)}) custom-call(s32[3]{0:T(128)S(1)} %pad_add_fusion.own, bf16[4,512,128]{2,1,0:T(8,128)(2,1)S(1)} %get-tuple-element.82.q_all, f32[2048,128]{1,0:T(8,128)S(1)} %get-tuple-element.85.refs_0_, ...), custom_call_target="tpu_custom_call" | custom-call | flops 805306368 | bytes 1048576 | tf_op jit(solution)/shard_map/attend_rest/pallas_call | solution.py:374
  57.2 0.6 collective-permute-start.13
  57.8 4.6 %collective-permute-done.16.refs_4_ = bf16[256,1024]{1,0:T(8,128)(2,1)S(1)} collective-permute-done((bf16[256,1024]{1,0:T(8,128)(2,1)S(1)}, bf16[256,1024]{1,0:T(8,128)(2,1)S(1)}, u32[]{:S(2)}, u32[]{:S(2)}) %collective-permute-start.16) | collective-permute-done | bytes 524320 | tf_op jit(solution)/shard_map/ppermute | solution.py:518
  62.4 0.3 collective-permute-start.17
  62.6 1.2 %collective-permute-start.15 = (bf16[256,512]{1,0:T(8,128)(2,1)S(1)}, bf16[256,512]{1,0:T(8,128)(2,1)S(1)}, u32[]{:S(2)}, u32[]{:S(2)}) collective-permute-start(bf16[256,512]{1,0:T(8,128)(2,1)S(1)} %get-tuple-element.98), channel_id=1, source_target_pairs={{0,2},{1,3},{2,0},{3,1},{4,6},{5,7},{6,4},{7,5},{8,10},{9,11},{10,... | collective-permute-start | bytes 786440 | tf_op jit(solution)/shard_map/ppermute | solution.py:518
  63.8 1.2 %collective-permute-start.20 = (bf16[256,1024]{1,0:T(8,128)(2,1)S(1)}, bf16[256,1024]{1,0:T(8,128)(2,1)S(1)}, u32[]{:S(2)}, u32[]{:S(2)}) collective-permute-start(bf16[256,1024]{1,0:T(8,128)(2,1)S(1)} %collective-permute-done.16.refs_4_), channel_id=1, source_target_pairs={{0,16},{16,0},{1,17},{17,1},{2,18},{18,2},{3,19},{19,3},{4,20},{20... | collective-permute-start | bytes 1572872 | tf_op jit(solution)/shard_map/ppermute | solution.py:522
  65.1 4.1 %collective-permute-done.17.refs_1_ = bf16[256,512]{1,0:T(8,128)(2,1)S(1)} collective-permute-done((bf16[256,512]{1,0:T(8,128)(2,1)S(1)}, bf16[256,512]{1,0:T(8,128)(2,1)S(1)}, u32[]{:S(2)}, u32[]{:S(2)}) %collective-permute-start.17) | collective-permute-done | bytes 262176 | tf_op jit(solution)/shard_map/ppermute | solution.py:518
  69.1 3.5 %collective-permute-start.19 = (bf16[256,512]{1,0:T(8,128)(2,1)S(1)}, bf16[256,512]{1,0:T(8,128)(2,1)S(1)}, u32[]{:S(2)}, u32[]{:S(2)}) collective-permute-start(bf16[256,512]{1,0:T(8,128)(2,1)S(1)} %collective-permute-done.17.refs_1_), channel_id=1, source_target_pairs={{0,1},{1,0},{2,3},{3,2},{4,5},{5,4},{6,7},{7,6},{8,9},{9,8},{10,11... | collective-permute-start | bytes 786440 | tf_op jit(solution)/shard_map/ppermute | solution.py:518
  72.6 2.1 %collective-permute-done.15.refs_0_ = bf16[256,512]{1,0:T(8,128)(2,1)S(1)} collective-permute-done((bf16[256,512]{1,0:T(8,128)(2,1)S(1)}, bf16[256,512]{1,0:T(8,128)(2,1)S(1)}, u32[]{:S(2)}, u32[]{:S(2)}) %collective-permute-start.15) | collective-permute-done | bytes 262176 | tf_op jit(solution)/shard_map/ppermute | solution.py:518
  74.8 1.9 %collective-permute-start.18 = (bf16[256,512]{1,0:T(8,128)(2,1)S(1)}, bf16[256,512]{1,0:T(8,128)(2,1)S(1)}, u32[]{:S(2)}, u32[]{:S(2)}) collective-permute-start(bf16[256,512]{1,0:T(8,128)(2,1)S(1)} %collective-permute-done.15.refs_0_), channel_id=1, source_target_pairs={{0,1},{1,0},{2,3},{3,2},{4,5},{5,4},{6,7},{7,6},{8,9},{9,8},{10,11... | collective-permute-start | bytes 786440 | tf_op jit(solution)/shard_map/ppermute | solution.py:518
  76.7 0.0 collective-permute-done.13.h1
  76.8 1.8 %keep.1 = (f32[512,1024]{1,0:T(8,128)S(1)}, f32[8,128]{1,0:T(8,128)}) custom-call(s32[1,512]{1,0:T(1,128)S(1)} %copy-done.6, bf16[512,1024]{1,0:T(8,128)(2,1)S(1)} %copy-done.2, bf16[512,512]{1,0:T(8,128)(2,1)S(1)} %get-tuple-element.92.h0, bf16[512,512]{1,0:T(8,128)(2,1)S(1)} %collective-permute-done.13.h1, bf16[512,1024]{1,0:T(8,128)(2,1)S(1)} %get-tuple-element.95.w0, ...), custom_call_target="tpu_custom_call" | custom-call | flops 1610612736 | bytes 5242880 | tf_op jit(solution)/shard_map/keep/pallas_call | solution.py:440
  78.6 1.5 %gather.1.most = f32[512,1024]{1,0:T(8,128)S(1)} custom-call(s32[3]{0:T(128)S(1)} %pad_add_fusion.own, f32[512,1024]{1,0:T(8,128)S(1)} %get-tuple-element.97.kept, bf16[256,512]{1,0:T(8,128)(2,1)S(1)} %collective-permute-done.15.refs_0_, bf16[256,512]{1,0:T(8,128)(2,1)S(1)} %collective-permute-done.17.refs_1_, ...), custom_call_target="tpu_custom_call" | custom-call | flops 805306368 | bytes 4194304 | tf_op jit(solution)/shard_map/gather/pallas_call | solution.py:472
  80.1 2.1 %finish.1 = (bf16[512,1024]{1,0:T(8,128)(2,1)}, f32[2,512]{1,0:T(2,128)S(1)}) custom-call(s32[3]{0:T(128)S(1)} %pad_add_fusion.own, f32[512,1024]{1,0:T(8,128)S(1)} %gather.1.most, bf16[256,512]{1,0:T(8,128)(2,1)S(1)} %collective-permute-done.15.refs_0_, bf16[256,512]{1,0:T(8,128)(2,1)S(1)} %collective-permute-done.17.refs_1_, ...), custom_call_target="tpu_custom_call" | custom-call | flops 268435456 | bytes 4194304 | tf_op jit(solution)/shard_map/finish/pallas_call | solution.py:502
  82.2 0.0 collective-permute-start.21
  82.3 0.2 collective-permute-start.22
  82.5 1.9 %collective-permute-start.23 = (f32[2,512]{1,0:T(2,128)S(1)}, f32[2,512]{1,0:T(2,128)S(1)}, u32[]{:S(2)}, u32[]{:S(2)}) collective-permute-start(f32[2,512]{1,0:T(2,128)S(1)} %get-tuple-element.105), channel_id=1, source_target_pairs={{0,3},{1,2},{2,1},{3,0},{4,7},{5,6},{6,5},{7,4},{8,11},{9,10},{10,... | collective-permute-start | bytes 12296 | tf_op jit(solution)/shard_map/ppermute | solution.py:518
  84.4 0.3 collective-permute-done.22
  84.7 1.2 %collective-permute-done.23 = f32[2,512]{1,0:T(2,128)S(1)} collective-permute-done((f32[2,512]{1,0:T(2,128)S(1)}, f32[2,512]{1,0:T(2,128)S(1)}, u32[]{:S(2)}, u32[]{:S(2)}) %collective-permute-start.23) | collective-permute-done | bytes 4128 | tf_op jit(solution)/shard_map/ppermute | solution.py:518
  86.0 0.6 fusion.2
  (25 shorter events, 0.1 us)
Async XLA Ops:
  0.6 4.1 %collective-permute-start = (bf16[512,1024]{1,0:T(8,128)(2,1)}, bf16[512,1024]{1,0:T(8,128)(2,1)S(1)}, u32[]{:S(2)}, u32[]{:S(2)}) collective-permute-start(bf16[512,1024]{1,0:T(8,128)(2,1)} %own.1), channel_id=1, source_target_pairs={{0,1},{1,0},{2,3},{3,2},{4,5},{5,4},{6,7},{7,6},{8,9},{9,8},{10,11... | collective-permute-start | bytes 3145736 | tf_op jit(solution)/shard_map/ppermute | solution.py:518
  2.6 13.6 %collective-permute-start.3 = (bf16[256,1024]{1,0:T(8,128)(2,1)S(1)}, bf16[256,1024]{1,0:T(8,128)(2,1)S(1)}, u32[]{:S(2)}, u32[]{:S(2)}) collective-permute-start(bf16[256,1024]{1,0:T(8,128)(2,1)S(1)} %get-tuple-element.106), channel_id=1, source_target_pairs={{0,2},{1,3},{2,0},{3,1},{4,6},{5,7},{6,4},{7,5},{8,10},{9,11},{10,... | collective-permute-start | bytes 1572872 | tf_op jit(solution)/shard_map/ppermute | solution.py:518
  4.7 10.5 %copy-start = (bf16[512,4096]{1,0:T(8,128)(2,1)S(1)}, bf16[512,4096]{1,0:T(8,128)(2,1)}, u32[]{:S(2)}) copy-start(bf16[512,4096]{1,0:T(8,128)(2,1)} %w_out.1) | copy-start | bytes 12582916
  4.7 1.4 %copy-start.1 = (bf16[512,1024]{1,0:T(8,128)(2,1)S(1)}, bf16[512,1024]{1,0:T(8,128)(2,1)}, u32[]{:S(2)}) copy-start(bf16[512,1024]{1,0:T(8,128)(2,1)} %own.1) | copy-start | bytes 3145732
  6.1 2.4 %copy-start.3 = (bf16[4096,512]{1,0:T(8,128)(2,1)S(1)}, bf16[4096,512]{1,0:T(8,128)(2,1)}, u32[]{:S(2)}) copy-start(bf16[4096,512]{1,0:T(8,128)(2,1)} %wq.1) | copy-start | bytes 12582916
  8.5 1.2 %copy-start.4 = (bf16[4096,128]{1,0:T(8,128)(2,1)S(1)}, bf16[4096,128]{1,0:T(8,128)(2,1)}, u32[]{:S(2)}) copy-start(bf16[4096,128]{1,0:T(8,128)(2,1)} %wk.1) | copy-start | bytes 3145732
  9.7 1.2 %copy-start.5 = (bf16[4096,128]{1,0:T(8,128)(2,1)S(1)}, bf16[4096,128]{1,0:T(8,128)(2,1)}, u32[]{:S(2)}) copy-start(bf16[4096,128]{1,0:T(8,128)(2,1)} %wv.1) | copy-start | bytes 3145732
  15.2 3.4 %copy-start.7 = (s32[512]{0:T(512)S(1)}, s32[512]{0:T(512)}, u32[]{:S(2)}) copy-start(s32[512]{0:T(512)} %param.14) | copy-start | bytes 6148
  15.2 3.4 %copy-start.8 = (s32[512]{0:T(512)S(1)}, s32[512]{0:T(512)}, u32[]{:S(2)}) copy-start(s32[512]{0:T(512)} %param.15) | copy-start | bytes 6148
  15.2 3.4 %copy-start.9 = (s32[1,4]{1,0:T(1,128)S(1)}, s32[1,4]{1,0:T(1,128)}, u32[]{:S(2)}) copy-start(s32[1,4]{1,0:T(1,128)} %loads.1) | copy-start | bytes 52
  16.2 3.9 %collective-permute-start.4 = (bf16[256,1024]{1,0:T(8,128)(2,1)S(1)}, bf16[256,1024]{1,0:T(8,128)(2,1)S(1)}, u32[]{:S(2)}, u32[]{:S(2)}) collective-permute-start(bf16[256,1024]{1,0:T(8,128)(2,1)S(1)} %collective-permute-done.3.r2), channel_id=1, source_target_pairs={{0,1},{1,0},{2,3},{3,2},{4,5},{5,4},{6,7},{7,6},{8,9},{9,8},{10,11... | collective-permute-start | bytes 1572872 | tf_op jit(solution)/shard_map/ppermute | solution.py:518
  17.0 13.6 %collective-permute-start.2 = (bf16[256,1024]{1,0:T(8,128)(2,1)S(1)}, bf16[256,1024]{1,0:T(8,128)(2,1)S(1)}, u32[]{:S(2)}, u32[]{:S(2)}) collective-permute-start(bf16[256,1024]{1,0:T(8,128)(2,1)S(1)} %get-tuple-element.107), channel_id=1, source_target_pairs={{0,2},{1,3},{2,0},{3,1},{4,6},{5,7},{6,4},{7,5},{8,10},{9,11},{10,... | collective-permute-start | bytes 1572872 | tf_op jit(solution)/shard_map/ppermute | solution.py:518
  18.3 21.0 %collective-permute-start.1 = (bf16[512,1024]{1,0:T(8,128)(2,1)S(1)}, bf16[512,1024]{1,0:T(8,128)(2,1)S(1)}, u32[]{:S(2)}, u32[]{:S(2)}) collective-permute-start(bf16[512,1024]{1,0:T(8,128)(2,1)S(1)} %get-tuple-element.55), channel_id=1, source_target_pairs={{0,1},{1,0},{2,3},{3,2},{4,5},{5,4},{6,7},{7,6},{8,9},{9,8},{10,11... | collective-permute-start | bytes 3145736 | tf_op jit(solution)/shard_map/ppermute | solution.py:518
  21.9 8.7 %collective-permute-start.7 = (bf16[272,256]{1,0:T(8,128)(2,1)S(1)}, bf16[272,256]{1,0:T(8,128)(2,1)S(1)}, u32[]{:S(2)}, u32[]{:S(2)}) collective-permute-start(bf16[272,256]{1,0:T(8,128)(2,1)S(1)} %get-tuple-element.67.refs_1_), channel_id=1, source_target_pairs={{0,4},{4,8},{8,12},{12,0},{1,5},{5,9},{9,13},{13,1},{2,6},{6,10},{... | collective-permute-start | bytes 417800 | tf_op jit(solution)/shard_map/ppermute | solution.py:604
  23.3 11.8 %collective-permute-start.6 = (bf16[272,256]{1,0:T(8,128)(2,1)S(1)}, bf16[272,256]{1,0:T(8,128)(2,1)S(1)}, u32[]{:S(2)}, u32[]{:S(2)}) collective-permute-start(bf16[272,256]{1,0:T(8,128)(2,1)S(1)} %get-tuple-element.67.refs_1_), channel_id=1, source_target_pairs={{0,8},{4,12},{8,0},{12,4},{1,9},{5,13},{9,1},{13,5},{2,10},{6,14},... | collective-permute-start | bytes 417800 | tf_op jit(solution)/shard_map/ppermute | solution.py:604
  24.4 13.0 %collective-permute-start.5 = (bf16[272,256]{1,0:T(8,128)(2,1)S(1)}, bf16[272,256]{1,0:T(8,128)(2,1)S(1)}, u32[]{:S(2)}, u32[]{:S(2)}) collective-permute-start(bf16[272,256]{1,0:T(8,128)(2,1)S(1)} %get-tuple-element.67.refs_1_), channel_id=1, source_target_pairs={{0,12},{4,0},{8,4},{12,8},{1,13},{5,1},{9,5},{13,9},{2,14},{6,2},{... | collective-permute-start | bytes 417800 | tf_op jit(solution)/shard_map/ppermute | solution.py:604
  37.4 2.0 %collective-permute-start.8 = (bf16[256,1024]{1,0:T(8,128)(2,1)S(1)}, bf16[256,1024]{1,0:T(8,128)(2,1)S(1)}, u32[]{:S(2)}, u32[]{:S(2)}) collective-permute-start(bf16[256,1024]{1,0:T(8,128)(2,1)S(1)} %collective-permute-done.2.r2), channel_id=1, source_target_pairs={{0,1},{1,0},{2,3},{3,2},{4,5},{5,4},{6,7},{7,6},{8,9},{9,8},{10,11... | collective-permute-start | bytes 1572872 | tf_op jit(solution)/shard_map/ppermute | solution.py:518
  37.9 14.2 %collective-permute-start.12 = (bf16[256,1024]{1,0:T(8,128)(2,1)S(1)}, bf16[256,1024]{1,0:T(8,128)(2,1)S(1)}, u32[]{:S(2)}, u32[]{:S(2)}) collective-permute-start(bf16[256,1024]{1,0:T(8,128)(2,1)S(1)} %get-tuple-element.89), channel_id=1, source_target_pairs={{0,3},{1,2},{2,1},{3,0},{4,7},{5,6},{6,5},{7,4},{8,11},{9,10},{10,... | collective-permute-start | bytes 1572872 | tf_op jit(solution)/shard_map/ppermute | solution.py:518
  38.1 24.3 %collective-permute-start.16 = (bf16[256,1024]{1,0:T(8,128)(2,1)S(1)}, bf16[256,1024]{1,0:T(8,128)(2,1)S(1)}, u32[]{:S(2)}, u32[]{:S(2)}) collective-permute-start(bf16[256,1024]{1,0:T(8,128)(2,1)S(1)} %get-tuple-element.100), channel_id=1, source_target_pairs={{0,2},{1,3},{2,0},{3,1},{4,6},{5,7},{6,4},{7,5},{8,10},{9,11},{10,... | collective-permute-start | bytes 1572872 | tf_op jit(solution)/shard_map/ppermute | solution.py:518
  41.3 12.6 %copy-start.6 = (s32[1,512]{1,0:T(1,128)S(1)}, s32[1,512]{1,0:T(1,128)}, u32[]{:S(2)}) copy-start(s32[1,512]{1,0:T(1,128)} %order.1) | copy-start | bytes 6148
  41.3 12.1 %collective-permute-start.10 = (bf16[272,256]{1,0:T(8,128)(2,1)S(1)}, bf16[272,256]{1,0:T(8,128)(2,1)S(1)}, u32[]{:S(2)}, u32[]{:S(2)}) collective-permute-start(bf16[272,256]{1,0:T(8,128)(2,1)S(1)} %get-tuple-element.88), channel_id=1, source_target_pairs={{0,8},{4,12},{8,0},{12,4},{1,9},{5,13},{9,1},{13,5},{2,10},{6,14},... | collective-permute-start | bytes 417800 | tf_op jit(solution)/shard_map/ppermute | solution.py:604
  42.7 10.7 %collective-permute-start.11 = (bf16[272,256]{1,0:T(8,128)(2,1)S(1)}, bf16[272,256]{1,0:T(8,128)(2,1)S(1)}, u32[]{:S(2)}, u32[]{:S(2)}) collective-permute-start(bf16[272,256]{1,0:T(8,128)(2,1)S(1)} %get-tuple-element.88), channel_id=1, source_target_pairs={{0,12},{4,0},{8,4},{12,8},{1,13},{5,1},{9,5},{13,9},{2,14},{6,2},{... | collective-permute-start | bytes 417800 | tf_op jit(solution)/shard_map/ppermute | solution.py:604
  42.7 11.2 %collective-permute-start.9 = (bf16[272,256]{1,0:T(8,128)(2,1)S(1)}, bf16[272,256]{1,0:T(8,128)(2,1)S(1)}, u32[]{:S(2)}, u32[]{:S(2)}) collective-permute-start(bf16[272,256]{1,0:T(8,128)(2,1)S(1)} %get-tuple-element.88), channel_id=1, source_target_pairs={{0,4},{4,8},{8,12},{12,0},{1,5},{5,9},{9,13},{13,1},{2,6},{6,10},{... | collective-permute-start | bytes 417800 | tf_op jit(solution)/shard_map/ppermute | solution.py:604
  49.2 27.5 %copy-start.10 = (bf16[1024]{0:T(1024)(128)(2,1)S(1)}, bf16[1024]{0:T(1024)(128)(2,1)}, u32[]{:S(2)}) copy-start(bf16[1024]{0:T(1024)(128)(2,1)} %param.22) | copy-start | bytes 6148
  49.2 27.5 %copy-start.11 = (bf16[1024]{0:T(1024)(128)(2,1)S(1)}, bf16[1024]{0:T(1024)(128)(2,1)}, u32[]{:S(2)}) copy-start(bf16[1024]{0:T(1024)(128)(2,1)} %param.23) | copy-start | bytes 6148
  49.2 27.6 %copy-start.2 = (bf16[512,1024]{1,0:T(8,128)(2,1)S(1)}, bf16[512,1024]{1,0:T(8,128)(2,1)}, u32[]{:S(2)}) copy-start(bf16[512,1024]{1,0:T(8,128)(2,1)} %own.1) | copy-start | bytes 3145732
  52.1 24.6 %collective-permute-start.14 = (bf16[256,1024]{1,0:T(8,128)(2,1)S(1)}, bf16[256,1024]{1,0:T(8,128)(2,1)S(1)}, u32[]{:S(2)}, u32[]{:S(2)}) collective-permute-start(bf16[256,1024]{1,0:T(8,128)(2,1)S(1)} %collective-permute-done.12.refs_5_), channel_id=1, source_target_pairs={{0,16},{16,0},{1,17},{17,1},{2,18},{18,2},{3,19},{19,3},{4,20},{20... | collective-permute-start | bytes 1572872 | tf_op jit(solution)/shard_map/ppermute | solution.py:522
  57.2 19.5 %collective-permute-start.13 = (bf16[512,512]{1,0:T(8,128)(2,1)S(1)}, bf16[512,512]{1,0:T(8,128)(2,1)S(1)}, u32[]{:S(2)}, u32[]{:S(2)}) collective-permute-start(bf16[512,512]{1,0:T(8,128)(2,1)S(1)} %get-tuple-element.92.h0), channel_id=1, source_target_pairs={{0,1},{1,0},{2,3},{3,2},{4,5},{5,4},{6,7},{7,6},{8,9},{9,8},{10,11... | collective-permute-start | bytes 1572872 | tf_op jit(solution)/shard_map/ppermute | solution.py:518
  62.4 6.8 %collective-permute-start.17 = (bf16[256,512]{1,0:T(8,128)(2,1)S(1)}, bf16[256,512]{1,0:T(8,128)(2,1)S(1)}, u32[]{:S(2)}, u32[]{:S(2)}) collective-permute-start(bf16[256,512]{1,0:T(8,128)(2,1)S(1)} %get-tuple-element.101), channel_id=1, source_target_pairs={{0,2},{1,3},{2,0},{3,1},{4,6},{5,7},{6,4},{7,5},{8,10},{9,11},{10,... | collective-permute-start | bytes 786440 | tf_op jit(solution)/shard_map/ppermute | solution.py:518
  62.6 12.1 %collective-permute-start.15 = (bf16[256,512]{1,0:T(8,128)(2,1)S(1)}, bf16[256,512]{1,0:T(8,128)(2,1)S(1)}, u32[]{:S(2)}, u32[]{:S(2)}) collective-permute-start(bf16[256,512]{1,0:T(8,128)(2,1)S(1)} %get-tuple-element.98), channel_id=1, source_target_pairs={{0,2},{1,3},{2,0},{3,1},{4,6},{5,7},{6,4},{7,5},{8,10},{9,11},{10,... | collective-permute-start | bytes 786440 | tf_op jit(solution)/shard_map/ppermute | solution.py:518
  63.8 16.3 %collective-permute-start.20 = (bf16[256,1024]{1,0:T(8,128)(2,1)S(1)}, bf16[256,1024]{1,0:T(8,128)(2,1)S(1)}, u32[]{:S(2)}, u32[]{:S(2)}) collective-permute-start(bf16[256,1024]{1,0:T(8,128)(2,1)S(1)} %collective-permute-done.16.refs_4_), channel_id=1, source_target_pairs={{0,16},{16,0},{1,17},{17,1},{2,18},{18,2},{3,19},{19,3},{4,20},{20... | collective-permute-start | bytes 1572872 | tf_op jit(solution)/shard_map/ppermute | solution.py:522
  69.1 9.4 %collective-permute-start.19 = (bf16[256,512]{1,0:T(8,128)(2,1)S(1)}, bf16[256,512]{1,0:T(8,128)(2,1)S(1)}, u32[]{:S(2)}, u32[]{:S(2)}) collective-permute-start(bf16[256,512]{1,0:T(8,128)(2,1)S(1)} %collective-permute-done.17.refs_1_), channel_id=1, source_target_pairs={{0,1},{1,0},{2,3},{3,2},{4,5},{5,4},{6,7},{7,6},{8,9},{9,8},{10,11... | collective-permute-start | bytes 786440 | tf_op jit(solution)/shard_map/ppermute | solution.py:518
  74.8 3.8 %collective-permute-start.18 = (bf16[256,512]{1,0:T(8,128)(2,1)S(1)}, bf16[256,512]{1,0:T(8,128)(2,1)S(1)}, u32[]{:S(2)}, u32[]{:S(2)}) collective-permute-start(bf16[256,512]{1,0:T(8,128)(2,1)S(1)} %collective-permute-done.15.refs_0_), channel_id=1, source_target_pairs={{0,1},{1,0},{2,3},{3,2},{4,5},{5,4},{6,7},{7,6},{8,9},{9,8},{10,11... | collective-permute-start | bytes 786440 | tf_op jit(solution)/shard_map/ppermute | solution.py:518
  82.2 2.1 %collective-permute-start.21 = (f32[2,512]{1,0:T(2,128)S(1)}, f32[2,512]{1,0:T(2,128)S(1)}, u32[]{:S(2)}, u32[]{:S(2)}) collective-permute-start(f32[2,512]{1,0:T(2,128)S(1)} %get-tuple-element.105), channel_id=1, source_target_pairs={{0,1},{1,0},{2,3},{3,2},{4,5},{5,4},{6,7},{7,6},{8,9},{9,8},{10,11... | collective-permute-start | bytes 12296 | tf_op jit(solution)/shard_map/ppermute | solution.py:518
  82.3 2.5 %collective-permute-start.22 = (f32[2,512]{1,0:T(2,128)S(1)}, f32[2,512]{1,0:T(2,128)S(1)}, u32[]{:S(2)}, u32[]{:S(2)}) collective-permute-start(f32[2,512]{1,0:T(2,128)S(1)} %get-tuple-element.105), channel_id=1, source_target_pairs={{0,2},{1,3},{2,0},{3,1},{4,6},{5,7},{6,4},{7,5},{8,10},{9,11},{10,... | collective-permute-start | bytes 12296 | tf_op jit(solution)/shard_map/ppermute | solution.py:518
  82.5 3.5 %collective-permute-start.23 = (f32[2,512]{1,0:T(2,128)S(1)}, f32[2,512]{1,0:T(2,128)S(1)}, u32[]{:S(2)}, u32[]{:S(2)}) collective-permute-start(f32[2,512]{1,0:T(2,128)S(1)} %get-tuple-element.105), channel_id=1, source_target_pairs={{0,3},{1,2},{2,1},{3,0},{4,7},{5,6},{6,5},{7,4},{8,11},{9,10},{10,... | collective-permute-start | bytes 12296 | tf_op jit(solution)/shard_map/ppermute | solution.py:518

commit v5 on v4

--- a/solution.py
+++ b/solution.py
@@ -17,7 +17,6 @@
 POS_SPAN = 1024
 POS_DIGIT = 128
 DIGIT_ROWS = 16
-N_PART = 2
 
 QUERY_BLOCK = 128
 KEY_BLOCK = 256
@@ -249,10 +248,22 @@
     )(own, before, acc, squares, r2, r3, gain, weights, cos, sin, digits, *q_old, *kv_old)
 
 
-def pick_rows(order, x):
-    rows = x.shape[0]
-    pick = (order == lax.broadcasted_iota(jnp.int32, (rows, rows), 0)).astype(jnp.bfloat16)
-    return lax.dot_general(pick, x, (((0,), (0,)), ((), ())), preferred_element_type=jnp.float32)
+def part_sizes(rows):
+    return (rows // 2, rows // 2)
+
+
+def pick_matrix(order, out):
+    rows = out.shape[0]
+    size = QUERY_BLOCK
+    for i in range(0, rows, size):
+        wanted = jnp.broadcast_to(order[:, i : i + size], (size, size)).T
+        for j in range(0, rows, size):
+            at = lax.broadcasted_iota(jnp.int32, (size, size), 1) + j
+            out[i : i + size, j : j + size] = jnp.where(wanted == at, 1.0, 0.0).astype(out.dtype)
+
+
+def pick_rows(pick, x):
+    return jnp.dot(pick, x, preferred_element_type=jnp.float32)
 
 
 def attend_kernel(pieces, last, own, q_all, *refs):
@@ -268,13 +279,13 @@
     if last:
         m_in, l_in, acc_in, own_keys = take(4)
         kv_in = take(len(pieces))
-        _, order, out, *parts = take(3 + N_PART)
+        _, pick, out, *parts = take(5)
         heads, kv_all, keys = take(3)
         unpack(pieces, kv_in, own, kv_all, keys)
         own_line = kv_all.shape[0] // QUERY_BLOCK
         keys[own_line : own_line + n_query, :] = own_keys[:n_query, :]
     else:
-        kv_all, keys, m_out, l_out, acc_out, _ = take(6)
+        kv_all, keys, order, m_out, l_out, acc_out, pick, _ = take(8)
         own_line = 0
     m_s, l_s, acc_s, keys_s, sem = refs
     n_key = kv_all.shape[0] // KEY_BLOCK
@@ -342,31 +353,35 @@
 
     lax.fori_loop(0, n_query, block, 0)
     if last:
-        picked = pick_rows(order[...], heads[...]).astype(jnp.bfloat16)
+        picked = pick_rows(pick[...], heads[...]).astype(jnp.bfloat16)
         out[...] = picked
-        for i, part in enumerate(parts):
-            part[...] = picked[i * part.shape[0] : (i + 1) * part.shape[0], :]
-
-
-def attend(own, q_all, kv_all, keys):
+        row = 0
+        for part in parts:
+            part[...] = picked[row : row + part.shape[0], :]
+            row += part.shape[0]
+    else:
+        pick_matrix(order, pick)
+
+
+def attend(own, q_all, kv_all, keys, order):
     n_head, rows, _ = q_all.shape
     stacked = n_head * QUERY_BLOCK
     n_key = kv_all.shape[0]
     running = jax.ShapeDtypeStruct((n_head * rows, HEAD_WIDTH), jnp.float32)
     return pl.pallas_call(
         functools.partial(attend_kernel, (), False),
-        out_shape=(running,) * 3 + (TOKEN,),
-        in_specs=[pl.BlockSpec(memory_space=pltpu.SMEM)] + [whole()] * 3,
-        out_specs=(whole(),) * 3 + (far_memory(),),
+        out_shape=(running,) * 3 + (jax.ShapeDtypeStruct((rows, rows), jnp.bfloat16), TOKEN),
+        in_specs=[pl.BlockSpec(memory_space=pltpu.SMEM)] + [whole()] * 4,
+        out_specs=(whole(),) * 4 + (far_memory(),),
         scratch_shapes=[VMEM((stacked, HEAD_WIDTH), jnp.float32)] * 3
         + [pltpu.SMEM(keys.shape, jnp.int32), pltpu.SemaphoreType.DMA(())],
         compiler_params=params(12),
         cost_estimate=cost(4 * rows * n_key * n_head * HEAD_WIDTH, 4 * rows * n_head * HEAD_WIDTH),
         name="attend",
-    )(own, q_all, kv_all, keys)
-
-
-def attend_rest(own, q_all, state, own_keys, pieces, kv_parts, token, order):
+    )(own, q_all, kv_all, keys, order)
+
+
+def attend_rest(own, q_all, state, own_keys, pieces, kv_parts, token, pick):
     n_head, rows, _ = q_all.shape
     stacked = n_head * QUERY_BLOCK
     n_key = sum(size for _, size in pieces)
@@ -375,12 +390,12 @@
         functools.partial(attend_kernel, tuple(pieces), True),
         out_shape=tuple(
             jax.ShapeDtypeStruct((size, n_head * HEAD_WIDTH), jnp.bfloat16)
-            for size in [rows] + [rows // N_PART] * N_PART
+            for size in (rows, *part_sizes(rows))
         ),
         in_specs=[pl.BlockSpec(memory_space=pltpu.SMEM)]
         + [whole()] * (5 + len(pieces))
         + [far_memory(), whole()],
-        out_specs=(whole(),) * (1 + N_PART),
+        out_specs=(whole(),) * 3,
         scratch_shapes=[
             VMEM((rows, n_head * HEAD_WIDTH), jnp.bfloat16),
             VMEM((n_key, 2 * HEAD_WIDTH), jnp.bfloat16),
@@ -391,7 +406,7 @@
         compiler_params=params(12 + n_key // 512),
         cost_estimate=cost(4 * rows * n_key * n_head * HEAD_WIDTH, 4 * rows * n_head * HEAD_WIDTH),
         name="attend_rest",
-    )(own, q_all, *state, own_keys, *kv_parts, token, order)
+    )(own, q_all, *state, own_keys, *kv_parts, token, pick)
 
 
 def columns_kernel(own, w_out, token_in, near, send_near, far, beside, token, sem):
@@ -427,14 +442,14 @@
     )(own, w_out, token)
 
 
-def keep_kernel(order, own, h0, h1, w0, w1, out, token):
+def keep_kernel(pick, own, h0, h1, w0, w1, out, token):
     del token
     total = jnp.dot(h0[...], w0[...], preferred_element_type=jnp.float32)
     total += jnp.dot(h1[...], w1[...], preferred_element_type=jnp.float32)
-    out[...] = total + pick_rows(order[...], own[...])
-
-
-def keep(order, own, h0, h1, w0, w1):
+    out[...] = total + pick_rows(pick[...], own[...])
+
+
+def keep(pick, own, h0, h1, w0, w1):
     rows, width = own.shape
     depth = h0.shape[1]
     return pl.pallas_call(
@@ -445,7 +460,7 @@
         compiler_params=params(12),
         cost_estimate=cost(2 * rows * (2 * depth + rows) * width, 4 * depth * width + 6 * rows * width),
         name="keep",
-    )(order, own, h0, h1, w0, w1)
+    )(pick, own, h0, h1, w0, w1)
 
 
 def shares(own, h):
@@ -453,41 +468,39 @@
     return tuple(pl.ds(pl.multiple_of(share * half, half), half) for share in (own[1], 1 - own[1]))
 
 
-def gather_kernel(own, kept, *refs):
-    *heads, w2, w3, other3, out = refs
-    rows = heads[0].shape[0]
-    for j in range(N_PART):
-        span = slice(j * rows, (j + 1) * rows)
-        h2, h3 = heads[j], heads[N_PART + j]
-        mine, others = shares(own, h2)
-        total = kept[span, :]
-        for h, columns, weight in ((h2, mine, w2), (h3, mine, w3), (h3, others, other3)):
-            total += jnp.dot(h[:, columns], weight[...], preferred_element_type=jnp.float32)
-        out[span, :] = total
-
-
-def gather(own, kept, heads2, heads3, w2, w3, other3):
-    rows, width = kept.shape
-    depth = heads2[0].shape[1]
+def add_heads(total, own, h2, h3, w2, w3, other3):
+    mine, others = shares(own, h2)
+    for h, columns, weight in ((h2, mine, w2), (h3, mine, w3), (h3, others, other3)):
+        total += jnp.dot(h[:, columns], weight[...], preferred_element_type=jnp.float32)
+    return total
+
+
+def gather_kernel(own, token, kept, h2, h3, w2, w3, other3, out):
+    del token
+    out[...] = add_heads(kept[: h2.shape[0], :], own, h2, h3, w2, w3, other3)
+
+
+def gather(own, token, kept, h2, h3, w2, w3, other3):
+    rows, depth = h2.shape
+    width = kept.shape[1]
     return pl.pallas_call(
         gather_kernel,
         out_shape=jax.ShapeDtypeStruct((rows, width), jnp.float32),
-        in_specs=[pl.BlockSpec(memory_space=pltpu.SMEM)] + [whole()] * (4 + 2 * N_PART),
+        in_specs=[pl.BlockSpec(memory_space=pltpu.SMEM), far_memory()] + [whole()] * 6,
         out_specs=whole(),
         compiler_params=params(14),
         cost_estimate=cost(3 * rows * depth * width, 8 * rows * width),
         name="gather",
-    )(own, kept, *heads2, *heads3, w2, w3, other3)
-
-
-def finish_kernel(own, most, *refs):
-    *heads, other2, gain, head, hidden_out, sums = refs
-    rows = heads[0].shape[0]
+    )(own, token, kept, h2, h3, w2, w3, other3)
+
+
+def finish_kernel(own, most, kept, top2, h2, h3, w2, w3, other3, other2, gain, head, hidden_out, sums):
+    first = most.shape[0]
     weight = gain[...].astype(jnp.float32) * head[...].astype(jnp.float32)
-    for j, h in enumerate(heads):
-        span = slice(j * rows, (j + 1) * rows)
+    rest = add_heads(kept[first:, :], own, h2, h3, w2, w3, other3)
+    for span, h, total in ((slice(0, first), top2, most[...]), (slice(first, kept.shape[0]), h2, rest)):
         _, others = shares(own, h)
-        total = most[span, :] + jnp.dot(h[:, others], other2[...], preferred_element_type=jnp.float32)
+        total += jnp.dot(h[:, others], other2[...], preferred_element_type=jnp.float32)
         hidden = total.astype(jnp.bfloat16)
         hidden_out[span, :] = hidden
         x = hidden.astype(jnp.float32)
@@ -496,21 +509,21 @@
             sums[i : i + 1, span] = jnp.sum(lanes.T, 0, keepdims=True)
 
 
-def finish(own, most, heads2, other2, gain, head):
-    rows, width = most.shape
-    depth = heads2[0].shape[1]
+def finish(own, most, kept, top2, h2, h3, w2, w3, other3, other2, gain, head):
+    rows, width = kept.shape
+    depth = h2.shape[1]
     return pl.pallas_call(
         finish_kernel,
         out_shape=(
             jax.ShapeDtypeStruct((rows, width), jnp.bfloat16),
             jax.ShapeDtypeStruct((2, rows), jnp.float32),
         ),
-        in_specs=[pl.BlockSpec(memory_space=pltpu.SMEM)] + [whole()] * (4 + N_PART),
+        in_specs=[pl.BlockSpec(memory_space=pltpu.SMEM)] + [whole()] * 11,
         out_specs=(whole(), whole()),
         compiler_params=params(14),
-        cost_estimate=cost(rows * depth * width, 8 * rows * width),
+        cost_estimate=cost(2 * rows * depth * width, 8 * rows * width),
         name="finish",
-    )(own, most, *heads2, other2, gain, head)
+    )(own, most, kept, top2, h2, h3, w2, w3, other3, other2, gain, head)
 
 
 def flip(x, bit):
@@ -605,7 +618,7 @@
 
     order = prompt_order.reshape(1, rows)
     q_all, (kv_all, keys) = q, side
-    *state, token = attend(t_own, q_all, kv_all, keys)
+    *state, pick, token = attend(t_own, q_all, kv_all, keys, order)
     far3, token = lax.optimization_barrier((far3, token))
     other3 = swap_parts(far3)
     heads, *parts = attend_rest(
@@ -616,7 +629,7 @@
         [(d, sizes[-1]) for d in range(1, n_dp)],
         [kv_parts[d][-1] for d in range(1, n_dp)],
         token,
-        order,
+        pick,
     )
     heads2 = [flip(parts[0], 2)]
     rest, far2 = lax.optimization_barrier((parts[1], far2))
@@ -624,12 +637,23 @@
     other2 = swap_parts(far2)
     heads_other = flip(heads, 1)
     heads_other, other3 = lax.optimization_barrier((heads_other, other3))
-    kept, token = keep(order, hidden_in, heads, heads_other, near, near_other)
+    kept, token = keep(pick, hidden_in, heads, heads_other, near, near_other)
     heads2[0], token = lax.optimization_barrier((heads2[0], token))
     heads3 = [flip(x, 1) for x in heads2]
-    most = gather(t_own, kept, heads2, heads3, far2, far3, other3)
+    most = gather(t_own, token, kept, heads2[0], heads3[0], far2, far3, other3)
     hidden, sums = finish(
-        t_own, most, heads2, other2, final_gain.reshape(1, width), value_head.reshape(1, width)
+        t_own,
+        most,
+        kept,
+        heads2[0],
+        heads2[1],
+        heads3[1],
+        far2,
+        far3,
+        other3,
+        other2,
+        final_gain.reshape(1, width),
+        value_head.reshape(1, width),
     )
     square, product = sums + flip(sums, 1) + (flip(sums, 2) + flip(sums, 3))
     return hidden, product * lax.rsqrt(square / MODEL_WIDTH + NORM_EPS)

time: 86.9 us -> 86 us (0.990); the launches traced: 86.6 us -> 84.3 us
  starting transfers between devices: 24.9 us -> 21.7 us
    ppermute x16, starting transfers between devices: 15.7 us -> 12.5 us  [flip(): return lax.ppermute(x, 'tensor', [(i, i ^ bit) for i in range(count)])]
    ppermute x2, waiting for transfers between devices: 0.01 us -> 2.16 us  [swap_parts(): return lax.ppermute(x, 'parts', [(0, 1), (1, 0)])]
    ppermute x16, waiting for transfers between devices: 20.4 us -> 19 us  [flip(): return lax.ppermute(x, 'tensor', [(i, i ^ bit) for i in range(count)])]
  transfers between devices with their start and end apart: 24 -> 24, of which waited for: 12 -> 12; matrix products, arithmetic and copies ran while one was open for 2% -> 2% of each run, Pallas kernels for 25% -> 26%
where the time goes in v5:
time: 86 us; the launch traced here: 84.3 us
  waiting for transfers between devices  28.5 us (33%)
  Pallas kernels  24.3 us (28%)
  starting transfers between devices  21.7 us (25%)
  local copies, waits for them, and re-layouts  8.23 us (10%)
    ppermute x16, waiting for transfers between devices, flip(): return lax.ppermute(x, 'tensor', [(i, i ^ bit) for i in range(count)])  19 us
    ppermute x16, starting transfers between devices, flip(): return lax.ppermute(x, 'tensor', [(i, i ^ bit) for i in range(count)])  12.5 us
    ppermute x6, waiting for transfers between devices, on_device(): lax.ppermute(kv, 'dp', [(i, (i + d) % n_dp) for i in range(n_dp)])  7.36 us
    ppermute x6, starting transfers between devices, on_device(): lax.ppermute(kv, 'dp', [(i, (i + d) % n_dp) for i in range(n_dp)])  6.71 us
    unnamed x24, local copies, waits for them, and re-layouts  6.25 us
    pallas_call x1, Pallas kernels, attend(): pl.pallas_call(functools.partial(attend_kernel, (), False), out_shape=(ru...  4.63 us
    pallas_call x1, Pallas kernels, early(): pl.pallas_call(early_kernel, out_shape=(jax.ShapeDtypeStruct((rows, colum...  4.23 us
    pallas_call x1, Pallas kernels, attend_rest(): pl.pallas_call(functools.partial(attend_kernel, tuple(pieces), True), out...  3.74 us
  transfers between devices with their start and end apart: 24, of which 12 were waited for; matrix products, arithmetic and copies ran while one was open for 2% of the time, Pallas kernels for 26%

profile of v5, /device:TPU:9, one launch (start us, length us, event | category | flops | bytes accessed | tf_op | source)
XLA Modules:
  0.0 84.3 jit_solution(7689509464640142500)
XLA Ops:
  0.6 0.7 collective-permute-start
  1.4 1.3 %fusion.3 = (bf16[256,1024]{1,0:T(8,128)(2,1)S(1)}, bf16[256,1024]{1,0:T(8,128)(2,1)S(1)}) fusion(bf16[512,1024]{1,0:T(8,128)(2,1)} %own.1), kind=kLoop, calls=%fused_computation.6 | loop fusion | bytes 2097152 | tf_op jit(solution)/shard_map/slice | solution.py:564
  2.6 1.3 %collective-permute-start.3 = (bf16[256,1024]{1,0:T(8,128)(2,1)S(1)}, bf16[256,1024]{1,0:T(8,128)(2,1)S(1)}, u32[]{:S(2)}, u32[]{:S(2)}) collective-permute-start(bf16[256,1024]{1,0:T(8,128)(2,1)S(1)} %get-tuple-element.114), channel_id=1, source_target_pairs={{0,2},{1,3},{2,0},{3,1},{4,6},{5,7},{6,4},{7,5},{8,10},{9,11},{10,... | collective-permute-start | bytes 1572872 | tf_op jit(solution)/shard_map/ppermute | solution.py:531
  3.9 0.7 reshape.25.gain
  4.6 0.1 pad_add_fusion.own
  4.7 0.0 collective-permute-done.r1
  4.7 1.4 %copy-done.1 = bf16[512,1024]{1,0:T(8,128)(2,1)S(1)} copy-done((bf16[512,1024]{1,0:T(8,128)(2,1)S(1)}, bf16[512,1024]{1,0:T(8,128)(2,1)}, u32[]{:S(2)}) %copy-start.1) | copy-done | bytes 1048600
  6.1 2.4 %copy-done.3 = bf16[4096,512]{1,0:T(8,128)(2,1)S(1)} copy-done((bf16[4096,512]{1,0:T(8,128)(2,1)S(1)}, bf16[4096,512]{1,0:T(8,128)(2,1)}, u32[]{:S(2)}) %copy-start.3) | copy-done | bytes 4194328
  8.5 1.2 %copy-done.4 = bf16[4096,128]{1,0:T(8,128)(2,1)S(1)} copy-done((bf16[4096,128]{1,0:T(8,128)(2,1)S(1)}, bf16[4096,128]{1,0:T(8,128)(2,1)}, u32[]{:S(2)}) %copy-start.4) | copy-done | bytes 1048600
  9.7 1.2 %copy-done.5 = bf16[4096,128]{1,0:T(8,128)(2,1)S(1)} copy-done((bf16[4096,128]{1,0:T(8,128)(2,1)S(1)}, bf16[4096,128]{1,0:T(8,128)(2,1)}, u32[]{:S(2)}) %copy-start.5) | copy-done | bytes 1048600
  10.9 4.2 %early.1 = (f32[512,768]{1,0:T(8,128)S(1)}, f32[512,1]{1,0:T(8,128)S(1)}, bf16[2,1024,768]{2,1,0:T(8,128)(2,1)S(1)}, f32[8,128]{1,0:T(8,128)S(1)}) custom-call(s32[3]{0:T(128)S(1)} %pad_add_fusion.own, bf16[512,1024]{1,0:T(8,128)(2,1)S(1)} %copy-done.1, bf16[512,1024]{1,0:T(8,128)(2,1)S(1)} %collective-permute-done.r1, bf16[1,4096]{1,0:T(2,128)(2,1)S(1)} %reshape.25.gain, ...), custom_call_target="tpu_custom_call" | custom-call | flops 1610612736 | bytes 6291456 | tf_op jit(solution)/shard_map/early/pallas_call | solution.py:143
  15.2 0.0 copy-start.6
  15.2 0.0 copy-start.7
  15.2 0.0 copy-start.9
  15.2 1.1 %columns.1 = (bf16[512,1024]{1,0:T(8,128)(2,1)S(1)}, bf16[512,1024]{1,0:T(8,128)(2,1)S(1)}, bf16[256,1024]{1,0:T(8,128)(2,1)S(1)}, bf16[256,1024]{1,0:T(8,128)(2,1)S(1)}, f32[8,128]{1,0:T(8,128)S(1)}) custom-call(s32[3]{0:T(128)S(1)} %pad_add_fusion.own, bf16[512,4096]{1,0:T(8,128)(2,1)S(1)} %copy-done, f32[8,128]{1,0:T(8,128)S(1)} %get-tuple-element.58.token_in), custom_call_target="tpu_custom_call" | custom-call | flops 1 | bytes 8388608 | tf_op jit(solution)/shard_map/columns/pallas_call | solution.py:433
  16.3 0.7 collective-permute-start.4
  17.0 1.2 %collective-permute-start.2 = (bf16[256,1024]{1,0:T(8,128)(2,1)S(1)}, bf16[256,1024]{1,0:T(8,128)(2,1)S(1)}, u32[]{:S(2)}, u32[]{:S(2)}) collective-permute-start(bf16[256,1024]{1,0:T(8,128)(2,1)S(1)} %get-tuple-element.115), channel_id=1, source_target_pairs={{0,2},{1,3},{2,0},{3,1},{4,6},{5,7},{6,4},{7,5},{8,10},{9,11},{10,... | collective-permute-start | bytes 1572872 | tf_op jit(solution)/shard_map/ppermute | solution.py:531
  18.3 0.3 collective-permute-start.1
  18.5 1.6 %prep.1 = (bf16[16,512]{1,0:T(8,128)(2,1)S(1)}, f32[512,128]{1,0:T(8,128)S(1)}, f32[512,128]{1,0:T(8,128)S(1)}) custom-call(s32[1,4]{1,0:T(1,128)S(1)} %copy-done.9, s32[4,128]{1,0:T(4,128)S(1)} %bitcast.6, s32[4,128]{1,0:T(4,128)S(1)} %bitcast.7), custom_call_target="tpu_custom_call" | custom-call | flops 2000000000 | bytes 40000000 | tf_op jit(solution)/shard_map/prep/pallas_call | solution.py:79
  20.1 0.0 collective-permute-done.4.r3
  20.1 1.8 %late.2 = (bf16[4,256,128]{2,1,0:T(8,128)(2,1)S(1)}, bf16[272,256]{1,0:T(8,128)(2,1)S(1)}, f32[8,128]{1,0:T(8,128)S(1)}) custom-call(s32[3]{0:T(128)S(1)} %pad_add_fusion.own, f32[8,128]{1,0:T(8,128)S(1)} %get-tuple-element.61.before, f32[512,768]{1,0:T(8,128)S(1)} %get-tuple-element.62.acc, f32[512,1]{1,0:T(8,128)S(1)} %get-tuple-element.63.squares, ...), custom_call_target="tpu_custom_call" | custom-call | flops 805306368 | bytes 3145728 | tf_op jit(solution)/shard_map/late/pallas_call | solution.py:234
  21.9 1.3 %collective-permute-start.7 = (bf16[272,256]{1,0:T(8,128)(2,1)S(1)}, bf16[272,256]{1,0:T(8,128)(2,1)S(1)}, u32[]{:S(2)}, u32[]{:S(2)}) collective-permute-start(bf16[272,256]{1,0:T(8,128)(2,1)S(1)} %get-tuple-element.71.refs_1_), channel_id=1, source_target_pairs={{0,4},{4,8},{8,12},{12,0},{1,5},{5,9},{9,13},{13,1},{2,6},{6,10},{... | collective-permute-start | bytes 417800 | tf_op jit(solution)/shard_map/ppermute | solution.py:617
  23.3 1.1 %collective-permute-start.6 = (bf16[272,256]{1,0:T(8,128)(2,1)S(1)}, bf16[272,256]{1,0:T(8,128)(2,1)S(1)}, u32[]{:S(2)}, u32[]{:S(2)}) collective-permute-start(bf16[272,256]{1,0:T(8,128)(2,1)S(1)} %get-tuple-element.71.refs_1_), channel_id=1, source_target_pairs={{0,8},{4,12},{8,0},{12,4},{1,9},{5,13},{9,1},{13,5},{2,10},{6,14},... | collective-permute-start | bytes 417800 | tf_op jit(solution)/shard_map/ppermute | solution.py:617
  24.4 1.4 %collective-permute-start.5 = (bf16[272,256]{1,0:T(8,128)(2,1)S(1)}, bf16[272,256]{1,0:T(8,128)(2,1)S(1)}, u32[]{:S(2)}, u32[]{:S(2)}) collective-permute-start(bf16[272,256]{1,0:T(8,128)(2,1)S(1)} %get-tuple-element.71.refs_1_), channel_id=1, source_target_pairs={{0,12},{4,0},{8,4},{12,8},{1,13},{5,1},{9,5},{13,9},{2,14},{6,2},{... | collective-permute-start | bytes 417800 | tf_op jit(solution)/shard_map/ppermute | solution.py:617
  25.8 4.8 %collective-permute-done.2.r2 = bf16[256,1024]{1,0:T(8,128)(2,1)S(1)} collective-permute-done((bf16[256,1024]{1,0:T(8,128)(2,1)S(1)}, bf16[256,1024]{1,0:T(8,128)(2,1)S(1)}, u32[]{:S(2)}, u32[]{:S(2)}) %collective-permute-start.2) | collective-permute-done | bytes 524320 | tf_op jit(solution)/shard_map/ppermute | solution.py:531
  30.6 0.0 collective-permute-done.7.refs_2_
  30.6 4.5 %collective-permute-done.6.refs_3_ = bf16[272,256]{1,0:T(8,128)(2,1)S(1)} collective-permute-done((bf16[272,256]{1,0:T(8,128)(2,1)S(1)}, bf16[272,256]{1,0:T(8,128)(2,1)S(1)}, u32[]{:S(2)}, u32[]{:S(2)}) %collective-permute-start.6) | collective-permute-done | bytes 139296 | tf_op jit(solution)/shard_map/ppermute | solution.py:617
  35.1 2.3 %collective-permute-done.5.refs_4_ = bf16[272,256]{1,0:T(8,128)(2,1)S(1)} collective-permute-done((bf16[272,256]{1,0:T(8,128)(2,1)S(1)}, bf16[272,256]{1,0:T(8,128)(2,1)S(1)}, u32[]{:S(2)}, u32[]{:S(2)}) %collective-permute-start.5) | collective-permute-done | bytes 139296 | tf_op jit(solution)/shard_map/ppermute | solution.py:617
  37.4 0.5 collective-permute-start.8
  37.9 0.2 collective-permute-start.12
  38.0 0.0 collective-permute-done.1.w1
  38.0 1.4 %collective-permute-done.8.r3 = bf16[256,1024]{1,0:T(8,128)(2,1)S(1)} collective-permute-done((bf16[256,1024]{1,0:T(8,128)(2,1)S(1)}, bf16[256,1024]{1,0:T(8,128)(2,1)S(1)}, u32[]{:S(2)}, u32[]{:S(2)}) %collective-permute-start.8) | collective-permute-done | bytes 524320 | tf_op jit(solution)/shard_map/ppermute | solution.py:531
  39.4 1.9 %late.3 = (bf16[4,512,128]{2,1,0:T(8,128)(2,1)S(1)}, bf16[272,256]{1,0:T(8,128)(2,1)S(1)}, bf16[1280,256]{1,0:T(8,128)(2,1)S(1)}, s32[10,128]{1,0:T(8,128)S(1)}, f32[8,128]{1,0:T(8,128)}) custom-call(s32[3]{0:T(128)S(1)} %pad_add_fusion.own, f32[8,128]{1,0:T(8,128)S(1)} %get-tuple-element.80.before, f32[512,768]{1,0:T(8,128)S(1)} %get-tuple-element.62.acc, ...), custom_call_target="tpu_custom_call" | custom-call | flops 805306368 | bytes 3145728 | tf_op jit(solution)/shard_map/late/pallas_call | solution.py:234
  41.3 1.4 %collective-permute-start.10 = (bf16[272,256]{1,0:T(8,128)(2,1)S(1)}, bf16[272,256]{1,0:T(8,128)(2,1)S(1)}, u32[]{:S(2)}, u32[]{:S(2)}) collective-permute-start(bf16[272,256]{1,0:T(8,128)(2,1)S(1)} %get-tuple-element.92), channel_id=1, source_target_pairs={{0,8},{4,12},{8,0},{12,4},{1,9},{5,13},{9,1},{13,5},{2,10},{6,14},... | collective-permute-start | bytes 417800 | tf_op jit(solution)/shard_map/ppermute | solution.py:617
  42.7 0.0 collective-permute-start.11
  42.7 1.5 %collective-permute-start.9 = (bf16[272,256]{1,0:T(8,128)(2,1)S(1)}, bf16[272,256]{1,0:T(8,128)(2,1)S(1)}, u32[]{:S(2)}, u32[]{:S(2)}) collective-permute-start(bf16[272,256]{1,0:T(8,128)(2,1)S(1)} %get-tuple-element.92), channel_id=1, source_target_pairs={{0,4},{4,8},{8,12},{12,0},{1,5},{5,9},{9,13},{13,1},{2,6},{6,10},{... | collective-permute-start | bytes 417800 | tf_op jit(solution)/shard_map/ppermute | solution.py:617
  44.2 0.2 collective-permute-start.17
  44.4 4.6 %attend.1 = (f32[2048,128]{1,0:T(8,128)S(1)}, f32[2048,128]{1,0:T(8,128)S(1)}, f32[2048,128]{1,0:T(8,128)S(1)}, bf16[512,512]{1,0:T(8,128)(2,1)S(1)}, f32[8,128]{1,0:T(8,128)S(1)}) custom-call(s32[3]{0:T(128)S(1)} %pad_add_fusion.own, bf16[4,512,128]{2,1,0:T(8,128)(2,1)S(1)} %get-tuple-element.86.q_all, bf16[1280,256]{1,0:T(8,128)(2,1)S(1)} %get-tuple-element.87.refs_0_, ...), custom_call_target="tpu_custom_call" | custom-call | flops 1342177280 | bytes 1048576 | tf_op jit(solution)/shard_map/attend/pallas_call | solution.py:371
  49.1 0.0 copy-start.2
  49.1 3.0 %collective-permute-done.12.w3 = bf16[256,1024]{1,0:T(8,128)(2,1)S(1)} collective-permute-done((bf16[256,1024]{1,0:T(8,128)(2,1)S(1)}, bf16[256,1024]{1,0:T(8,128)(2,1)S(1)}, u32[]{:S(2)}, u32[]{:S(2)}) %collective-permute-start.12) | collective-permute-done | bytes 524320 | tf_op jit(solution)/shard_map/ppermute | solution.py:531
  52.1 1.2 %collective-permute-start.15 = (bf16[256,1024]{1,0:T(8,128)(2,1)S(1)}, bf16[256,1024]{1,0:T(8,128)(2,1)S(1)}, u32[]{:S(2)}, u32[]{:S(2)}) collective-permute-start(bf16[256,1024]{1,0:T(8,128)(2,1)S(1)} %collective-permute-done.12.w3), channel_id=1, source_target_pairs={{0,16},{16,0},{1,17},{17,1},{2,18},{18,2},{3,19},{19,3},{4,20},{20... | collective-permute-start | bytes 1572872 | tf_op jit(solution)/shard_map/ppermute | solution.py:535
  53.4 0.6 collective-permute-done.9.refs_4_
  53.9 3.7 %attend_rest.1 = (bf16[512,512]{1,0:T(8,128)(2,1)S(1)}, bf16[256,512]{1,0:T(8,128)(2,1)S(1)}, bf16[256,512]{1,0:T(8,128)(2,1)S(1)}) custom-call(s32[3]{0:T(128)S(1)} %pad_add_fusion.own, bf16[4,512,128]{2,1,0:T(8,128)(2,1)S(1)} %get-tuple-element.86.q_all, f32[2048,128]{1,0:T(8,128)S(1)} %get-tuple-element.89.refs_0_, ...), custom_call_target="tpu_custom_call" | custom-call | flops 805306368 | bytes 1048576 | tf_op jit(solution)/shard_map/attend_rest/pallas_call | solution.py:389
  57.7 0.0 copy-start.10
  57.7 0.0 copy-start.11
  57.7 0.5 collective-permute-start.14
  58.3 0.5 collective-permute-start.13
  58.7 3.6 %collective-permute-done.17.w2 = bf16[256,1024]{1,0:T(8,128)(2,1)S(1)} collective-permute-done((bf16[256,1024]{1,0:T(8,128)(2,1)S(1)}, bf16[256,1024]{1,0:T(8,128)(2,1)S(1)}, u32[]{:S(2)}, u32[]{:S(2)}) %collective-permute-start.17) | collective-permute-done | bytes 524320 | tf_op jit(solution)/shard_map/ppermute | solution.py:531
  62.4 0.3 collective-permute-start.18
  62.6 1.2 %collective-permute-start.20 = (bf16[256,1024]{1,0:T(8,128)(2,1)S(1)}, bf16[256,1024]{1,0:T(8,128)(2,1)S(1)}, u32[]{:S(2)}, u32[]{:S(2)}) collective-permute-start(bf16[256,1024]{1,0:T(8,128)(2,1)S(1)} %collective-permute-done.17.w2), channel_id=1, source_target_pairs={{0,16},{16,0},{1,17},{17,1},{2,18},{18,2},{3,19},{19,3},{4,20},{20... | collective-permute-start | bytes 1572872 | tf_op jit(solution)/shard_map/ppermute | solution.py:535
  63.8 2.2 %collective-permute-done.15.other3 = bf16[256,1024]{1,0:T(8,128)(2,1)S(1)} collective-permute-done((bf16[256,1024]{1,0:T(8,128)(2,1)S(1)}, bf16[256,1024]{1,0:T(8,128)(2,1)S(1)}, u32[]{:S(2)}, u32[]{:S(2)}) %collective-permute-start.15) | collective-permute-done | bytes 524320 | tf_op jit(solution)/shard_map/ppermute | solution.py:535
  66.0 1.8 %keep.1 = (f32[512,1024]{1,0:T(8,128)S(1)}, f32[8,128]{1,0:T(8,128)S(1)}) custom-call(bf16[512,512]{1,0:T(8,128)(2,1)S(1)} %get-tuple-element.96.refs_8_.pick, bf16[512,1024]{1,0:T(8,128)(2,1)S(1)} %copy-done.2, bf16[512,512]{1,0:T(8,128)(2,1)S(1)} %get-tuple-element.98.h0, bf16[512,512]{1,0:T(8,128)(2,1)S(1)} %collective-permute-done.14.h1, ...), custom_call_target="tpu_custom_call" | custom-call | flops 1610612736 | bytes 5242880 | tf_op jit(solution)/shard_map/keep/pallas_call | solution.py:455
  67.8 0.2 collective-permute-done.13.h2.top2
  68.0 1.6 %collective-permute-start.16 = (bf16[256,512]{1,0:T(8,128)(2,1)S(1)}, bf16[256,512]{1,0:T(8,128)(2,1)S(1)}, u32[]{:S(2)}, u32[]{:S(2)}) collective-permute-start(bf16[256,512]{1,0:T(8,128)(2,1)S(1)} %collective-permute-done.13.h2.top2), channel_id=1, source_target_pairs={{0,1},{1,0},{2,3},{3,2},{4,5},{5,4},{6,7},{7,6},{8,9},{9,8},{10,11... | collective-permute-start | bytes 786440 | tf_op jit(solution)/shard_map/ppermute | solution.py:531
  69.6 4.0 %collective-permute-done.18.h2 = bf16[256,512]{1,0:T(8,128)(2,1)S(1)} collective-permute-done((bf16[256,512]{1,0:T(8,128)(2,1)S(1)}, bf16[256,512]{1,0:T(8,128)(2,1)S(1)}, u32[]{:S(2)}, u32[]{:S(2)}) %collective-permute-start.18) | collective-permute-done | bytes 262176 | tf_op jit(solution)/shard_map/ppermute | solution.py:531
  73.6 1.0 %collective-permute-start.19 = (bf16[256,512]{1,0:T(8,128)(2,1)S(1)}, bf16[256,512]{1,0:T(8,128)(2,1)S(1)}, u32[]{:S(2)}, u32[]{:S(2)}) collective-permute-start(bf16[256,512]{1,0:T(8,128)(2,1)S(1)} %collective-permute-done.18.h2), channel_id=1, source_target_pairs={{0,1},{1,0},{2,3},{3,2},{4,5},{5,4},{6,7},{7,6},{8,9},{9,8},{10,11... | collective-permute-start | bytes 786440 | tf_op jit(solution)/shard_map/ppermute | solution.py:531
  74.6 1.1 %gather.1.most = f32[256,1024]{1,0:T(8,128)S(1)} custom-call(s32[3]{0:T(128)S(1)} %pad_add_fusion.own, f32[8,128]{1,0:T(8,128)S(1)} %get-tuple-element.104.token, f32[512,1024]{1,0:T(8,128)S(1)} %get-tuple-element.105.kept, bf16[256,512]{1,0:T(8,128)(2,1)S(1)} %collective-permute-done.13.h2.top2, bf16[256,512]{1,0:T(8,128)(2,1)S(1)} %collective-permute-done.16.h3, ...), custom_call_target="tpu_custom_call" | custom-call | flops 402653184 | bytes 2097152 | tf_op jit(solution)/shard_map/gather/pallas_call | solution.py:486
  75.8 2.5 %finish.1 = (bf16[512,1024]{1,0:T(8,128)(2,1)}, f32[2,512]{1,0:T(2,128)S(1)}) custom-call(s32[3]{0:T(128)S(1)} %pad_add_fusion.own, f32[256,1024]{1,0:T(8,128)S(1)} %gather.1.most, f32[512,1024]{1,0:T(8,128)S(1)} %get-tuple-element.105.kept, bf16[256,512]{1,0:T(8,128)(2,1)S(1)} %collective-permute-done.13.h2.top2, ...), custom_call_target="tpu_custom_call" | custom-call | flops 536870912 | bytes 4194304 | tf_op jit(solution)/shard_map/finish/pallas_call | solution.py:515
  78.3 1.9 %collective-permute-start.21 = (f32[2,512]{1,0:T(2,128)S(1)}, f32[2,512]{1,0:T(2,128)S(1)}, u32[]{:S(2)}, u32[]{:S(2)}) collective-permute-start(f32[2,512]{1,0:T(2,128)S(1)} %get-tuple-element.113), channel_id=1, source_target_pairs={{0,1},{1,0},{2,3},{3,2},{4,5},{5,4},{6,7},{7,6},{8,9},{9,8},{10,11... | collective-permute-start | bytes 12296 | tf_op jit(solution)/shard_map/ppermute | solution.py:531
  80.1 0.5 collective-permute-start.22
  80.7 1.1 %collective-permute-start.23 = (f32[2,512]{1,0:T(2,128)S(1)}, f32[2,512]{1,0:T(2,128)S(1)}, u32[]{:S(2)}, u32[]{:S(2)}) collective-permute-start(f32[2,512]{1,0:T(2,128)S(1)} %get-tuple-element.113), channel_id=1, source_target_pairs={{0,3},{1,2},{2,1},{3,0},{4,7},{5,6},{6,5},{7,4},{8,11},{9,10},{10,... | collective-permute-start | bytes 12296 | tf_op jit(solution)/shard_map/ppermute | solution.py:531
  81.8 0.8 collective-permute-done.22
  82.6 1.1 %collective-permute-done.23 = f32[2,512]{1,0:T(2,128)S(1)} collective-permute-done((f32[2,512]{1,0:T(2,128)S(1)}, f32[2,512]{1,0:T(2,128)S(1)}, u32[]{:S(2)}, u32[]{:S(2)}) %collective-permute-start.23) | collective-permute-done | bytes 4128 | tf_op jit(solution)/shard_map/ppermute | solution.py:531
  83.7 0.6 fusion.2
  (25 shorter events, 0.1 us)
Async XLA Ops:
  0.6 4.1 %collective-permute-start = (bf16[512,1024]{1,0:T(8,128)(2,1)}, bf16[512,1024]{1,0:T(8,128)(2,1)S(1)}, u32[]{:S(2)}, u32[]{:S(2)}) collective-permute-start(bf16[512,1024]{1,0:T(8,128)(2,1)} %own.1), channel_id=1, source_target_pairs={{0,1},{1,0},{2,3},{3,2},{4,5},{5,4},{6,7},{7,6},{8,9},{9,8},{10,11... | collective-permute-start | bytes 3145736 | tf_op jit(solution)/shard_map/ppermute | solution.py:531
  2.6 13.7 %collective-permute-start.3 = (bf16[256,1024]{1,0:T(8,128)(2,1)S(1)}, bf16[256,1024]{1,0:T(8,128)(2,1)S(1)}, u32[]{:S(2)}, u32[]{:S(2)}) collective-permute-start(bf16[256,1024]{1,0:T(8,128)(2,1)S(1)} %get-tuple-element.114), channel_id=1, source_target_pairs={{0,2},{1,3},{2,0},{3,1},{4,6},{5,7},{6,4},{7,5},{8,10},{9,11},{10,... | collective-permute-start | bytes 1572872 | tf_op jit(solution)/shard_map/ppermute | solution.py:531
  4.7 10.5 %copy-start = (bf16[512,4096]{1,0:T(8,128)(2,1)S(1)}, bf16[512,4096]{1,0:T(8,128)(2,1)}, u32[]{:S(2)}) copy-start(bf16[512,4096]{1,0:T(8,128)(2,1)} %w_out.1) | copy-start | bytes 12582916
  4.7 1.4 %copy-start.1 = (bf16[512,1024]{1,0:T(8,128)(2,1)S(1)}, bf16[512,1024]{1,0:T(8,128)(2,1)}, u32[]{:S(2)}) copy-start(bf16[512,1024]{1,0:T(8,128)(2,1)} %own.1) | copy-start | bytes 3145732
  6.1 2.4 %copy-start.3 = (bf16[4096,512]{1,0:T(8,128)(2,1)S(1)}, bf16[4096,512]{1,0:T(8,128)(2,1)}, u32[]{:S(2)}) copy-start(bf16[4096,512]{1,0:T(8,128)(2,1)} %wq.1) | copy-start | bytes 12582916
  8.5 1.2 %copy-start.4 = (bf16[4096,128]{1,0:T(8,128)(2,1)S(1)}, bf16[4096,128]{1,0:T(8,128)(2,1)}, u32[]{:S(2)}) copy-start(bf16[4096,128]{1,0:T(8,128)(2,1)} %wk.1) | copy-start | bytes 3145732
  9.7 1.2 %copy-start.5 = (bf16[4096,128]{1,0:T(8,128)(2,1)S(1)}, bf16[4096,128]{1,0:T(8,128)(2,1)}, u32[]{:S(2)}) copy-start(bf16[4096,128]{1,0:T(8,128)(2,1)} %wv.1) | copy-start | bytes 3145732
  15.2 3.4 %copy-start.6 = (s32[512]{0:T(512)S(1)}, s32[512]{0:T(512)}, u32[]{:S(2)}) copy-start(s32[512]{0:T(512)} %param.14) | copy-start | bytes 6148
  15.2 3.4 %copy-start.7 = (s32[512]{0:T(512)S(1)}, s32[512]{0:T(512)}, u32[]{:S(2)}) copy-start(s32[512]{0:T(512)} %param.15) | copy-start | bytes 6148
  15.2 3.4 %copy-start.9 = (s32[1,4]{1,0:T(1,128)S(1)}, s32[1,4]{1,0:T(1,128)}, u32[]{:S(2)}) copy-start(s32[1,4]{1,0:T(1,128)} %loads.1) | copy-start | bytes 52
  16.3 3.8 %collective-permute-start.4 = (bf16[256,1024]{1,0:T(8,128)(2,1)S(1)}, bf16[256,1024]{1,0:T(8,128)(2,1)S(1)}, u32[]{:S(2)}, u32[]{:S(2)}) collective-permute-start(bf16[256,1024]{1,0:T(8,128)(2,1)S(1)} %collective-permute-done.3.r2), channel_id=1, source_target_pairs={{0,1},{1,0},{2,3},{3,2},{4,5},{5,4},{6,7},{7,6},{8,9},{9,8},{10,11... | collective-permute-start | bytes 1572872 | tf_op jit(solution)/shard_map/ppermute | solution.py:531
  17.0 13.6 %collective-permute-start.2 = (bf16[256,1024]{1,0:T(8,128)(2,1)S(1)}, bf16[256,1024]{1,0:T(8,128)(2,1)S(1)}, u32[]{:S(2)}, u32[]{:S(2)}) collective-permute-start(bf16[256,1024]{1,0:T(8,128)(2,1)S(1)} %get-tuple-element.115), channel_id=1, source_target_pairs={{0,2},{1,3},{2,0},{3,1},{4,6},{5,7},{6,4},{7,5},{8,10},{9,11},{10,... | collective-permute-start | bytes 1572872 | tf_op jit(solution)/shard_map/ppermute | solution.py:531
  18.3 19.8 %collective-permute-start.1 = (bf16[512,1024]{1,0:T(8,128)(2,1)S(1)}, bf16[512,1024]{1,0:T(8,128)(2,1)S(1)}, u32[]{:S(2)}, u32[]{:S(2)}) collective-permute-start(bf16[512,1024]{1,0:T(8,128)(2,1)S(1)} %get-tuple-element.59), channel_id=1, source_target_pairs={{0,1},{1,0},{2,3},{3,2},{4,5},{5,4},{6,7},{7,6},{8,9},{9,8},{10,11... | collective-permute-start | bytes 3145736 | tf_op jit(solution)/shard_map/ppermute | solution.py:531
  21.9 8.7 %collective-permute-start.7 = (bf16[272,256]{1,0:T(8,128)(2,1)S(1)}, bf16[272,256]{1,0:T(8,128)(2,1)S(1)}, u32[]{:S(2)}, u32[]{:S(2)}) collective-permute-start(bf16[272,256]{1,0:T(8,128)(2,1)S(1)} %get-tuple-element.71.refs_1_), channel_id=1, source_target_pairs={{0,4},{4,8},{8,12},{12,0},{1,5},{5,9},{9,13},{13,1},{2,6},{6,10},{... | collective-permute-start | bytes 417800 | tf_op jit(solution)/shard_map/ppermute | solution.py:617
  23.3 11.8 %collective-permute-start.6 = (bf16[272,256]{1,0:T(8,128)(2,1)S(1)}, bf16[272,256]{1,0:T(8,128)(2,1)S(1)}, u32[]{:S(2)}, u32[]{:S(2)}) collective-permute-start(bf16[272,256]{1,0:T(8,128)(2,1)S(1)} %get-tuple-element.71.refs_1_), channel_id=1, source_target_pairs={{0,8},{4,12},{8,0},{12,4},{1,9},{5,13},{9,1},{13,5},{2,10},{6,14},... | collective-permute-start | bytes 417800 | tf_op jit(solution)/shard_map/ppermute | solution.py:617
  24.4 13.0 %collective-permute-start.5 = (bf16[272,256]{1,0:T(8,128)(2,1)S(1)}, bf16[272,256]{1,0:T(8,128)(2,1)S(1)}, u32[]{:S(2)}, u32[]{:S(2)}) collective-permute-start(bf16[272,256]{1,0:T(8,128)(2,1)S(1)} %get-tuple-element.71.refs_1_), channel_id=1, source_target_pairs={{0,12},{4,0},{8,4},{12,8},{1,13},{5,1},{9,5},{13,9},{2,14},{6,2},{... | collective-permute-start | bytes 417800 | tf_op jit(solution)/shard_map/ppermute | solution.py:617
  37.4 2.0 %collective-permute-start.8 = (bf16[256,1024]{1,0:T(8,128)(2,1)S(1)}, bf16[256,1024]{1,0:T(8,128)(2,1)S(1)}, u32[]{:S(2)}, u32[]{:S(2)}) collective-permute-start(bf16[256,1024]{1,0:T(8,128)(2,1)S(1)} %collective-permute-done.2.r2), channel_id=1, source_target_pairs={{0,1},{1,0},{2,3},{3,2},{4,5},{5,4},{6,7},{7,6},{8,9},{9,8},{10,11... | collective-permute-start | bytes 1572872 | tf_op jit(solution)/shard_map/ppermute | solution.py:531
  37.9 14.2 %collective-permute-start.12 = (bf16[256,1024]{1,0:T(8,128)(2,1)S(1)}, bf16[256,1024]{1,0:T(8,128)(2,1)S(1)}, u32[]{:S(2)}, u32[]{:S(2)}) collective-permute-start(bf16[256,1024]{1,0:T(8,128)(2,1)S(1)} %get-tuple-element.93), channel_id=1, source_target_pairs={{0,3},{1,2},{2,1},{3,0},{4,7},{5,6},{6,5},{7,4},{8,11},{9,10},{10,... | collective-permute-start | bytes 1572872 | tf_op jit(solution)/shard_map/ppermute | solution.py:531
  39.4 5.0 %copy-start.8 = (s32[1,512]{1,0:T(1,128)S(1)}, s32[1,512]{1,0:T(1,128)}, u32[]{:S(2)}) copy-start(s32[1,512]{1,0:T(1,128)} %refs_2_.1) | copy-start | bytes 6148
  41.3 12.1 %collective-permute-start.10 = (bf16[272,256]{1,0:T(8,128)(2,1)S(1)}, bf16[272,256]{1,0:T(8,128)(2,1)S(1)}, u32[]{:S(2)}, u32[]{:S(2)}) collective-permute-start(bf16[272,256]{1,0:T(8,128)(2,1)S(1)} %get-tuple-element.92), channel_id=1, source_target_pairs={{0,8},{4,12},{8,0},{12,4},{1,9},{5,13},{9,1},{13,5},{2,10},{6,14},... | collective-permute-start | bytes 417800 | tf_op jit(solution)/shard_map/ppermute | solution.py:617
  42.7 10.7 %collective-permute-start.11 = (bf16[272,256]{1,0:T(8,128)(2,1)S(1)}, bf16[272,256]{1,0:T(8,128)(2,1)S(1)}, u32[]{:S(2)}, u32[]{:S(2)}) collective-permute-start(bf16[272,256]{1,0:T(8,128)(2,1)S(1)} %get-tuple-element.92), channel_id=1, source_target_pairs={{0,12},{4,0},{8,4},{12,8},{1,13},{5,1},{9,5},{13,9},{2,14},{6,2},{... | collective-permute-start | bytes 417800 | tf_op jit(solution)/shard_map/ppermute | solution.py:617
  42.7 11.2 %collective-permute-start.9 = (bf16[272,256]{1,0:T(8,128)(2,1)S(1)}, bf16[272,256]{1,0:T(8,128)(2,1)S(1)}, u32[]{:S(2)}, u32[]{:S(2)}) collective-permute-start(bf16[272,256]{1,0:T(8,128)(2,1)S(1)} %get-tuple-element.92), channel_id=1, source_target_pairs={{0,4},{4,8},{8,12},{12,0},{1,5},{5,9},{9,13},{13,1},{2,6},{6,10},{... | collective-permute-start | bytes 417800 | tf_op jit(solution)/shard_map/ppermute | solution.py:617
  44.2 18.2 %collective-permute-start.17 = (bf16[256,1024]{1,0:T(8,128)(2,1)S(1)}, bf16[256,1024]{1,0:T(8,128)(2,1)S(1)}, u32[]{:S(2)}, u32[]{:S(2)}) collective-permute-start(bf16[256,1024]{1,0:T(8,128)(2,1)S(1)} %get-tuple-element.108), channel_id=1, source_target_pairs={{0,2},{1,3},{2,0},{3,1},{4,6},{5,7},{6,4},{7,5},{8,10},{9,11},{10,... | collective-permute-start | bytes 1572872 | tf_op jit(solution)/shard_map/ppermute | solution.py:531
  49.1 16.9 %copy-start.2 = (bf16[512,1024]{1,0:T(8,128)(2,1)S(1)}, bf16[512,1024]{1,0:T(8,128)(2,1)}, u32[]{:S(2)}) copy-start(bf16[512,1024]{1,0:T(8,128)(2,1)} %own.1) | copy-start | bytes 3145732
  52.1 13.9 %collective-permute-start.15 = (bf16[256,1024]{1,0:T(8,128)(2,1)S(1)}, bf16[256,1024]{1,0:T(8,128)(2,1)S(1)}, u32[]{:S(2)}, u32[]{:S(2)}) collective-permute-start(bf16[256,1024]{1,0:T(8,128)(2,1)S(1)} %collective-permute-done.12.w3), channel_id=1, source_target_pairs={{0,16},{16,0},{1,17},{17,1},{2,18},{18,2},{3,19},{19,3},{4,20},{20... | collective-permute-start | bytes 1572872 | tf_op jit(solution)/shard_map/ppermute | solution.py:535
  57.7 16.9 %copy-start.10 = (bf16[1024]{0:T(1024)(128)(2,1)S(1)}, bf16[1024]{0:T(1024)(128)(2,1)}, u32[]{:S(2)}) copy-start(bf16[1024]{0:T(1024)(128)(2,1)} %param.22) | copy-start | bytes 6148
  57.7 16.9 %copy-start.11 = (bf16[1024]{0:T(1024)(128)(2,1)S(1)}, bf16[1024]{0:T(1024)(128)(2,1)}, u32[]{:S(2)}) copy-start(bf16[1024]{0:T(1024)(128)(2,1)} %param.23) | copy-start | bytes 6148
  57.7 8.3 %collective-permute-start.14 = (bf16[512,512]{1,0:T(8,128)(2,1)S(1)}, bf16[512,512]{1,0:T(8,128)(2,1)S(1)}, u32[]{:S(2)}, u32[]{:S(2)}) collective-permute-start(bf16[512,512]{1,0:T(8,128)(2,1)S(1)} %get-tuple-element.98.h0), channel_id=1, source_target_pairs={{0,1},{1,0},{2,3},{3,2},{4,5},{5,4},{6,7},{7,6},{8,9},{9,8},{10,11... | collective-permute-start | bytes 1572872 | tf_op jit(solution)/shard_map/ppermute | solution.py:531
  58.3 9.7 %collective-permute-start.13 = (bf16[256,512]{1,0:T(8,128)(2,1)S(1)}, bf16[256,512]{1,0:T(8,128)(2,1)S(1)}, u32[]{:S(2)}, u32[]{:S(2)}) collective-permute-start(bf16[256,512]{1,0:T(8,128)(2,1)S(1)} %get-tuple-element.97), channel_id=1, source_target_pairs={{0,2},{1,3},{2,0},{3,1},{4,6},{5,7},{6,4},{7,5},{8,10},{9,11},{10,... | collective-permute-start | bytes 786440 | tf_op jit(solution)/shard_map/ppermute | solution.py:531
  62.4 11.2 %collective-permute-start.18 = (bf16[256,512]{1,0:T(8,128)(2,1)S(1)}, bf16[256,512]{1,0:T(8,128)(2,1)S(1)}, u32[]{:S(2)}, u32[]{:S(2)}) collective-permute-start(bf16[256,512]{1,0:T(8,128)(2,1)S(1)} %get-tuple-element.111), channel_id=1, source_target_pairs={{0,2},{1,3},{2,0},{3,1},{4,6},{5,7},{6,4},{7,5},{8,10},{9,11},{10,... | collective-permute-start | bytes 786440 | tf_op jit(solution)/shard_map/ppermute | solution.py:531
  62.6 13.2 %collective-permute-start.20 = (bf16[256,1024]{1,0:T(8,128)(2,1)S(1)}, bf16[256,1024]{1,0:T(8,128)(2,1)S(1)}, u32[]{:S(2)}, u32[]{:S(2)}) collective-permute-start(bf16[256,1024]{1,0:T(8,128)(2,1)S(1)} %collective-permute-done.17.w2), channel_id=1, source_target_pairs={{0,16},{16,0},{1,17},{17,1},{2,18},{18,2},{3,19},{19,3},{4,20},{20... | collective-permute-start | bytes 1572872 | tf_op jit(solution)/shard_map/ppermute | solution.py:535
  68.0 6.7 %collective-permute-start.16 = (bf16[256,512]{1,0:T(8,128)(2,1)S(1)}, bf16[256,512]{1,0:T(8,128)(2,1)S(1)}, u32[]{:S(2)}, u32[]{:S(2)}) collective-permute-start(bf16[256,512]{1,0:T(8,128)(2,1)S(1)} %collective-permute-done.13.h2.top2), channel_id=1, source_target_pairs={{0,1},{1,0},{2,3},{3,2},{4,5},{5,4},{6,7},{7,6},{8,9},{9,8},{10,11... | collective-permute-start | bytes 786440 | tf_op jit(solution)/shard_map/ppermute | solution.py:531
  73.6 2.2 %collective-permute-start.19 = (bf16[256,512]{1,0:T(8,128)(2,1)S(1)}, bf16[256,512]{1,0:T(8,128)(2,1)S(1)}, u32[]{:S(2)}, u32[]{:S(2)}) collective-permute-start(bf16[256,512]{1,0:T(8,128)(2,1)S(1)} %collective-permute-done.18.h2), channel_id=1, source_target_pairs={{0,1},{1,0},{2,3},{3,2},{4,5},{5,4},{6,7},{7,6},{8,9},{9,8},{10,11... | collective-permute-start | bytes 786440 | tf_op jit(solution)/shard_map/ppermute | solution.py:531
  78.3 3.5 %collective-permute-start.21 = (f32[2,512]{1,0:T(2,128)S(1)}, f32[2,512]{1,0:T(2,128)S(1)}, u32[]{:S(2)}, u32[]{:S(2)}) collective-permute-start(f32[2,512]{1,0:T(2,128)S(1)} %get-tuple-element.113), channel_id=1, source_target_pairs={{0,1},{1,0},{2,3},{3,2},{4,5},{5,4},{6,7},{7,6},{8,9},{9,8},{10,11... | collective-permute-start | bytes 12296 | tf_op jit(solution)/shard_map/ppermute | solution.py:531
  80.1 2.5 %collective-permute-start.22 = (f32[2,512]{1,0:T(2,128)S(1)}, f32[2,512]{1,0:T(2,128)S(1)}, u32[]{:S(2)}, u32[]{:S(2)}) collective-permute-start(f32[2,512]{1,0:T(2,128)S(1)} %get-tuple-element.113), channel_id=1, source_target_pairs={{0,2},{1,3},{2,0},{3,1},{4,6},{5,7},{6,4},{7,5},{8,10},{9,11},{10,... | collective-permute-start | bytes 12296 | tf_op jit(solution)/shard_map/ppermute | solution.py:531
  80.7 3.0 %collective-permute-start.23 = (f32[2,512]{1,0:T(2,128)S(1)}, f32[2,512]{1,0:T(2,128)S(1)}, u32[]{:S(2)}, u32[]{:S(2)}) collective-permute-start(f32[2,512]{1,0:T(2,128)S(1)} %get-tuple-element.113), channel_id=1, source_target_pairs={{0,3},{1,2},{2,1},{3,0},{4,7},{5,6},{6,5},{7,4},{8,11},{9,10},{10,... | collective-permute-start | bytes 12296 | tf_op jit(solution)/shard_map/ppermute | solution.py:531

commit v6 on v5

--- a/solution.py
+++ b/solution.py
@@ -442,11 +442,13 @@
     )(own, w_out, token)
 
 
-def keep_kernel(pick, own, h0, h1, w0, w1, out, token):
+def keep_kernel(pick, own, h0, h1, w0, w1, top, bottom, token):
     del token
     total = jnp.dot(h0[...], w0[...], preferred_element_type=jnp.float32)
     total += jnp.dot(h1[...], w1[...], preferred_element_type=jnp.float32)
-    out[...] = total + pick_rows(pick[...], own[...])
+    total += pick_rows(pick[...], own[...])
+    top[...] = total[: top.shape[0], :]
+    bottom[...] = total[top.shape[0] :, :]
 
 
 def keep(pick, own, h0, h1, w0, w1):
@@ -454,9 +456,9 @@
     depth = h0.shape[1]
     return pl.pallas_call(
         keep_kernel,
-        out_shape=(jax.ShapeDtypeStruct((rows, width), jnp.float32), TOKEN),
+        out_shape=(*(jax.ShapeDtypeStruct((size, width), jnp.float32) for size in part_sizes(rows)), TOKEN),
         in_specs=[whole()] * 6,
-        out_specs=(whole(), far_memory()),
+        out_specs=(whole(), whole(), far_memory()),
         compiler_params=params(12),
         cost_estimate=cost(2 * rows * (2 * depth + rows) * width, 4 * depth * width + 6 * rows * width),
         name="keep",
@@ -475,9 +477,9 @@
     return total
 
 
-def gather_kernel(own, token, kept, h2, h3, w2, w3, other3, out):
-    del token
-    out[...] = add_heads(kept[: h2.shape[0], :], own, h2, h3, w2, w3, other3)
+def gather_kernel(own, token_in, kept, h2, h3, w2, w3, other3, out, token):
+    del token_in, token
+    out[...] = add_heads(kept[...], own, h2, h3, w2, w3, other3)
 
 
 def gather(own, token, kept, h2, h3, w2, w3, other3):
@@ -485,22 +487,21 @@
     width = kept.shape[1]
     return pl.pallas_call(
         gather_kernel,
-        out_shape=jax.ShapeDtypeStruct((rows, width), jnp.float32),
+        out_shape=(jax.ShapeDtypeStruct((rows, width), jnp.float32), TOKEN),
         in_specs=[pl.BlockSpec(memory_space=pltpu.SMEM), far_memory()] + [whole()] * 6,
-        out_specs=whole(),
+        out_specs=(whole(), far_memory()),
         compiler_params=params(14),
         cost_estimate=cost(3 * rows * depth * width, 8 * rows * width),
         name="gather",
     )(own, token, kept, h2, h3, w2, w3, other3)
 
 
-def finish_kernel(own, most, kept, top2, h2, h3, w2, w3, other3, other2, gain, head, hidden_out, sums):
-    first = most.shape[0]
+def finish_kernel(own, most0, most1, top2, h2, other2, gain, head, hidden_out, sums):
     weight = gain[...].astype(jnp.float32) * head[...].astype(jnp.float32)
-    rest = add_heads(kept[first:, :], own, h2, h3, w2, w3, other3)
-    for span, h, total in ((slice(0, first), top2, most[...]), (slice(first, kept.shape[0]), h2, rest)):
+    first = most0.shape[0]
+    for span, h, most in ((slice(0, first), top2, most0), (slice(first, first + most1.shape[0]), h2, most1)):
         _, others = shares(own, h)
-        total += jnp.dot(h[:, others], other2[...], preferred_element_type=jnp.float32)
+        total = most[...] + jnp.dot(h[:, others], other2[...], preferred_element_type=jnp.float32)
         hidden = total.astype(jnp.bfloat16)
         hidden_out[span, :] = hidden
         x = hidden.astype(jnp.float32)
@@ -509,8 +510,8 @@
             sums[i : i + 1, span] = jnp.sum(lanes.T, 0, keepdims=True)
 
 
-def finish(own, most, kept, top2, h2, h3, w2, w3, other3, other2, gain, head):
-    rows, width = kept.shape
+def finish(own, most0, most1, top2, h2, other2, gain, head):
+    rows, width = most0.shape[0] + most1.shape[0], most0.shape[1]
     depth = h2.shape[1]
     return pl.pallas_call(
         finish_kernel,
@@ -518,12 +519,12 @@
             jax.ShapeDtypeStruct((rows, width), jnp.bfloat16),
             jax.ShapeDtypeStruct((2, rows), jnp.float32),
         ),
-        in_specs=[pl.BlockSpec(memory_space=pltpu.SMEM)] + [whole()] * 11,
+        in_specs=[pl.BlockSpec(memory_space=pltpu.SMEM)] + [whole()] * 7,
         out_specs=(whole(), whole()),
         compiler_params=params(14),
-        cost_estimate=cost(2 * rows * depth * width, 8 * rows * width),
+        cost_estimate=cost(rows * depth * width, 8 * rows * width),
         name="finish",
-    )(own, most, kept, top2, h2, h3, w2, w3, other3, other2, gain, head)
+    )(own, most0, most1, top2, h2, other2, gain, head)
 
 
 def flip(x, bit):
@@ -637,23 +638,13 @@
     other2 = swap_parts(far2)
     heads_other = flip(heads, 1)
     heads_other, other3 = lax.optimization_barrier((heads_other, other3))
-    kept, token = keep(pick, hidden_in, heads, heads_other, near, near_other)
+    kept0, kept1, token = keep(pick, hidden_in, heads, heads_other, near, near_other)
     heads2[0], token = lax.optimization_barrier((heads2[0], token))
     heads3 = [flip(x, 1) for x in heads2]
-    most = gather(t_own, token, kept, heads2[0], heads3[0], far2, far3, other3)
+    most0, token = gather(t_own, token, kept0, heads2[0], heads3[0], far2, far3, other3)
+    most1, _ = gather(t_own, token, kept1, heads2[1], heads3[1], far2, far3, other3)
     hidden, sums = finish(
-        t_own,
-        most,
-        kept,
-        heads2[0],
-        heads2[1],
-        heads3[1],
-        far2,
-        far3,
-        other3,
-        other2,
-        final_gain.reshape(1, width),
-        value_head.reshape(1, width),
+        t_own, most0, most1, *heads2, other2, final_gain.reshape(1, width), value_head.reshape(1, width)
     )
     square, product = sums + flip(sums, 1) + (flip(sums, 2) + flip(sums, 3))
     return hidden, product * lax.rsqrt(square / MODEL_WIDTH + NORM_EPS)

time: 86 us -> 84.7 us (0.985); the launches traced: 84.3 us -> 84.1 us
  Pallas kernels: 24.3 us -> 28.3 us
  waiting for transfers between devices: 28.5 us -> 25.5 us
  starting transfers between devices: 21.7 us -> 20.5 us
    pallas_call x1, Pallas kernels: 4.63 us -> 7.04 us  [attend(): pl.pallas_call(functools.partial(attend_kernel, (), False), out_shape=(ru...]
    ppermute x16, waiting for transfers between devices: 19 us -> 16.9 us  [flip(): return lax.ppermute(x, 'tensor', [(i, i ^ bit) for i in range(count)])]
    ppermute x16, starting transfers between devices: 12.5 us -> 11.3 us  [flip(): return lax.ppermute(x, 'tensor', [(i, i ^ bit) for i in range(count)])]
    pallas_call x2 -> x3, Pallas kernels: 2.91 us -> 4.05 us  [the longest x2 2.26 us: gather(): pl.pallas_call(gather_kernel, out_shape=(jax.ShapeDtypeStruct((rows, widt...]
    ppermute x2, waiting for transfers between devices: 2.16 us -> 1.19 us  [swap_parts(): return lax.ppermute(x, 'parts', [(0, 1), (1, 0)])]
    pallas_call x1, Pallas kernels: 3.74 us -> 4.71 us  [attend_rest(): pl.pallas_call(functools.partial(attend_kernel, tuple(pieces), True), out...]
  transfers between devices with their start and end apart: 24 -> 24, of which waited for: 12 -> 13; matrix products, arithmetic and copies ran while one was open for 2% -> 2% of each run, Pallas kernels for 26% -> 31%
where the time goes in v6:
time: 84.7 us; the launch traced here: 84.1 us
  Pallas kernels  28.3 us (33%)
  waiting for transfers between devices  25.5 us (30%)
  starting transfers between devices  20.5 us (24%)
  local copies, waits for them, and re-layouts  8.23 us (10%)
    ppermute x16, waiting for transfers between devices, flip(): return lax.ppermute(x, 'tensor', [(i, i ^ bit) for i in range(count)])  16.9 us
    ppermute x16, starting transfers between devices, flip(): return lax.ppermute(x, 'tensor', [(i, i ^ bit) for i in range(count)])  11.3 us
    ppermute x6, waiting for transfers between devices, on_device(): lax.ppermute(kv, 'dp', [(i, (i + d) % n_dp) for i in range(n_dp)])  7.38 us
    pallas_call x1, Pallas kernels, attend(): pl.pallas_call(functools.partial(attend_kernel, (), False), out_shape=(ru...  7.04 us
    ppermute x6, starting transfers between devices, on_device(): lax.ppermute(kv, 'dp', [(i, (i + d) % n_dp) for i in range(n_dp)])  6.71 us
    unnamed x24, local copies, waits for them, and re-layouts  6.24 us
    pallas_call x1, Pallas kernels, attend_rest(): pl.pallas_call(functools.partial(attend_kernel, tuple(pieces), True), out...  4.71 us
    pallas_call x1, Pallas kernels, early(): pl.pallas_call(early_kernel, out_shape=(jax.ShapeDtypeStruct((rows, colum...  4.23 us
  transfers between devices with their start and end apart: 24, of which 13 were waited for; matrix products, arithmetic and copies ran while one was open for 2% of the time, Pallas kernels for 31%

profile of v6, /device:TPU:9, one launch (start us, length us, event | category | flops | bytes accessed | tf_op | source)
XLA Modules:
  0.0 84.1 jit_solution(6908903511578855866)
XLA Ops:
  0.6 0.7 collective-permute-start
  1.4 1.3 %fusion.3 = (bf16[256,1024]{1,0:T(8,128)(2,1)S(1)}, bf16[256,1024]{1,0:T(8,128)(2,1)S(1)}) fusion(bf16[512,1024]{1,0:T(8,128)(2,1)} %own.1), kind=kLoop, calls=%fused_computation.6 | loop fusion | bytes 2097152 | tf_op jit(solution)/shard_map/slice | solution.py:565
  2.6 1.3 %collective-permute-start.3 = (bf16[256,1024]{1,0:T(8,128)(2,1)S(1)}, bf16[256,1024]{1,0:T(8,128)(2,1)S(1)}, u32[]{:S(2)}, u32[]{:S(2)}) collective-permute-start(bf16[256,1024]{1,0:T(8,128)(2,1)S(1)} %get-tuple-element.122), channel_id=1, source_target_pairs={{0,2},{1,3},{2,0},{3,1},{4,6},{5,7},{6,4},{7,5},{8,10},{9,11},{10,... | collective-permute-start | bytes 1572872 | tf_op jit(solution)/shard_map/ppermute | solution.py:532
  3.9 0.7 reshape.25.gain
  4.6 0.1 pad_add_fusion.own
  4.7 1.4 %copy-done.1 = bf16[512,1024]{1,0:T(8,128)(2,1)S(1)} copy-done((bf16[512,1024]{1,0:T(8,128)(2,1)S(1)}, bf16[512,1024]{1,0:T(8,128)(2,1)}, u32[]{:S(2)}) %copy-start.1) | copy-done | bytes 1048600
  6.1 2.4 %copy-done.3 = bf16[4096,512]{1,0:T(8,128)(2,1)S(1)} copy-done((bf16[4096,512]{1,0:T(8,128)(2,1)S(1)}, bf16[4096,512]{1,0:T(8,128)(2,1)}, u32[]{:S(2)}) %copy-start.3) | copy-done | bytes 4194328
  8.5 1.2 %copy-done.4 = bf16[4096,128]{1,0:T(8,128)(2,1)S(1)} copy-done((bf16[4096,128]{1,0:T(8,128)(2,1)S(1)}, bf16[4096,128]{1,0:T(8,128)(2,1)}, u32[]{:S(2)}) %copy-start.4) | copy-done | bytes 1048600
  9.7 1.2 %copy-done.5 = bf16[4096,128]{1,0:T(8,128)(2,1)S(1)} copy-done((bf16[4096,128]{1,0:T(8,128)(2,1)S(1)}, bf16[4096,128]{1,0:T(8,128)(2,1)}, u32[]{:S(2)}) %copy-start.5) | copy-done | bytes 1048600
  10.9 4.2 %early.1 = (f32[512,768]{1,0:T(8,128)S(1)}, f32[512,1]{1,0:T(8,128)S(1)}, bf16[2,1024,768]{2,1,0:T(8,128)(2,1)S(1)}, f32[8,128]{1,0:T(8,128)S(1)}) custom-call(s32[3]{0:T(128)S(1)} %pad_add_fusion.own, bf16[512,1024]{1,0:T(8,128)(2,1)S(1)} %copy-done.1, bf16[512,1024]{1,0:T(8,128)(2,1)S(1)} %collective-permute-done.r1, bf16[1,4096]{1,0:T(2,128)(2,1)S(1)} %reshape.25.gain, ...), custom_call_target="tpu_custom_call" | custom-call | flops 1610612736 | bytes 6291456 | tf_op jit(solution)/shard_map/early/pallas_call | solution.py:143
  15.2 0.0 copy-start.6
  15.2 0.0 copy-start.7
  15.2 0.0 copy-start.9
  15.2 1.0 %columns.1 = (bf16[512,1024]{1,0:T(8,128)(2,1)S(1)}, bf16[512,1024]{1,0:T(8,128)(2,1)S(1)}, bf16[256,1024]{1,0:T(8,128)(2,1)S(1)}, bf16[256,1024]{1,0:T(8,128)(2,1)S(1)}, f32[8,128]{1,0:T(8,128)S(1)}) custom-call(s32[3]{0:T(128)S(1)} %pad_add_fusion.own, bf16[512,4096]{1,0:T(8,128)(2,1)S(1)} %copy-done, f32[8,128]{1,0:T(8,128)S(1)} %get-tuple-element.62.token_in), custom_call_target="tpu_custom_call" | custom-call | flops 1 | bytes 8388608 | tf_op jit(solution)/shard_map/columns/pallas_call | solution.py:433
  16.2 0.1 collective-permute-done.3.r2
  16.2 0.8 collective-permute-start.4
  17.0 1.2 %collective-permute-start.2 = (bf16[256,1024]{1,0:T(8,128)(2,1)S(1)}, bf16[256,1024]{1,0:T(8,128)(2,1)S(1)}, u32[]{:S(2)}, u32[]{:S(2)}) collective-permute-start(bf16[256,1024]{1,0:T(8,128)(2,1)S(1)} %get-tuple-element.123), channel_id=1, source_target_pairs={{0,2},{1,3},{2,0},{3,1},{4,6},{5,7},{6,4},{7,5},{8,10},{9,11},{10,... | collective-permute-start | bytes 1572872 | tf_op jit(solution)/shard_map/ppermute | solution.py:532
  18.3 0.3 collective-permute-start.1
  18.5 1.6 %prep.1 = (bf16[16,512]{1,0:T(8,128)(2,1)S(1)}, f32[512,128]{1,0:T(8,128)S(1)}, f32[512,128]{1,0:T(8,128)S(1)}) custom-call(s32[1,4]{1,0:T(1,128)S(1)} %copy-done.9, s32[4,128]{1,0:T(4,128)S(1)} %bitcast.6, s32[4,128]{1,0:T(4,128)S(1)} %bitcast.7), custom_call_target="tpu_custom_call" | custom-call | flops 2000000000 | bytes 40000000 | tf_op jit(solution)/shard_map/prep/pallas_call | solution.py:79
  20.1 1.8 %late.2 = (bf16[4,256,128]{2,1,0:T(8,128)(2,1)S(1)}, bf16[272,256]{1,0:T(8,128)(2,1)S(1)}, f32[8,128]{1,0:T(8,128)S(1)}) custom-call(s32[3]{0:T(128)S(1)} %pad_add_fusion.own, f32[8,128]{1,0:T(8,128)S(1)} %get-tuple-element.65.before, f32[512,768]{1,0:T(8,128)S(1)} %get-tuple-element.66.acc, f32[512,1]{1,0:T(8,128)S(1)} %get-tuple-element.67.squares, ...), custom_call_target="tpu_custom_call" | custom-call | flops 805306368 | bytes 3145728 | tf_op jit(solution)/shard_map/late/pallas_call | solution.py:234
  21.9 0.0 copy-start.8
  22.0 1.3 %collective-permute-start.7 = (bf16[272,256]{1,0:T(8,128)(2,1)S(1)}, bf16[272,256]{1,0:T(8,128)(2,1)S(1)}, u32[]{:S(2)}, u32[]{:S(2)}) collective-permute-start(bf16[272,256]{1,0:T(8,128)(2,1)S(1)} %get-tuple-element.75.refs_1_), channel_id=1, source_target_pairs={{0,4},{4,8},{8,12},{12,0},{1,5},{5,9},{9,13},{13,1},{2,6},{6,10},{... | collective-permute-start | bytes 417800 | tf_op jit(solution)/shard_map/ppermute | solution.py:618
  23.3 1.1 %collective-permute-start.6 = (bf16[272,256]{1,0:T(8,128)(2,1)S(1)}, bf16[272,256]{1,0:T(8,128)(2,1)S(1)}, u32[]{:S(2)}, u32[]{:S(2)}) collective-permute-start(bf16[272,256]{1,0:T(8,128)(2,1)S(1)} %get-tuple-element.75.refs_1_), channel_id=1, source_target_pairs={{0,8},{4,12},{8,0},{12,4},{1,9},{5,13},{9,1},{13,5},{2,10},{6,14},... | collective-permute-start | bytes 417800 | tf_op jit(solution)/shard_map/ppermute | solution.py:618
  24.4 1.4 %collective-permute-start.5 = (bf16[272,256]{1,0:T(8,128)(2,1)S(1)}, bf16[272,256]{1,0:T(8,128)(2,1)S(1)}, u32[]{:S(2)}, u32[]{:S(2)}) collective-permute-start(bf16[272,256]{1,0:T(8,128)(2,1)S(1)} %get-tuple-element.75.refs_1_), channel_id=1, source_target_pairs={{0,12},{4,0},{8,4},{12,8},{1,13},{5,1},{9,5},{13,9},{2,14},{6,2},{... | collective-permute-start | bytes 417800 | tf_op jit(solution)/shard_map/ppermute | solution.py:618
  25.8 4.8 %collective-permute-done.2.r2 = bf16[256,1024]{1,0:T(8,128)(2,1)S(1)} collective-permute-done((bf16[256,1024]{1,0:T(8,128)(2,1)S(1)}, bf16[256,1024]{1,0:T(8,128)(2,1)S(1)}, u32[]{:S(2)}, u32[]{:S(2)}) %collective-permute-start.2) | collective-permute-done | bytes 524320 | tf_op jit(solution)/shard_map/ppermute | solution.py:532
  30.6 4.5 %collective-permute-done.6.refs_3_ = bf16[272,256]{1,0:T(8,128)(2,1)S(1)} collective-permute-done((bf16[272,256]{1,0:T(8,128)(2,1)S(1)}, bf16[272,256]{1,0:T(8,128)(2,1)S(1)}, u32[]{:S(2)}, u32[]{:S(2)}) %collective-permute-start.6) | collective-permute-done | bytes 139296 | tf_op jit(solution)/shard_map/ppermute | solution.py:618
  35.1 2.3 %collective-permute-done.5.refs_4_ = bf16[272,256]{1,0:T(8,128)(2,1)S(1)} collective-permute-done((bf16[272,256]{1,0:T(8,128)(2,1)S(1)}, bf16[272,256]{1,0:T(8,128)(2,1)S(1)}, u32[]{:S(2)}, u32[]{:S(2)}) %collective-permute-start.5) | collective-permute-done | bytes 139296 | tf_op jit(solution)/shard_map/ppermute | solution.py:618
  37.4 0.5 collective-permute-start.8
  37.9 0.2 collective-permute-start.12
  38.1 1.4 %collective-permute-done.8.r3 = bf16[256,1024]{1,0:T(8,128)(2,1)S(1)} collective-permute-done((bf16[256,1024]{1,0:T(8,128)(2,1)S(1)}, bf16[256,1024]{1,0:T(8,128)(2,1)S(1)}, u32[]{:S(2)}, u32[]{:S(2)}) %collective-permute-start.8) | collective-permute-done | bytes 524320 | tf_op jit(solution)/shard_map/ppermute | solution.py:532
  39.4 1.9 %late.3 = (bf16[4,512,128]{2,1,0:T(8,128)(2,1)S(1)}, bf16[272,256]{1,0:T(8,128)(2,1)S(1)}, bf16[1280,256]{1,0:T(8,128)(2,1)S(1)}, s32[10,128]{1,0:T(8,128)S(1)}, f32[8,128]{1,0:T(8,128)}) custom-call(s32[3]{0:T(128)S(1)} %pad_add_fusion.own, f32[8,128]{1,0:T(8,128)S(1)} %get-tuple-element.84.before, f32[512,768]{1,0:T(8,128)S(1)} %get-tuple-element.66.acc, ...), custom_call_target="tpu_custom_call" | custom-call | flops 805306368 | bytes 3145728 | tf_op jit(solution)/shard_map/late/pallas_call | solution.py:234
  41.3 1.4 %collective-permute-start.10 = (bf16[272,256]{1,0:T(8,128)(2,1)S(1)}, bf16[272,256]{1,0:T(8,128)(2,1)S(1)}, u32[]{:S(2)}, u32[]{:S(2)}) collective-permute-start(bf16[272,256]{1,0:T(8,128)(2,1)S(1)} %get-tuple-element.96), channel_id=1, source_target_pairs={{0,8},{4,12},{8,0},{12,4},{1,9},{5,13},{9,1},{13,5},{2,10},{6,14},... | collective-permute-start | bytes 417800 | tf_op jit(solution)/shard_map/ppermute | solution.py:618
  42.7 0.0 collective-permute-start.11
  42.7 1.5 %collective-permute-start.9 = (bf16[272,256]{1,0:T(8,128)(2,1)S(1)}, bf16[272,256]{1,0:T(8,128)(2,1)S(1)}, u32[]{:S(2)}, u32[]{:S(2)}) collective-permute-start(bf16[272,256]{1,0:T(8,128)(2,1)S(1)} %get-tuple-element.96), channel_id=1, source_target_pairs={{0,4},{4,8},{8,12},{12,0},{1,5},{5,9},{9,13},{13,1},{2,6},{6,10},{... | collective-permute-start | bytes 417800 | tf_op jit(solution)/shard_map/ppermute | solution.py:618
  44.2 0.3 collective-permute-start.17
  44.5 7.0 %attend.1 = (f32[2048,128]{1,0:T(8,128)S(1)}, f32[2048,128]{1,0:T(8,128)S(1)}, f32[2048,128]{1,0:T(8,128)S(1)}, bf16[512,512]{1,0:T(8,128)(2,1)S(1)}, f32[8,128]{1,0:T(8,128)S(1)}) custom-call(s32[3]{0:T(128)S(1)} %pad_add_fusion.own, bf16[4,512,128]{2,1,0:T(8,128)(2,1)S(1)} %get-tuple-element.90.q_all, bf16[1280,256]{1,0:T(8,128)(2,1)S(1)} %get-tuple-element.91.refs_0_, ...), custom_call_target="tpu_custom_call" | custom-call | flops 1342177280 | bytes 1048576 | tf_op jit(solution)/shard_map/attend/pallas_call | solution.py:371
  51.5 0.6 collective-permute-done.12.w3
  52.1 1.2 %collective-permute-start.15 = (bf16[256,1024]{1,0:T(8,128)(2,1)S(1)}, bf16[256,1024]{1,0:T(8,128)(2,1)S(1)}, u32[]{:S(2)}, u32[]{:S(2)}) collective-permute-start(bf16[256,1024]{1,0:T(8,128)(2,1)S(1)} %collective-permute-done.12.w3), channel_id=1, source_target_pairs={{0,16},{16,0},{1,17},{17,1},{2,18},{18,2},{3,19},{19,3},{4,20},{20... | collective-permute-start | bytes 1572872 | tf_op jit(solution)/shard_map/ppermute | solution.py:536
  53.4 0.0 collective-permute-done.10.refs_5_
  53.4 0.0 collective-permute-done.11.refs_6_
  53.4 0.6 collective-permute-done.9.refs_4_
  54.0 4.7 %attend_rest.1 = (bf16[512,512]{1,0:T(8,128)(2,1)S(1)}, bf16[256,512]{1,0:T(8,128)(2,1)S(1)}, bf16[256,512]{1,0:T(8,128)(2,1)S(1)}) custom-call(s32[3]{0:T(128)S(1)} %pad_add_fusion.own, bf16[4,512,128]{2,1,0:T(8,128)(2,1)S(1)} %get-tuple-element.90.q_all, f32[2048,128]{1,0:T(8,128)S(1)} %get-tuple-element.93.refs_0_, ...), custom_call_target="tpu_custom_call" | custom-call | flops 805306368 | bytes 1048576 | tf_op jit(solution)/shard_map/attend_rest/pallas_call | solution.py:389
  58.7 0.5 collective-permute-start.14
  59.2 0.3 collective-permute-start.13
  59.5 2.9 %collective-permute-done.17.w2 = bf16[256,1024]{1,0:T(8,128)(2,1)S(1)} collective-permute-done((bf16[256,1024]{1,0:T(8,128)(2,1)S(1)}, bf16[256,1024]{1,0:T(8,128)(2,1)S(1)}, u32[]{:S(2)}, u32[]{:S(2)}) %collective-permute-start.17) | collective-permute-done | bytes 524320 | tf_op jit(solution)/shard_map/ppermute | solution.py:532
  62.4 0.3 collective-permute-start.18
  62.6 1.2 %collective-permute-start.20 = (bf16[256,1024]{1,0:T(8,128)(2,1)S(1)}, bf16[256,1024]{1,0:T(8,128)(2,1)S(1)}, u32[]{:S(2)}, u32[]{:S(2)}) collective-permute-start(bf16[256,1024]{1,0:T(8,128)(2,1)S(1)} %collective-permute-done.17.w2), channel_id=1, source_target_pairs={{0,16},{16,0},{1,17},{17,1},{2,18},{18,2},{3,19},{19,3},{4,20},{20... | collective-permute-start | bytes 1572872 | tf_op jit(solution)/shard_map/ppermute | solution.py:536
  63.9 1.2 %collective-permute-done.15.other3 = bf16[256,1024]{1,0:T(8,128)(2,1)S(1)} collective-permute-done((bf16[256,1024]{1,0:T(8,128)(2,1)S(1)}, bf16[256,1024]{1,0:T(8,128)(2,1)S(1)}, u32[]{:S(2)}, u32[]{:S(2)}) %collective-permute-start.15) | collective-permute-done | bytes 524320 | tf_op jit(solution)/shard_map/ppermute | solution.py:536
  65.1 1.8 %keep.1 = (f32[256,1024]{1,0:T(8,128)S(1)}, f32[256,1024]{1,0:T(8,128)S(1)}, f32[8,128]{1,0:T(8,128)S(1)}) custom-call(bf16[512,512]{1,0:T(8,128)(2,1)S(1)} %get-tuple-element.100.refs_8_.pick, bf16[512,1024]{1,0:T(8,128)(2,1)S(1)} %copy-done.2, bf16[512,512]{1,0:T(8,128)(2,1)S(1)} %get-tuple-element.102.h0, ...), custom_call_target="tpu_custom_call" | custom-call | flops 1610612736 | bytes 5242880 | tf_op jit(solution)/shard_map/keep/pallas_call | solution.py:457
  66.9 1.1 %collective-permute-done.13.h2.top2 = bf16[256,512]{1,0:T(8,128)(2,1)S(1)} collective-permute-done((bf16[256,512]{1,0:T(8,128)(2,1)S(1)}, bf16[256,512]{1,0:T(8,128)(2,1)S(1)}, u32[]{:S(2)}, u32[]{:S(2)}) %collective-permute-start.13) | collective-permute-done | bytes 262176 | tf_op jit(solution)/shard_map/ppermute | solution.py:532
  68.0 1.6 %collective-permute-start.16 = (bf16[256,512]{1,0:T(8,128)(2,1)S(1)}, bf16[256,512]{1,0:T(8,128)(2,1)S(1)}, u32[]{:S(2)}, u32[]{:S(2)}) collective-permute-start(bf16[256,512]{1,0:T(8,128)(2,1)S(1)} %collective-permute-done.13.h2.top2), channel_id=1, source_target_pairs={{0,1},{1,0},{2,3},{3,2},{4,5},{5,4},{6,7},{7,6},{8,9},{9,8},{10,11... | collective-permute-start | bytes 786440 | tf_op jit(solution)/shard_map/ppermute | solution.py:532
  69.6 4.0 %collective-permute-done.18.h2 = bf16[256,512]{1,0:T(8,128)(2,1)S(1)} collective-permute-done((bf16[256,512]{1,0:T(8,128)(2,1)S(1)}, bf16[256,512]{1,0:T(8,128)(2,1)S(1)}, u32[]{:S(2)}, u32[]{:S(2)}) %collective-permute-start.18) | collective-permute-done | bytes 262176 | tf_op jit(solution)/shard_map/ppermute | solution.py:532
  73.6 1.0 %collective-permute-start.19 = (bf16[256,512]{1,0:T(8,128)(2,1)S(1)}, bf16[256,512]{1,0:T(8,128)(2,1)S(1)}, u32[]{:S(2)}, u32[]{:S(2)}) collective-permute-start(bf16[256,512]{1,0:T(8,128)(2,1)S(1)} %collective-permute-done.18.h2), channel_id=1, source_target_pairs={{0,1},{1,0},{2,3},{3,2},{4,5},{5,4},{6,7},{7,6},{8,9},{9,8},{10,11... | collective-permute-start | bytes 786440 | tf_op jit(solution)/shard_map/ppermute | solution.py:532
  74.7 1.1 %gather.2 = (f32[256,1024]{1,0:T(8,128)S(1)}, f32[8,128]{1,0:T(8,128)S(1)}) custom-call(s32[3]{0:T(128)S(1)} %pad_add_fusion.own, f32[8,128]{1,0:T(8,128)S(1)} %get-tuple-element.108.token_in, f32[256,1024]{1,0:T(8,128)S(1)} %get-tuple-element.109.kept, bf16[256,512]{1,0:T(8,128)(2,1)S(1)} %collective-permute-done.13.h2.top2, ...), custom_call_target="tpu_custom_call" | custom-call | flops 402653184 | bytes 2097152 | tf_op jit(solution)/shard_map/gather/pallas_call | solution.py:488
  75.8 0.0 collective-permute-done.19.h3
  75.8 1.1 %gather.3 = (f32[256,1024]{1,0:T(8,128)S(1)}, f32[8,128]{1,0:T(8,128)}) custom-call(s32[3]{0:T(128)S(1)} %pad_add_fusion.own, f32[8,128]{1,0:T(8,128)S(1)} %get-tuple-element.116.token_in, f32[256,1024]{1,0:T(8,128)S(1)} %get-tuple-element.117.kept, bf16[256,512]{1,0:T(8,128)(2,1)S(1)} %collective-permute-done.18.h2, ...), custom_call_target="tpu_custom_call" | custom-call | flops 402653184 | bytes 2097152 | tf_op jit(solution)/shard_map/gather/pallas_call | solution.py:488
  76.9 0.0 collective-permute-done.20.other2
  76.9 2.1 %finish.1 = (bf16[512,1024]{1,0:T(8,128)(2,1)}, f32[2,512]{1,0:T(2,128)S(1)}) custom-call(s32[3]{0:T(128)S(1)} %pad_add_fusion.own, f32[256,1024]{1,0:T(8,128)S(1)} %get-tuple-element.115.most0, f32[256,1024]{1,0:T(8,128)S(1)} %get-tuple-element.119.most1, bf16[256,512]{1,0:T(8,128)(2,1)S(1)} %collective-permute-done.13.h2.top2, ...), custom_call_target="tpu_custom_call" | custom-call | flops 268435456 | bytes 4194304 | tf_op jit(solution)/shard_map/finish/pallas_call | solution.py:516
  79.1 0.8 collective-permute-start.21
  79.8 0.7 collective-permute-start.22
  80.5 1.0 %collective-permute-start.23 = (f32[2,512]{1,0:T(2,128)S(1)}, f32[2,512]{1,0:T(2,128)S(1)}, u32[]{:S(2)}, u32[]{:S(2)}) collective-permute-start(f32[2,512]{1,0:T(2,128)S(1)} %get-tuple-element.121), channel_id=1, source_target_pairs={{0,3},{1,2},{2,1},{3,0},{4,7},{5,6},{6,5},{7,4},{8,11},{9,10},{10,... | collective-permute-start | bytes 12296 | tf_op jit(solution)/shard_map/ppermute | solution.py:532
  81.5 0.8 collective-permute-done.22
  82.3 1.2 %collective-permute-done.23 = f32[2,512]{1,0:T(2,128)S(1)} collective-permute-done((f32[2,512]{1,0:T(2,128)S(1)}, f32[2,512]{1,0:T(2,128)S(1)}, u32[]{:S(2)}, u32[]{:S(2)}) %collective-permute-start.23) | collective-permute-done | bytes 4128 | tf_op jit(solution)/shard_map/ppermute | solution.py:532
  83.5 0.6 fusion.2
  (26 shorter events, 0.1 us)
Async XLA Ops:
  0.6 4.1 %collective-permute-start = (bf16[512,1024]{1,0:T(8,128)(2,1)}, bf16[512,1024]{1,0:T(8,128)(2,1)S(1)}, u32[]{:S(2)}, u32[]{:S(2)}) collective-permute-start(bf16[512,1024]{1,0:T(8,128)(2,1)} %own.1), channel_id=1, source_target_pairs={{0,1},{1,0},{2,3},{3,2},{4,5},{5,4},{6,7},{7,6},{8,9},{9,8},{10,11... | collective-permute-start | bytes 3145736 | tf_op jit(solution)/shard_map/ppermute | solution.py:532
  2.6 13.6 %collective-permute-start.3 = (bf16[256,1024]{1,0:T(8,128)(2,1)S(1)}, bf16[256,1024]{1,0:T(8,128)(2,1)S(1)}, u32[]{:S(2)}, u32[]{:S(2)}) collective-permute-start(bf16[256,1024]{1,0:T(8,128)(2,1)S(1)} %get-tuple-element.122), channel_id=1, source_target_pairs={{0,2},{1,3},{2,0},{3,1},{4,6},{5,7},{6,4},{7,5},{8,10},{9,11},{10,... | collective-permute-start | bytes 1572872 | tf_op jit(solution)/shard_map/ppermute | solution.py:532
  4.7 10.5 %copy-start = (bf16[512,4096]{1,0:T(8,128)(2,1)S(1)}, bf16[512,4096]{1,0:T(8,128)(2,1)}, u32[]{:S(2)}) copy-start(bf16[512,4096]{1,0:T(8,128)(2,1)} %w_out.1) | copy-start | bytes 12582916
  4.7 1.4 %copy-start.1 = (bf16[512,1024]{1,0:T(8,128)(2,1)S(1)}, bf16[512,1024]{1,0:T(8,128)(2,1)}, u32[]{:S(2)}) copy-start(bf16[512,1024]{1,0:T(8,128)(2,1)} %own.1) | copy-start | bytes 3145732
  6.1 2.4 %copy-start.3 = (bf16[4096,512]{1,0:T(8,128)(2,1)S(1)}, bf16[4096,512]{1,0:T(8,128)(2,1)}, u32[]{:S(2)}) copy-start(bf16[4096,512]{1,0:T(8,128)(2,1)} %wq.1) | copy-start | bytes 12582916
  8.5 1.2 %copy-start.4 = (bf16[4096,128]{1,0:T(8,128)(2,1)S(1)}, bf16[4096,128]{1,0:T(8,128)(2,1)}, u32[]{:S(2)}) copy-start(bf16[4096,128]{1,0:T(8,128)(2,1)} %wk.1) | copy-start | bytes 3145732
  9.7 1.2 %copy-start.5 = (bf16[4096,128]{1,0:T(8,128)(2,1)S(1)}, bf16[4096,128]{1,0:T(8,128)(2,1)}, u32[]{:S(2)}) copy-start(bf16[4096,128]{1,0:T(8,128)(2,1)} %wv.1) | copy-start | bytes 3145732
  15.2 3.4 %copy-start.6 = (s32[512]{0:T(512)S(1)}, s32[512]{0:T(512)}, u32[]{:S(2)}) copy-start(s32[512]{0:T(512)} %param.14) | copy-start | bytes 6148
  15.2 3.4 %copy-start.7 = (s32[512]{0:T(512)S(1)}, s32[512]{0:T(512)}, u32[]{:S(2)}) copy-start(s32[512]{0:T(512)} %param.15) | copy-start | bytes 6148
  15.2 3.4 %copy-start.9 = (s32[1,4]{1,0:T(1,128)S(1)}, s32[1,4]{1,0:T(1,128)}, u32[]{:S(2)}) copy-start(s32[1,4]{1,0:T(1,128)} %loads.1) | copy-start | bytes 52
  16.2 3.9 %collective-permute-start.4 = (bf16[256,1024]{1,0:T(8,128)(2,1)S(1)}, bf16[256,1024]{1,0:T(8,128)(2,1)S(1)}, u32[]{:S(2)}, u32[]{:S(2)}) collective-permute-start(bf16[256,1024]{1,0:T(8,128)(2,1)S(1)} %collective-permute-done.3.r2), channel_id=1, source_target_pairs={{0,1},{1,0},{2,3},{3,2},{4,5},{5,4},{6,7},{7,6},{8,9},{9,8},{10,11... | collective-permute-start | bytes 1572872 | tf_op jit(solution)/shard_map/ppermute | solution.py:532
  17.0 13.6 %collective-permute-start.2 = (bf16[256,1024]{1,0:T(8,128)(2,1)S(1)}, bf16[256,1024]{1,0:T(8,128)(2,1)S(1)}, u32[]{:S(2)}, u32[]{:S(2)}) collective-permute-start(bf16[256,1024]{1,0:T(8,128)(2,1)S(1)} %get-tuple-element.123), channel_id=1, source_target_pairs={{0,2},{1,3},{2,0},{3,1},{4,6},{5,7},{6,4},{7,5},{8,10},{9,11},{10,... | collective-permute-start | bytes 1572872 | tf_op jit(solution)/shard_map/ppermute | solution.py:532
  18.3 19.8 %collective-permute-start.1 = (bf16[512,1024]{1,0:T(8,128)(2,1)S(1)}, bf16[512,1024]{1,0:T(8,128)(2,1)S(1)}, u32[]{:S(2)}, u32[]{:S(2)}) collective-permute-start(bf16[512,1024]{1,0:T(8,128)(2,1)S(1)} %get-tuple-element.63), channel_id=1, source_target_pairs={{0,1},{1,0},{2,3},{3,2},{4,5},{5,4},{6,7},{7,6},{8,9},{9,8},{10,11... | collective-permute-start | bytes 3145736 | tf_op jit(solution)/shard_map/ppermute | solution.py:532
  21.9 22.5 %copy-start.8 = (s32[1,512]{1,0:T(1,128)S(1)}, s32[1,512]{1,0:T(1,128)}, u32[]{:S(2)}) copy-start(s32[1,512]{1,0:T(1,128)} %refs_2_.1) | copy-start | bytes 6148
  22.0 8.6 %collective-permute-start.7 = (bf16[272,256]{1,0:T(8,128)(2,1)S(1)}, bf16[272,256]{1,0:T(8,128)(2,1)S(1)}, u32[]{:S(2)}, u32[]{:S(2)}) collective-permute-start(bf16[272,256]{1,0:T(8,128)(2,1)S(1)} %get-tuple-element.75.refs_1_), channel_id=1, source_target_pairs={{0,4},{4,8},{8,12},{12,0},{1,5},{5,9},{9,13},{13,1},{2,6},{6,10},{... | collective-permute-start | bytes 417800 | tf_op jit(solution)/shard_map/ppermute | solution.py:618
  23.3 11.8 %collective-permute-start.6 = (bf16[272,256]{1,0:T(8,128)(2,1)S(1)}, bf16[272,256]{1,0:T(8,128)(2,1)S(1)}, u32[]{:S(2)}, u32[]{:S(2)}) collective-permute-start(bf16[272,256]{1,0:T(8,128)(2,1)S(1)} %get-tuple-element.75.refs_1_), channel_id=1, source_target_pairs={{0,8},{4,12},{8,0},{12,4},{1,9},{5,13},{9,1},{13,5},{2,10},{6,14},... | collective-permute-start | bytes 417800 | tf_op jit(solution)/shard_map/ppermute | solution.py:618
  24.4 13.0 %collective-permute-start.5 = (bf16[272,256]{1,0:T(8,128)(2,1)S(1)}, bf16[272,256]{1,0:T(8,128)(2,1)S(1)}, u32[]{:S(2)}, u32[]{:S(2)}) collective-permute-start(bf16[272,256]{1,0:T(8,128)(2,1)S(1)} %get-tuple-element.75.refs_1_), channel_id=1, source_target_pairs={{0,12},{4,0},{8,4},{12,8},{1,13},{5,1},{9,5},{13,9},{2,14},{6,2},{... | collective-permute-start | bytes 417800 | tf_op jit(solution)/shard_map/ppermute | solution.py:618
  37.4 2.0 %collective-permute-start.8 = (bf16[256,1024]{1,0:T(8,128)(2,1)S(1)}, bf16[256,1024]{1,0:T(8,128)(2,1)S(1)}, u32[]{:S(2)}, u32[]{:S(2)}) collective-permute-start(bf16[256,1024]{1,0:T(8,128)(2,1)S(1)} %collective-permute-done.2.r2), channel_id=1, source_target_pairs={{0,1},{1,0},{2,3},{3,2},{4,5},{5,4},{6,7},{7,6},{8,9},{9,8},{10,11... | collective-permute-start | bytes 1572872 | tf_op jit(solution)/shard_map/ppermute | solution.py:532
  37.9 14.2 %collective-permute-start.12 = (bf16[256,1024]{1,0:T(8,128)(2,1)S(1)}, bf16[256,1024]{1,0:T(8,128)(2,1)S(1)}, u32[]{:S(2)}, u32[]{:S(2)}) collective-permute-start(bf16[256,1024]{1,0:T(8,128)(2,1)S(1)} %get-tuple-element.97), channel_id=1, source_target_pairs={{0,3},{1,2},{2,1},{3,0},{4,7},{5,6},{6,5},{7,4},{8,11},{9,10},{10,... | collective-permute-start | bytes 1572872 | tf_op jit(solution)/shard_map/ppermute | solution.py:532
  41.3 12.1 %collective-permute-start.10 = (bf16[272,256]{1,0:T(8,128)(2,1)S(1)}, bf16[272,256]{1,0:T(8,128)(2,1)S(1)}, u32[]{:S(2)}, u32[]{:S(2)}) collective-permute-start(bf16[272,256]{1,0:T(8,128)(2,1)S(1)} %get-tuple-element.96), channel_id=1, source_target_pairs={{0,8},{4,12},{8,0},{12,4},{1,9},{5,13},{9,1},{13,5},{2,10},{6,14},... | collective-permute-start | bytes 417800 | tf_op jit(solution)/shard_map/ppermute | solution.py:618
  42.7 10.7 %collective-permute-start.11 = (bf16[272,256]{1,0:T(8,128)(2,1)S(1)}, bf16[272,256]{1,0:T(8,128)(2,1)S(1)}, u32[]{:S(2)}, u32[]{:S(2)}) collective-permute-start(bf16[272,256]{1,0:T(8,128)(2,1)S(1)} %get-tuple-element.96), channel_id=1, source_target_pairs={{0,12},{4,0},{8,4},{12,8},{1,13},{5,1},{9,5},{13,9},{2,14},{6,2},{... | collective-permute-start | bytes 417800 | tf_op jit(solution)/shard_map/ppermute | solution.py:618
  42.7 11.2 %collective-permute-start.9 = (bf16[272,256]{1,0:T(8,128)(2,1)S(1)}, bf16[272,256]{1,0:T(8,128)(2,1)S(1)}, u32[]{:S(2)}, u32[]{:S(2)}) collective-permute-start(bf16[272,256]{1,0:T(8,128)(2,1)S(1)} %get-tuple-element.96), channel_id=1, source_target_pairs={{0,4},{4,8},{8,12},{12,0},{1,5},{5,9},{9,13},{13,1},{2,6},{6,10},{... | collective-permute-start | bytes 417800 | tf_op jit(solution)/shard_map/ppermute | solution.py:618
  44.2 18.2 %collective-permute-start.17 = (bf16[256,1024]{1,0:T(8,128)(2,1)S(1)}, bf16[256,1024]{1,0:T(8,128)(2,1)S(1)}, u32[]{:S(2)}, u32[]{:S(2)}) collective-permute-start(bf16[256,1024]{1,0:T(8,128)(2,1)S(1)} %get-tuple-element.112), channel_id=1, source_target_pairs={{0,2},{1,3},{2,0},{3,1},{4,6},{5,7},{6,4},{7,5},{8,10},{9,11},{10,... | collective-permute-start | bytes 1572872 | tf_op jit(solution)/shard_map/ppermute | solution.py:532
  44.4 20.6 %copy-start.2 = (bf16[512,1024]{1,0:T(8,128)(2,1)S(1)}, bf16[512,1024]{1,0:T(8,128)(2,1)}, u32[]{:S(2)}) copy-start(bf16[512,1024]{1,0:T(8,128)(2,1)} %own.1) | copy-start | bytes 3145732
  52.1 12.9 %collective-permute-start.15 = (bf16[256,1024]{1,0:T(8,128)(2,1)S(1)}, bf16[256,1024]{1,0:T(8,128)(2,1)S(1)}, u32[]{:S(2)}, u32[]{:S(2)}) collective-permute-start(bf16[256,1024]{1,0:T(8,128)(2,1)S(1)} %collective-permute-done.12.w3), channel_id=1, source_target_pairs={{0,16},{16,0},{1,17},{17,1},{2,18},{18,2},{3,19},{19,3},{4,20},{20... | collective-permute-start | bytes 1572872 | tf_op jit(solution)/shard_map/ppermute | solution.py:536
  53.9 20.7 %copy-start.10 = (bf16[1024]{0:T(1024)(128)(2,1)S(1)}, bf16[1024]{0:T(1024)(128)(2,1)}, u32[]{:S(2)}) copy-start(bf16[1024]{0:T(1024)(128)(2,1)} %param.22) | copy-start | bytes 6148
  53.9 20.7 %copy-start.11 = (bf16[1024]{0:T(1024)(128)(2,1)S(1)}, bf16[1024]{0:T(1024)(128)(2,1)}, u32[]{:S(2)}) copy-start(bf16[1024]{0:T(1024)(128)(2,1)} %param.23) | copy-start | bytes 6148
  58.7 6.4 %collective-permute-start.14 = (bf16[512,512]{1,0:T(8,128)(2,1)S(1)}, bf16[512,512]{1,0:T(8,128)(2,1)S(1)}, u32[]{:S(2)}, u32[]{:S(2)}) collective-permute-start(bf16[512,512]{1,0:T(8,128)(2,1)S(1)} %get-tuple-element.102.h0), channel_id=1, source_target_pairs={{0,1},{1,0},{2,3},{3,2},{4,5},{5,4},{6,7},{7,6},{8,9},{9,8},{10,11... | collective-permute-start | bytes 1572872 | tf_op jit(solution)/shard_map/ppermute | solution.py:532
  59.2 8.8 %collective-permute-start.13 = (bf16[256,512]{1,0:T(8,128)(2,1)S(1)}, bf16[256,512]{1,0:T(8,128)(2,1)S(1)}, u32[]{:S(2)}, u32[]{:S(2)}) collective-permute-start(bf16[256,512]{1,0:T(8,128)(2,1)S(1)} %get-tuple-element.101), channel_id=1, source_target_pairs={{0,2},{1,3},{2,0},{3,1},{4,6},{5,7},{6,4},{7,5},{8,10},{9,11},{10,... | collective-permute-start | bytes 786440 | tf_op jit(solution)/shard_map/ppermute | solution.py:532
  62.4 11.2 %collective-permute-start.18 = (bf16[256,512]{1,0:T(8,128)(2,1)S(1)}, bf16[256,512]{1,0:T(8,128)(2,1)S(1)}, u32[]{:S(2)}, u32[]{:S(2)}) collective-permute-start(bf16[256,512]{1,0:T(8,128)(2,1)S(1)} %get-tuple-element.118), channel_id=1, source_target_pairs={{0,2},{1,3},{2,0},{3,1},{4,6},{5,7},{6,4},{7,5},{8,10},{9,11},{10,... | collective-permute-start | bytes 786440 | tf_op jit(solution)/shard_map/ppermute | solution.py:532
  62.6 14.3 %collective-permute-start.20 = (bf16[256,1024]{1,0:T(8,128)(2,1)S(1)}, bf16[256,1024]{1,0:T(8,128)(2,1)S(1)}, u32[]{:S(2)}, u32[]{:S(2)}) collective-permute-start(bf16[256,1024]{1,0:T(8,128)(2,1)S(1)} %collective-permute-done.17.w2), channel_id=1, source_target_pairs={{0,16},{16,0},{1,17},{17,1},{2,18},{18,2},{3,19},{19,3},{4,20},{20... | collective-permute-start | bytes 1572872 | tf_op jit(solution)/shard_map/ppermute | solution.py:536
  68.0 6.7 %collective-permute-start.16 = (bf16[256,512]{1,0:T(8,128)(2,1)S(1)}, bf16[256,512]{1,0:T(8,128)(2,1)S(1)}, u32[]{:S(2)}, u32[]{:S(2)}) collective-permute-start(bf16[256,512]{1,0:T(8,128)(2,1)S(1)} %collective-permute-done.13.h2.top2), channel_id=1, source_target_pairs={{0,1},{1,0},{2,3},{3,2},{4,5},{5,4},{6,7},{7,6},{8,9},{9,8},{10,11... | collective-permute-start | bytes 786440 | tf_op jit(solution)/shard_map/ppermute | solution.py:532
  73.6 2.2 %collective-permute-start.19 = (bf16[256,512]{1,0:T(8,128)(2,1)S(1)}, bf16[256,512]{1,0:T(8,128)(2,1)S(1)}, u32[]{:S(2)}, u32[]{:S(2)}) collective-permute-start(bf16[256,512]{1,0:T(8,128)(2,1)S(1)} %collective-permute-done.18.h2), channel_id=1, source_target_pairs={{0,1},{1,0},{2,3},{3,2},{4,5},{5,4},{6,7},{7,6},{8,9},{9,8},{10,11... | collective-permute-start | bytes 786440 | tf_op jit(solution)/shard_map/ppermute | solution.py:532
  79.1 2.4 %collective-permute-start.21 = (f32[2,512]{1,0:T(2,128)S(1)}, f32[2,512]{1,0:T(2,128)S(1)}, u32[]{:S(2)}, u32[]{:S(2)}) collective-permute-start(f32[2,512]{1,0:T(2,128)S(1)} %get-tuple-element.121), channel_id=1, source_target_pairs={{0,1},{1,0},{2,3},{3,2},{4,5},{5,4},{6,7},{7,6},{8,9},{9,8},{10,11... | collective-permute-start | bytes 12296 | tf_op jit(solution)/shard_map/ppermute | solution.py:532
  79.8 2.5 %collective-permute-start.22 = (f32[2,512]{1,0:T(2,128)S(1)}, f32[2,512]{1,0:T(2,128)S(1)}, u32[]{:S(2)}, u32[]{:S(2)}) collective-permute-start(f32[2,512]{1,0:T(2,128)S(1)} %get-tuple-element.121), channel_id=1, source_target_pairs={{0,2},{1,3},{2,0},{3,1},{4,6},{5,7},{6,4},{7,5},{8,10},{9,11},{10,... | collective-permute-start | bytes 12296 | tf_op jit(solution)/shard_map/ppermute | solution.py:532
  80.5 3.0 %collective-permute-start.23 = (f32[2,512]{1,0:T(2,128)S(1)}, f32[2,512]{1,0:T(2,128)S(1)}, u32[]{:S(2)}, u32[]{:S(2)}) collective-permute-start(f32[2,512]{1,0:T(2,128)S(1)} %get-tuple-element.121), channel_id=1, source_target_pairs={{0,3},{1,2},{2,1},{3,0},{4,7},{5,6},{6,5},{7,4},{8,11},{9,10},{10,... | collective-permute-start | bytes 12296 | tf_op jit(solution)/shard_map/ppermute | solution.py:532
